TPU v7x, 32 devices: a whole 2x2x4 slice. The times are simulated.
32 devices in a mesh: groups: 2 (over y), seq: 16 (over z, x, core).
Axes of the slice: x: 2, y: 2, z: 4, core: 2. Of those that a mesh axis runs over, the one named last changes fastest.
Arguments:
- features: bfloat16 [4096, 512], P(('groups', 'seq')), parts along dimension 0, may hold values from -6 to 6
- gain_attn: float32 [512], replicated, may hold values from 0.5 to 1.5
- gain_ffn: float32 [512], replicated, may hold values from 0.5 to 1.5
- query_key_value_weight: bfloat16 [512, 1536], replicated, may hold values from -0.5 to 0.5
- w_out: bfloat16 [512, 512], replicated, may hold values from -0.25 to 0.25
- w_in: bfloat16 [512, 2048], replicated, may hold values from -0.25 to 0.25
- w_down: bfloat16 [1024, 512], replicated, may hold values from -0.1875 to 0.1875
- tile_lists: int32 [32, 4], P(('groups', 'seq')), parts along dimension 0, may hold values from 0 to 15, as said below
- tile_count: int32 [32], P(('groups', 'seq')), parts along dimension 0, may hold values from 1 to 4, as said below
- partition: int32 [4096], P(('groups', 'seq')), parts along dimension 0, may hold values from 0 to 31, never falling along the last dimension, each value on 1 to 128 neighbouring positions
- grad_out: bfloat16 [4096, 512], P(('groups', 'seq')), parts along dimension 0, may hold values from -6 to 6
Outputs:
- layer_out: bfloat16 [4096, 512], P(('groups', 'seq')), parts along dimension 0
- d_features: bfloat16 [4096, 512], P(('groups', 'seq')), parts along dimension 0
- grad_qkv: float32 [1024, 1536], P(('groups', 'seq')), parts along dimension 0
- grad_w_out: float32 [1024, 512], P(('groups', 'seq')), parts along dimension 0
- grad_w_in: float32 [1024, 2048], P(('groups', 'seq')), parts along dimension 0
- grad_w_down: float32 [2048, 512], P(('groups', 'seq')), parts along dimension 0
- grad_gains: float32 [2048], P(('groups', 'seq')), parts along dimension 0
There are 2 independent parts, one for each index of `groups`. A program takes and returns all parts, laid end to end along the dimension named above; an argument that names none is the same for every part. Nothing has to cross between parts.
Inputs may be any that keep to these rules, and one draw needn't show every extreme that they name: `tile_lists`: row t holds 4 different tiles, the first of them t. `tile_count`: tile 0 uses all 4 entries. Never falls along the nodes; every partition has 1 to 128 nodes.
All inputs are finite; a program needn't handle non-finite values.
Results may differ from a plain program's by a relative error of at most 0.018.
The roundings to bfloat16 on the way count: a program that leaves them out, or rounds other values in their place, can miss the bound.
Values may be sent and summed in bfloat16 or wider, within the bound.
A program may use at most 128 MiB of HBM per device.

v0:
```python
import math

import jax
import jax.numpy as jnp
from jax import lax
from jax.sharding import PartitionSpec as P

HEADS = 16
TILE = 128
KT = 4
VN_DEV = 2


CAP = 30.0
EPS = 1e-06
HIGH_PRECISION = lax.Precision.HIGHEST


def rms_parts(values):
    inverse = lax.rsqrt(jnp.mean(values * values, axis=-1, keepdims=True) + EPS)
    return (inverse, values * inverse)


def wide_shape(query_rows, key_matrix):
    return (
        query_rows.shape[0],
        query_rows.shape[2],
        query_rows.shape[1],
        key_matrix.shape[1],
        key_matrix.shape[4],
    )


def attend_scores(query_rows, key_matrix, virtual_key_rows, active_mask):
    scale = 1.0 / math.sqrt(query_rows.shape[-1])
    block_units, unit_rows, heads_here, head_dim = query_rows.shape
    near = jnp.einsum(
        "buhe,bkhet->bhukt", query_rows, key_matrix, preferred_element_type=jnp.float32
    )
    near = near.reshape(block_units, heads_here, unit_rows, -1) * scale
    far = (
        jnp.einsum(
            "buhe,phe->bhup", query_rows, virtual_key_rows, preferred_element_type=jnp.float32
        )
        * scale
    )
    near_tanh = jnp.tanh(near / CAP)
    far_tanh = jnp.tanh(far / CAP)
    near_w = jnp.exp(CAP * near_tanh) * active_mask[:, None, None, :]
    far_w = jnp.exp(CAP * far_tanh)
    totals = jnp.sum(near_w, axis=-1, keepdims=True) + jnp.sum(far_w, axis=-1, keepdims=True)
    return (near_w / totals, far_w / totals, near_tanh, far_tanh)


def attend_forward(
    query_rows, key_matrix, value_matrix, virtual_key_rows, virtual_value_rows, active_mask
):
    near_p, far_p, near_tanh, far_tanh = attend_scores(
        query_rows, key_matrix, virtual_key_rows, active_mask
    )
    shape_wide = wide_shape(query_rows, key_matrix)
    output = jnp.einsum(
        "bhukt,bkhet->buhe",
        near_p.astype(jnp.bfloat16).reshape(shape_wide),
        value_matrix,
        preferred_element_type=jnp.float32,
    )
    output = output + jnp.einsum(
        "bhup,phe->buhe",
        far_p.astype(jnp.bfloat16),
        virtual_value_rows,
        preferred_element_type=jnp.float32,
    )
    return output.astype(jnp.bfloat16)


def attention_backward(
    query_rows,
    key_matrix,
    value_matrix,
    virtual_key_rows,
    virtual_value_rows,
    active_mask,
    grad_rows,
):
    near_p, far_p, near_tanh, far_tanh = attend_scores(
        query_rows, key_matrix, virtual_key_rows, active_mask
    )
    shape_wide = wide_shape(query_rows, key_matrix)
    near_b = near_p.astype(jnp.bfloat16).reshape(shape_wide)
    far_b = far_p.astype(jnp.bfloat16)
    near_dp = jnp.einsum(
        "buhe,bkhet->bhukt", grad_rows, value_matrix, preferred_element_type=jnp.float32
    ).reshape(near_p.shape)
    far_dp = jnp.einsum(
        "buhe,phe->bhup", grad_rows, virtual_value_rows, preferred_element_type=jnp.float32
    )
    inner = jnp.sum(near_p * near_dp, axis=-1, keepdims=True) + jnp.sum(
        far_p * far_dp, axis=-1, keepdims=True
    )
    scale = 1.0 / math.sqrt(query_rows.shape[-1])
    near_ds = (
        (near_p * (near_dp - inner) * (1.0 - near_tanh * near_tanh) * scale)
        .astype(jnp.bfloat16)
        .reshape(shape_wide)
    )
    distant_score_gradient = (
        far_p * (far_dp - inner) * (1.0 - far_tanh * far_tanh) * scale
    ).astype(jnp.bfloat16)
    query_gradient = jnp.einsum(
        "bhukt,bkhet->buhe", near_ds, key_matrix, preferred_element_type=jnp.float32
    )
    query_gradient = query_gradient + jnp.einsum(
        "bhup,phe->buhe",
        distant_score_gradient,
        virtual_key_rows,
        preferred_element_type=jnp.float32,
    )
    key_gradient = jnp.einsum(
        "bhukt,buhe->bkhet", near_ds, query_rows, preferred_element_type=jnp.float32
    )
    value_gradient = jnp.einsum(
        "bhukt,buhe->bkhet", near_b, grad_rows, preferred_element_type=jnp.float32
    )
    virtual_key_gradient = jnp.einsum(
        "mjsr,msjz->rjz", distant_score_gradient, query_rows, preferred_element_type=jnp.float32
    )
    virtual_value_gradient = jnp.einsum(
        "mjsr,msjz->rjz", far_b, grad_rows, preferred_element_type=jnp.float32
    )
    return (
        query_gradient,
        key_gradient,
        value_gradient,
        virtual_key_gradient,
        virtual_value_gradient,
    )


def summarize(totals, counts):
    part_mean = totals / counts[:, None]
    inverse, unit_vn = rms_parts(part_mean)
    return (unit_vn, inverse, unit_vn.astype(jnp.bfloat16))


def back_summary(virtual_node_gradient, unit_vn, inverse, counts):
    inner = jnp.mean(virtual_node_gradient * unit_vn, axis=-1, keepdims=True)
    return inverse * (virtual_node_gradient - unit_vn * inner) / counts[:, None]


def to_heads(local, slices, groups, head_span):
    row_count = local.shape[0]
    strip_rows = row_count // slices
    arranged = jnp.transpose(local.reshape(slices, strip_rows, groups, head_span), (2, 0, 1, 3))
    return arranged.reshape(groups * slices * strip_rows, head_span)


def from_heads(remote, slices, groups, head_span):
    strip_rows = remote.shape[0] // (groups * slices)
    arranged = jnp.transpose(remote.reshape(groups, slices, strip_rows, head_span), (1, 2, 0, 3))
    return arranged.reshape(slices * strip_rows, groups * head_span)


def on_device(
    features,
    gain_attn,
    gain_ffn,
    query_key_value_weight,
    w_out,
    w_in,
    w_down,
    tile_lists,
    tile_count,
    partition,
    grad_out,
):
    row_count, model_width = features.shape
    head_dim = model_width // HEADS
    hidden_units = w_down.shape[0]
    seq_size = lax.axis_size("seq")
    my_index = lax.axis_index("seq")
    parts_all = VN_DEV * seq_size
    x_f = features.astype(jnp.float32)
    inv_attn, unit_attn = rms_parts(x_f)
    normed = (unit_attn * gain_attn).astype(jnp.bfloat16)
    member = (partition[:, None] == jnp.arange(parts_all, dtype=jnp.int32)[None, :]).astype(
        jnp.bfloat16
    )
    member_f = member.astype(jnp.float32)
    part_sums = jnp.einsum("rp,rd->pd", member, normed, preferred_element_type=jnp.float32)
    part_count = jnp.sum(member_f, axis=0)
    totals, counts = lax.psum((part_sums, part_count), "seq")
    unit_vn, inv_vn, virtual = summarize(totals, counts)
    heads_here = 2
    groups = HEADS // heads_here
    slices = seq_size // groups
    my_group = my_index // slices
    my_slice = my_index % slices
    head_span = heads_here * head_dim
    tile_total = seq_size * row_count // TILE
    strip_rows = row_count // slices
    unit_rows = math.gcd(strip_rows, TILE)
    per_strip = strip_rows // unit_rows
    unit_total = seq_size * per_strip
    unit_ids = jnp.arange(unit_total, dtype=jnp.int32)
    unit_start = (
        unit_ids // per_strip * row_count + my_slice * strip_rows + unit_ids % per_strip * unit_rows
    )
    block_units = math.gcd(unit_total, max(1, 512 // unit_rows))
    block_total = unit_total // block_units
    qkv = jnp.dot(normed, query_key_value_weight, preferred_element_type=jnp.float32).astype(
        jnp.bfloat16
    )
    qkv_groups = qkv.reshape(row_count, 3, groups, head_span)
    kv_local = jnp.transpose(qkv_groups[:, 1:], (2, 0, 1, 3))
    kv_send = jnp.broadcast_to(
        kv_local[:, None], (groups, slices, row_count, 2, head_span)
    ).reshape(seq_size * row_count, 2 * head_span)
    kv_all = lax.all_to_all(kv_send, "seq", split_axis=0, concat_axis=0, tiled=True)
    kv_tiles = jnp.transpose(
        kv_all.reshape(tile_total, TILE, 2, heads_here, head_dim), (0, 2, 3, 4, 1)
    )
    query_local = qkv_groups[:, 0].reshape(row_count, model_width)
    q_recv = lax.all_to_all(
        to_heads(query_local, slices, groups, head_span),
        "seq",
        split_axis=0,
        concat_axis=0,
        tiled=True,
    )
    query_rows = q_recv.reshape(unit_total, unit_rows, heads_here, head_dim)
    pattern, counts_all = (
        lax.all_gather(tile_lists, "seq", axis=0, tiled=True),
        lax.all_gather(tile_count, "seq", axis=0, tiled=True),
    )
    unit_tile = unit_start // TILE
    unit_lists = pattern[unit_tile]
    unit_live = (jnp.arange(KT, dtype=jnp.int32)[None, :] < counts_all[unit_tile][:, None]).astype(
        jnp.float32
    )
    key_cols = lax.dynamic_slice_in_dim(
        query_key_value_weight, model_width + my_group * head_span, head_span, 1
    )
    value_cols = lax.dynamic_slice_in_dim(
        query_key_value_weight, 2 * model_width + my_group * head_span, head_span, 1
    )
    virtual_key_rows = (
        jnp.dot(virtual, key_cols, preferred_element_type=jnp.float32)
        .astype(jnp.bfloat16)
        .reshape(parts_all, heads_here, head_dim)
    )
    virtual_value_rows = (
        jnp.dot(virtual, value_cols, preferred_element_type=jnp.float32)
        .astype(jnp.bfloat16)
        .reshape(parts_all, heads_here, head_dim)
    )

    def block_inputs(block_index, query_all):
        first = block_index * block_units
        lists_here = lax.dynamic_slice_in_dim(unit_lists, first, block_units, 0)
        live_here = lax.dynamic_slice_in_dim(unit_live, first, block_units, 0)
        picked = kv_tiles[lists_here]
        key_matrix = picked[:, :, 0]
        value_matrix = picked[:, :, 1]
        active_mask = jnp.broadcast_to(live_here[:, :, None], (block_units, KT, TILE)).reshape(
            block_units, KT * TILE
        )
        query_block = lax.dynamic_slice_in_dim(query_all, first, block_units, 0)
        return (query_block, key_matrix, value_matrix, active_mask, lists_here)

    def forward_block(block_index):
        query_block, key_matrix, value_matrix, active_mask, lists_here = block_inputs(
            block_index, query_rows
        )
        return attend_forward(
            query_block, key_matrix, value_matrix, virtual_key_rows, virtual_value_rows, active_mask
        )

    outs = lax.map(forward_block, jnp.arange(block_total, dtype=jnp.int32))
    out_rows = outs.reshape(unit_total * unit_rows, head_span)
    attn_out = from_heads(
        lax.all_to_all(out_rows, "seq", split_axis=0, concat_axis=0, tiled=True),
        slices,
        groups,
        head_span,
    )
    mixed = jnp.dot(attn_out, w_out, preferred_element_type=jnp.float32)
    resid = (x_f + mixed).astype(jnp.bfloat16)
    res_f = resid.astype(jnp.float32)
    inv_ffn, unit_ffn = rms_parts(res_f)
    normed_ffn = (unit_ffn * gain_ffn).astype(jnp.bfloat16)
    gate_up = jnp.dot(normed_ffn, w_in, preferred_element_type=jnp.float32)
    gate_proj = gate_up[:, :hidden_units]
    up_proj = gate_up[:, hidden_units:]
    sigmoid_gate = jax.nn.sigmoid(gate_proj)
    activated = gate_proj * sigmoid_gate
    hidden = (activated * up_proj).astype(jnp.bfloat16)
    layer_out = (res_f + jnp.dot(hidden, w_down, preferred_element_type=jnp.float32)).astype(
        jnp.bfloat16
    )
    d_hidden = jnp.einsum("rd,fd->rf", grad_out, w_down, preferred_element_type=jnp.float32)
    d_gate = d_hidden * up_proj * sigmoid_gate * (1.0 + gate_proj * (1.0 - sigmoid_gate))
    d_up = d_hidden * activated
    d_both = jnp.concatenate([d_gate, d_up], axis=1).astype(jnp.bfloat16)
    d_normed_ffn = jnp.einsum("rf,df->rd", d_both, w_in, preferred_element_type=jnp.float32)
    scaled_ffn = d_normed_ffn * gain_ffn
    d_resid = (
        grad_out.astype(jnp.float32)
        + inv_ffn
        * (scaled_ffn - unit_ffn * jnp.mean(scaled_ffn * unit_ffn, axis=-1, keepdims=True))
    ).astype(jnp.bfloat16)
    d_attn = jnp.einsum("re,de->rd", d_resid, w_out, preferred_element_type=jnp.float32).astype(
        jnp.bfloat16
    )
    grad_out_local = jnp.einsum("rd,re->de", attn_out, d_resid, preferred_element_type=jnp.float32)
    grad_in_local = jnp.einsum("rd,rf->df", normed_ffn, d_both, preferred_element_type=jnp.float32)
    grad_down_local = jnp.einsum("rf,rd->fd", hidden, grad_out, preferred_element_type=jnp.float32)
    dout_recv = lax.all_to_all(
        to_heads(d_attn, slices, groups, head_span), "seq", split_axis=0, concat_axis=0, tiled=True
    )
    grad_units = dout_recv.reshape(unit_total, unit_rows, heads_here, head_dim)

    def backward_block(carry, block_index):
        key_value_gradient, virtual_key_grad_rows, virtual_value_grad_rows = carry
        query_block, key_matrix, value_matrix, active_mask, lists_here = block_inputs(
            block_index, query_rows
        )
        grad_block = lax.dynamic_slice_in_dim(grad_units, block_index * block_units, block_units, 0)
        (
            query_gradient,
            key_gradient,
            value_gradient,
            virtual_key_gradient,
            virtual_value_gradient,
        ) = attention_backward(
            query_block,
            key_matrix,
            value_matrix,
            virtual_key_rows,
            virtual_value_rows,
            active_mask,
            grad_block,
        )
        kv_pair = jnp.stack([key_gradient, value_gradient], axis=2)
        key_value_gradient = key_value_gradient.at[lists_here].add(kv_pair)
        return (
            (
                key_value_gradient,
                virtual_key_grad_rows + virtual_key_gradient,
                virtual_value_grad_rows + virtual_value_gradient,
            ),
            query_gradient.astype(jnp.bfloat16),
        )

    start_carry = (
        jnp.zeros((tile_total, 2, heads_here, head_dim, TILE), jnp.float32),
        jnp.zeros((parts_all, heads_here, head_dim), jnp.float32),
        jnp.zeros((parts_all, heads_here, head_dim), jnp.float32),
    )
    (key_value_gradient, virtual_key_grad_rows, virtual_value_grad_rows), dq_blocks = lax.scan(
        backward_block, start_carry, jnp.arange(block_total, dtype=jnp.int32)
    )
    dq_rows = dq_blocks.reshape(unit_total * unit_rows, head_span)
    query_gradient = from_heads(
        lax.all_to_all(dq_rows, "seq", split_axis=0, concat_axis=0, tiled=True),
        slices,
        groups,
        head_span,
    )
    kv_rows = jnp.transpose(key_value_gradient, (0, 4, 1, 2, 3)).reshape(
        seq_size * row_count, 2 * head_span
    )
    kv_back = lax.all_to_all(
        kv_rows.astype(jnp.bfloat16), "seq", split_axis=0, concat_axis=0, tiled=True
    ).astype(kv_rows.dtype)
    kv_summed = jnp.sum(kv_back.reshape(groups, slices, row_count, 2, head_span), axis=1)
    d_kv = jnp.transpose(kv_summed, (1, 2, 0, 3)).reshape(row_count, 2 * model_width)
    d_qkv = jnp.concatenate([query_gradient, d_kv.astype(jnp.bfloat16)], axis=1)
    flat_vk = virtual_key_grad_rows.reshape(parts_all, head_span)
    flat_vv = virtual_value_grad_rows.reshape(parts_all, head_span)
    vn_part = jnp.einsum(
        "ps,ds->pd", flat_vk, key_cols.astype(jnp.float32), precision=HIGH_PRECISION
    )
    vn_part = vn_part + jnp.einsum(
        "ps,ds->pd", flat_vv, value_cols.astype(jnp.float32), precision=HIGH_PRECISION
    )
    virtual_node_gradient = lax.psum(vn_part, "seq")
    per_part = back_summary(virtual_node_gradient, unit_vn, inv_vn, counts)
    d_normed = jnp.einsum(
        "rc,dc->rd", d_qkv, query_key_value_weight, preferred_element_type=jnp.float32
    )
    d_normed = d_normed + jnp.dot(member_f, per_part, precision=HIGH_PRECISION)
    scaled_attn = d_normed * gain_attn
    d_features = (
        d_resid.astype(jnp.float32)
        + inv_attn
        * (scaled_attn - unit_attn * jnp.mean(scaled_attn * unit_attn, axis=-1, keepdims=True))
    ).astype(jnp.bfloat16)
    virtual_float = virtual.astype(jnp.float32)
    virt_gk = jnp.einsum("pd,ps->ds", virtual_float, flat_vk, precision=HIGH_PRECISION)
    virt_gv = jnp.einsum("pd,ps->ds", virtual_float, flat_vv, precision=HIGH_PRECISION)
    grad_qkv_local = jnp.einsum("rd,rc->dc", normed, d_qkv, preferred_element_type=jnp.float32)
    grad_qkv_local = grad_qkv_local.reshape(model_width, 3, groups, head_span)
    grad_qkv_local = grad_qkv_local.at[:, 1, my_group].add(virt_gk)
    grad_qkv_local = grad_qkv_local.at[:, 2, my_group].add(virt_gv)
    grad_qkv_local = grad_qkv_local.reshape(model_width, 3 * model_width)
    gain_local = jnp.concatenate(
        [jnp.sum(d_normed * unit_attn, axis=0), jnp.sum(d_normed_ffn * unit_ffn, axis=0)]
    )
    grad_qkv, grad_w_out, grad_w_in, grad_w_down, grad_gains = (
        lax.psum_scatter(grad_qkv_local, "seq", scatter_dimension=0, tiled=True),
        lax.psum_scatter(grad_out_local, "seq", scatter_dimension=0, tiled=True),
        lax.psum_scatter(grad_in_local, "seq", scatter_dimension=0, tiled=True),
        lax.psum_scatter(grad_down_local, "seq", scatter_dimension=0, tiled=True),
        lax.psum_scatter(gain_local, "seq", scatter_dimension=0, tiled=True),
    )
    return (layer_out, d_features, grad_qkv, grad_w_out, grad_w_in, grad_w_down, grad_gains)


def solution(mesh):
    return jax.shard_map(
        on_device,
        mesh=mesh,
        in_specs=(
            P(("groups", "seq"), None),
            P(),
            P(),
            P(),
            P(),
            P(),
            P(),
            P(("groups", "seq"), None),
            P(("groups", "seq")),
            P(("groups", "seq")),
            P(("groups", "seq"), None),
        ),
        out_specs=(
            P(("groups", "seq"), None),
            P(("groups", "seq"), None),
            P(("groups", "seq"), None),
            P(("groups", "seq"), None),
            P(("groups", "seq"), None),
            P(("groups", "seq"), None),
            P(("groups", "seq")),
        ),
        check_vma=False,
    )
```

profile of v0, /device:TPU:0, one launch (start us, length us, event | category | flops | bytes accessed | tf_op | source)
XLA Modules:
  0.0 581.6 jit_solution(9963370828798598010)
XLA Ops:
  8.4 1.8 fusion.81
  10.2 1.9 convolution_convert_fusion
  13.5 7.4 %all-to-all-start.1 = ((bf16[16,2,2048]{2,1,0:T(2,128)(2,1)}), bf16[16,2,2048]{2,1,0:T(2,128)(2,1)S(1)}, u32[]{:S(2)}, u32[]{:S(2)}) async-start(bf16[16,2,2048]{2,1,0:T(2,128)(2,1)} %reshape.427), calls=%async_computation.1 | async-start | bytes 262144 | tf_op jit(solution)/shard_map/all_to_all | solution.py:224
  22.9 12.4 %all-reduce = s32[16]{0:T(128)S(1)} all-reduce(s32[16]{0:T(128)S(1)} %dynamic-update-slice.6), channel_id=1, replica_groups=mesh['groups'=2,'seq'=16] {'seq'}, use_global_device_ids=true, to_apply=%add | all-reduce | flops 16 | bytes 128
  36.9 3.6 all-to-all-start
  40.7 24.6 %all-gather = s32[16,1,4]{2,1,0:T(1,128)S(1)} all-gather(s32[1,1,4]{2,1,0:T(1,128)S(1)} %bitcast.340), channel_id=1, replica_groups=mesh['groups'=2,'seq'=16] {'seq'}, dimensions={0}, use_global_device_ids=true | all-gather | bytes 272 | tf_op jit(solution)/shard_map/all_gather | solution.py:233
  66.5 31.4 %psum.22 = f32[32]{0:T(128)S(1)} all-reduce(f32[32]{0:T(128)S(1)} %convert_reduce_fusion), channel_id=1, replica_groups=mesh['groups'=2,'seq'=16] {'seq'}, use_global_device_ids=true, to_apply=%region_3.0 | all-reduce | flops 32 | bytes 256 | tf_op jit(solution)/shard_map/psum | solution.py:192
  97.9 1.8 all-reduce.5.cloned.1.call-done
  100.7 1.2 convolution_convert_fusion.3
  102.0 1.2 convolution_convert_fusion.2
  104.6 15.0 %while.35 = (s32[]{:T(128)}, bf16[2,8,64,2,32]{2,4,3,1,0:T(8,128)(2,1)}, s32[2]{0:T(128)S(1)}, s32[16,4]{1,0:T(8,128)}, bf16[16,2,2,32,128]{4,3,2,1,0:T(8,128)(2...) while((s32[]{:T(128)}, ...), condition=%wide.region_8.9_spmd, body=%wide.region_5.8_spmd.sunk | while | flops 74678368 | bytes 10421959 | solution.py:279
  106.6 1.7 gather_fusion
  108.2 1.3 fusion.156
  114.1 1.7 gather_fusion
  115.7 1.3 fusion.156
  119.5 1.9 reshape.429
  121.5 14.3 %all_to_all.51 = bf16[16,2,2048]{2,1,0:T(2,128)(2,1)} all-to-all(bf16[16,2,2048]{2,1,0:T(2,128)(2,1)} %reshape.429), channel_id=1, replica_groups=mesh['groups'=2,'seq'=16] {'seq'}, dimensions={0} | all-to-all | bytes 262144 | tf_op jit(solution)/shard_map/all_to_all | solution.py:282
  135.8 1.8 reshape.430
  137.6 1.8 copy.282
  139.4 1.8 reshape.342
  141.3 1.3 multiply_reduce_fusion.4
  143.1 1.3 multiply_convert_fusion.2
  144.4 1.4 multiply_reduce_fusion.2
  149.1 3.5 all-to-all-start.3
  153.6 1.3 copy.286
  155.0 5.5 all-to-all-done.3
  163.4 52.0 %while.36 = (s32[]{:T(128)}, f32[16,2,2,32,128]{4,3,2,1,0:T(8,128)}, f32[32,2,32]{0,2,1:T(8,128)}, f32[32,2,32]{0,2,1:T(8,128)}, bf16[2,8,64,2,32]{2,4,3,1,0:T(8...) while((s32[]{:T(128)}, ...), condition=%wide.region_17.18_spmd.clone, body=%wide.region_11.17_spmd.clone.sunk | while | flops 193567840 | bytes 63889748 | solution.py:360
  166.5 1.7 gather_fusion.1
  168.1 1.3 fusion.171
  170.7 1.2 multiply_reduce_fusion.9
  172.9 1.2 multiply_convert_fusion.13
  176.1 1.8 fusion.175
  180.4 1.5 copy.389
  181.9 7.0 %scatter_fusion = f32[16,2,2,32,128]{4,3,2,1,0:T(8,128)} fusion(f32[16,2,2,32,128]{4,3,2,1,0:T(8,128)} %get-tuple-element.901, s32[32]{0:T(128)S(1)} %reshape.450, f32[32,2,2,32,128]{4,3,2,1,0:T(8,128)} %bitcast.318), kind=kCustom, calls=%fused_computation.4.clone.clone.1 | custom fusion | flops 524288 | bytes 6291584 | tf_op jit(solution)/shard_map/while/body/eval_jaxpr/scatter-add | solution.py:345
  192.1 1.7 gather_fusion.1
  193.8 1.3 fusion.171
  196.3 1.2 multiply_reduce_fusion.9
  198.5 1.2 multiply_convert_fusion.13
  201.7 1.8 fusion.175
  203.5 1.5 fusion.174
  206.8 1.5 copy.389
  208.3 7.0 %scatter_fusion = f32[16,2,2,32,128]{4,3,2,1,0:T(8,128)} fusion(f32[16,2,2,32,128]{4,3,2,1,0:T(8,128)} %get-tuple-element.901, s32[32]{0:T(128)S(1)} %reshape.450, f32[32,2,2,32,128]{4,3,2,1,0:T(8,128)} %bitcast.318), kind=kCustom, calls=%fused_computation.4.clone.clone.1 | custom fusion | flops 524288 | bytes 6291584 | tf_op jit(solution)/shard_map/while/body/eval_jaxpr/scatter-add | solution.py:345
  215.4 1.3 fusion.69
  216.7 1.9 convolution_add_fusion.3
  218.7 2.3 fusion.105
  221.0 1.9 fusion.106
  222.9 1.9 reshape.433
  224.8 3.5 all-to-all-start.4
  229.2 7.1 %all-to-all-done.4 = bf16[16,2,2048]{2,1,0:T(2,128)(2,1)S(1)} async-done(((bf16[16,2,2048]{2,1,0:T(2,128)(2,1)}), bf16[16,2,2048]{2,1,0:T(2,128)(2,1)S(1)}, u32[]{:S(2)}, u32[]{:S(2)}) %all-to-all-start.4) | async-done | bytes 131104 | tf_op jit(solution)/shard_map/all_to_all | solution.py:365
  236.3 3.6 all-to-all-start.5
  243.1 11.2 %all-to-all-done.5 = bf16[16,128,128]{1,2,0:T(8,128)(2,1)S(1)} async-done(((bf16[16,128,128]{1,2,0:T(8,128)(2,1)}), bf16[16,128,128]{1,2,0:T(8,128)(2,1)S(1)}, u32[]{:S(2)}, u32[]{:S(2)}) %all-to-all-start.5) | async-done | bytes 524320 | tf_op jit(solution)/shard_map/all_to_all | solution.py:373
  254.5 2.3 fusion.65
  256.8 2.5 fusion.46
  259.3 2.5 fusion.49
  261.8 3.6 copy.292
  266.4 3.7 fusion.55
  270.7 2.2 fusion.43
  273.0 28.3 %all-reduce.7.cloned.1.call-done = f32[32,512]{1,0:T(8,128)} async-done(((f32[32,512]{1,0:T(8,128)}), f32[32,512]{1,0:T(8,128)}) %all-reduce.7.cloned.1.call-update) | async-done | bytes 65552 | tf_op jit(solution)/shard_map/psum | solution.py:387
  302.3 2.1 fusion.66
  304.9 31.9 %all-reduce.1 = f32[1024]{0:T(1024)S(1)} all-reduce(f32[1024]{0:T(1024)S(1)} %pad_maximum_fusion.7), channel_id=6, replica_groups=mesh['groups'=2,'seq'=16] {'seq'}, use_global_device_ids=true, to_apply=%region_30.31.clone | all-reduce | flops 1024 | bytes 8192
  338.2 26.3 %reduce-scatter.7.cloned.1.call-done = f32[32,512]{1,0:T(8,128)} async-done(((f32[512,512]{1,0:T(8,128)}), f32[32,512]{1,0:T(8,128)}) %reduce-scatter.7.cloned.1.call-update) | async-done | bytes 65552 | tf_op jit(solution)/shard_map/reduce_scatter | solution.py:412
  364.5 65.3 %reduce-scatter.11.cloned.1.call-done = f32[64,512]{1,0:T(8,128)} async-done(((f32[1024,512]{1,0:T(8,128)}), f32[64,512]{1,0:T(8,128)}) %reduce-scatter.11.cloned.1.call-update) | async-done | bytes 131088 | tf_op jit(solution)/shard_map/reduce_scatter | solution.py:414
  429.7 69.4 %reduce-scatter.5.cloned.1.call-done = f32[32,1536]{1,0:T(8,128)} async-done(((f32[512,1536]{1,0:T(8,128)}), f32[32,1536]{1,0:T(8,128)}) %reduce-scatter.5.cloned.1.call-update) | async-done | bytes 196624 | tf_op jit(solution)/shard_map/reduce_scatter | solution.py:411
  499.2 75.6 %reduce-scatter.9.cloned.1.call-done = f32[32,2048]{1,0:T(8,128)} async-done(((f32[512,2048]{1,0:T(8,128)}), f32[32,2048]{1,0:T(8,128)}) %reduce-scatter.9.cloned.1.call-update) | async-done | bytes 262160 | tf_op jit(solution)/shard_map/reduce_scatter | solution.py:413
  (271 shorter events, 50.3 us)
Async XLA Ops:
  7.2 135.4 %copy-start = (bf16[512,2048]{1,0:T(8,128)(2,1)S(1)}, bf16[512,2048]{1,0:T(8,128)(2,1)}, u32[]{:S(2)}) copy-start(bf16[512,2048]{1,0:T(8,128)(2,1)} %param.24) | copy-start | bytes 6291460
  7.2 92.5 %all-reduce.5.cloned.1.call-start = ((), (), s32[]{:S(2)}) async-start(), calls=%async_computation.10 | async-start | bytes 131072 | tf_op jit(solution)/shard_map/psum | solution.py:192
  10.2 11.3 %copy-start.44 = (u32[32]{0:T(128)S(1)}, u32[32]{0:T(128)}, u32[]{:S(2)}) copy-start(u32[32]{0:T(128)} %constant.294) | copy-start | bytes 388
  12.6 28.0 %copy-start.50 = (s32[128]{0:T(128)S(1)}, s32[128]{0:T(128)}, u32[]{:S(2)}) copy-start(s32[128]{0:T(128)} %param.28) | copy-start | bytes 1540
  12.6 28.2 %copy-start.48 = (s32[1,4]{1,0:T(1,128)S(1)}, s32[1,4]{1,0:T(1,128)}, u32[]{:S(2)}) copy-start(s32[1,4]{1,0:T(1,128)} %param.26) | copy-start | bytes 52
  13.5 22.5 %all-to-all-start.1 = ((bf16[16,2,2048]{2,1,0:T(2,128)(2,1)}), bf16[16,2,2048]{2,1,0:T(2,128)(2,1)S(1)}, u32[]{:S(2)}, u32[]{:S(2)}) async-start(bf16[16,2,2048]{2,1,0:T(2,128)(2,1)} %reshape.427), calls=%async_computation.1 | async-start | bytes 262144 | tf_op jit(solution)/shard_map/all_to_all | solution.py:224
  36.9 66.8 %all-to-all-start = ((bf16[16,128,128]{1,2,0:T(8,128)(2,1)}), bf16[16,128,128]{1,2,0:T(8,128)(2,1)S(1)}, u32[]{:S(2)}, u32[]{:S(2)}) async-start(bf16[16,128,128]{1,2,0:T(8,128)(2,1)} %bitcast.20), calls=%async_computation | async-start | bytes 1048576 | tf_op jit(solution)/shard_map/all_to_all | solution.py:219
  97.9 4.1 copy-start.42
  102.0 2.6 copy-start.31
  104.6 36.7 %copy-start.8 = (bf16[128,512]{1,0:T(8,128)(2,1)S(1)}, bf16[128,512]{1,0:T(8,128)(2,1)}, u32[]{:S(2)}) copy-start(bf16[128,512]{1,0:T(8,128)(2,1)} %param.19) | copy-start | bytes 393220
  119.5 21.7 %copy-start.12 = (bf16[512,512]{1,0:T(8,128)(2,1)S(1)}, bf16[512,512]{1,0:T(8,128)(2,1)}, u32[]{:S(2)}) copy-start(bf16[512,512]{1,0:T(8,128)(2,1)} %param.23) | copy-start | bytes 1572868
  119.5 23.1 %copy-start.35 = (f32[512]{0:T(512)S(1)}, f32[512]{0:T(512)}, u32[]{:S(2)}) copy-start(f32[512]{0:T(512)} %param.21) | copy-start | bytes 6148
  141.3 1.9 copy-start.23
  142.6 3.3 copy-start.6
  142.6 3.3 copy-start.38
  146.0 16.6 %copy-start.13 = (bf16[128,512]{1,0:T(8,128)(2,1)}, bf16[128,512]{1,0:T(8,128)(2,1)S(1)}, u32[]{:S(2)}) copy-start(bf16[128,512]{1,0:T(8,128)(2,1)S(1)} %add_convert_fusion) | copy-start | bytes 393220
  149.1 11.4 %all-to-all-start.3 = ((bf16[16,2,2048]{2,1,0:T(2,128)(2,1)}), bf16[16,2,2048]{2,1,0:T(2,128)(2,1)S(1)}, u32[]{:S(2)}, u32[]{:S(2)}) async-start(bf16[16,2,2048]{2,1,0:T(2,128)(2,1)} %reshape.431), calls=%async_computation.3 | async-start | bytes 262144 | tf_op jit(solution)/shard_map/all_to_all | solution.py:318
  152.6 148.7 %all-reduce.7.cloned.1.call-start = ((), (), s32[]{:S(2)}) async-start(), calls=%async_computation.11 | async-start | bytes 131072 | tf_op jit(solution)/shard_map/psum | solution.py:387
  163.4 2.3 copy-start.52
  163.4 4.7 copy-start.10
  163.4 6.0 %copy-start.1 = (bf16[16,2,2,32,128]{4,3,2,1,0:T(8,128)(2,1)}, bf16[16,2,2,32,128]{4,3,2,1,0:T(8,128)(2,1)S(1)}, u32[]{:S(2)}) copy-start(bf16[16,2,2,32,128]{4,3,2,1,0:T(8,128)(2,1)S(1)} %get-tuple-element.925) | copy-start | bytes 1572868 | tf_op jit(solution)/shard_map/while
  163.4 6.0 %copy-start.25 = (f32[16,4]{1,0:T(8,128)}, f32[16,4]{1,0:T(8,128)S(1)}, u32[]{:S(2)}) copy-start(f32[16,4]{1,0:T(8,128)S(1)} %get-tuple-element.926) | copy-start | bytes 772 | tf_op jit(solution)/shard_map/while
  163.4 7.0 %copy-start.21 = (bf16[32,2,32]{0,2,1:T(8,128)(2,1)}, bf16[32,2,32]{0,2,1:T(8,128)(2,1)S(1)}, u32[]{:S(2)}) copy-start(bf16[32,2,32]{0,2,1:T(8,128)(2,1)S(1)} %get-tuple-element.927) | copy-start | bytes 12292 | tf_op jit(solution)/shard_map/while
  170.4 2.5 copy-start.4
  176.1 2.9 copy-start.5
  181.9 7.0 %copy-start.2 = (bf16[16,2,2,32,128]{4,3,2,1,0:T(8,128)(2,1)S(1)}, bf16[16,2,2,32,128]{4,3,2,1,0:T(8,128)(2,1)}, u32[]{:S(2)}) copy-start(bf16[16,2,2,32,128]{4,3,2,1,0:T(8,128)(2,1)} %copy-done.1) | copy-start | bytes 1572868 | tf_op jit(solution)/shard_map/while
  181.9 7.0 %copy-start.11 = (bf16[16,64,2,32]{1,3,2,0:T(8,128)(2,1)S(1)}, bf16[16,64,2,32]{1,3,2,0:T(8,128)(2,1)}, u32[]{:S(2)}) copy-start(bf16[16,64,2,32]{1,3,2,0:T(8,128)(2,1)} %copy-done.10) | copy-start | bytes 393220 | tf_op jit(solution)/shard_map/while
  181.9 7.0 %copy-start.22 = (bf16[32,2,32]{0,2,1:T(8,128)(2,1)S(1)}, bf16[32,2,32]{0,2,1:T(8,128)(2,1)}, u32[]{:S(2)}) copy-start(bf16[32,2,32]{0,2,1:T(8,128)(2,1)} %copy-done.21) | copy-start | bytes 12292 | tf_op jit(solution)/shard_map/while
  181.9 7.0 %copy-start.26 = (f32[16,4]{1,0:T(8,128)S(1)}, f32[16,4]{1,0:T(8,128)}, u32[]{:S(2)}) copy-start(f32[16,4]{1,0:T(8,128)} %copy-done.25) | copy-start | bytes 772 | tf_op jit(solution)/shard_map/while
  181.9 7.0 %copy-start.53 = (s32[2]{0:T(128)S(1)}, s32[2]{0:T(128)}, u32[]{:S(2)}) copy-start(s32[2]{0:T(128)} %copy-done.52) | copy-start | bytes 28 | tf_op jit(solution)/shard_map/while
  189.0 2.3 copy-start.52
  189.0 4.8 copy-start.10
  189.0 6.1 %copy-start.1 = (bf16[16,2,2,32,128]{4,3,2,1,0:T(8,128)(2,1)}, bf16[16,2,2,32,128]{4,3,2,1,0:T(8,128)(2,1)S(1)}, u32[]{:S(2)}) copy-start(bf16[16,2,2,32,128]{4,3,2,1,0:T(8,128)(2,1)S(1)} %get-tuple-element.925) | copy-start | bytes 1572868 | tf_op jit(solution)/shard_map/while
  189.0 6.1 %copy-start.25 = (f32[16,4]{1,0:T(8,128)}, f32[16,4]{1,0:T(8,128)S(1)}, u32[]{:S(2)}) copy-start(f32[16,4]{1,0:T(8,128)S(1)} %get-tuple-element.926) | copy-start | bytes 772 | tf_op jit(solution)/shard_map/while
  189.0 7.0 %copy-start.21 = (bf16[32,2,32]{0,2,1:T(8,128)(2,1)}, bf16[32,2,32]{0,2,1:T(8,128)(2,1)S(1)}, u32[]{:S(2)}) copy-start(bf16[32,2,32]{0,2,1:T(8,128)(2,1)S(1)} %get-tuple-element.927) | copy-start | bytes 12292 | tf_op jit(solution)/shard_map/while
  196.0 2.5 copy-start.4
  201.7 3.7 copy-start.5
  208.3 7.0 %copy-start.2 = (bf16[16,2,2,32,128]{4,3,2,1,0:T(8,128)(2,1)S(1)}, bf16[16,2,2,32,128]{4,3,2,1,0:T(8,128)(2,1)}, u32[]{:S(2)}) copy-start(bf16[16,2,2,32,128]{4,3,2,1,0:T(8,128)(2,1)} %copy-done.1) | copy-start | bytes 1572868 | tf_op jit(solution)/shard_map/while
  208.3 7.0 %copy-start.11 = (bf16[16,64,2,32]{1,3,2,0:T(8,128)(2,1)S(1)}, bf16[16,64,2,32]{1,3,2,0:T(8,128)(2,1)}, u32[]{:S(2)}) copy-start(bf16[16,64,2,32]{1,3,2,0:T(8,128)(2,1)} %copy-done.10) | copy-start | bytes 393220 | tf_op jit(solution)/shard_map/while
  208.3 7.0 %copy-start.22 = (bf16[32,2,32]{0,2,1:T(8,128)(2,1)S(1)}, bf16[32,2,32]{0,2,1:T(8,128)(2,1)}, u32[]{:S(2)}) copy-start(bf16[32,2,32]{0,2,1:T(8,128)(2,1)} %copy-done.21) | copy-start | bytes 12292 | tf_op jit(solution)/shard_map/while
  208.3 7.0 %copy-start.26 = (f32[16,4]{1,0:T(8,128)S(1)}, f32[16,4]{1,0:T(8,128)}, u32[]{:S(2)}) copy-start(f32[16,4]{1,0:T(8,128)} %copy-done.25) | copy-start | bytes 772 | tf_op jit(solution)/shard_map/while
  208.3 7.0 %copy-start.53 = (s32[2]{0:T(128)S(1)}, s32[2]{0:T(128)}, u32[]{:S(2)}) copy-start(s32[2]{0:T(128)} %copy-done.52) | copy-start | bytes 28 | tf_op jit(solution)/shard_map/while
  215.4 5.6 copy-start.17
  215.4 5.6 copy-start.24
  218.6 145.8 %reduce-scatter.7.cloned.1.call-start = ((), (), s32[]{:S(2)}) async-start(), calls=%async_computation.13 | async-start | bytes 1114112 | tf_op jit(solution)/shard_map/reduce_scatter | solution.py:412
  220.9 208.8 %reduce-scatter.11.cloned.1.call-start = ((), (), s32[]{:S(2)}) async-start(), calls=%async_computation.15 | async-start | bytes 2228224 | tf_op jit(solution)/shard_map/reduce_scatter | solution.py:414
  221.0 7.3 %copy-start.3 = (f32[16,2,2,32,128]{4,3,2,1,0:T(8,128)S(1)}, f32[16,2,2,32,128]{4,3,2,1,0:T(8,128)}, u32[]{:S(2)}) copy-start(f32[16,2,2,32,128]{4,3,2,1,0:T(8,128)} %get-tuple-element.370) | copy-start | bytes 3145732
  222.9 17.0 %copy-start.49 = (s32[4]{0:T(128)S(1)}, s32[4]{0:T(128)}, u32[]{:S(2)}) copy-start(s32[4]{0:T(128)} %constant.286.clone.1) | copy-start | bytes 52
  224.8 11.5 %all-to-all-start.4 = ((bf16[16,2,2048]{2,1,0:T(2,128)(2,1)}), bf16[16,2,2048]{2,1,0:T(2,128)(2,1)S(1)}, u32[]{:S(2)}, u32[]{:S(2)}) async-start(bf16[16,2,2048]{2,1,0:T(2,128)(2,1)} %reshape.433), calls=%async_computation.4 | async-start | bytes 262144 | tf_op jit(solution)/shard_map/all_to_all | solution.py:365
  229.2 25.3 %copy-start.9 = (bf16[128,512]{1,0:T(8,128)(2,1)S(1)}, bf16[128,512]{1,0:T(8,128)(2,1)}, u32[]{:S(2)}) copy-start(bf16[128,512]{1,0:T(8,128)(2,1)} %param.19) | copy-start | bytes 393220
  229.2 25.3 %copy-start.34 = (f32[512]{0:T(512)S(1)}, f32[512]{0:T(512)}, u32[]{:S(2)}) copy-start(f32[512]{0:T(512)} %param.20) | copy-start | bytes 6148
  229.2 25.3 %copy-start.41 = (f32[128]{0:T(128)S(1)}, f32[128]{0:T(128)}, u32[]{:S(2)}) copy-start(f32[128]{0:T(128)} %copy-done.40) | copy-start | bytes 1540
  236.3 18.0 %all-to-all-start.5 = ((bf16[16,128,128]{1,2,0:T(8,128)(2,1)}), bf16[16,128,128]{1,2,0:T(8,128)(2,1)S(1)}, u32[]{:S(2)}, u32[]{:S(2)}) async-start(bf16[16,128,128]{1,2,0:T(8,128)(2,1)} %bitcast.325), calls=%async_computation.5 | async-start | bytes 1048576 | tf_op jit(solution)/shard_map/all_to_all | solution.py:373
  239.9 259.3 %reduce-scatter.5.cloned.1.call-start = ((), (), s32[]{:S(2)}) async-start(), calls=%async_computation.12 | async-start | bytes 3342336 | tf_op jit(solution)/shard_map/reduce_scatter | solution.py:411
  254.4 2.4 copy-start.15
  254.4 2.4 copy-start.30
  254.4 2.4 copy-start.43
  254.4 2.4 copy-start.47
  254.5 4.9 copy-start.16
  265.4 309.3 %reduce-scatter.9.cloned.1.call-start = ((), (), s32[]{:S(2)}) async-start(), calls=%async_computation.14 | async-start | bytes 4456448 | tf_op jit(solution)/shard_map/reduce_scatter | solution.py:413
  270.2 34.3 %copy-start.51 = (s32[128]{0:T(128)S(1)}, s32[128]{0:T(128)}, u32[]{:S(2)}) copy-start(s32[128]{0:T(128)} %param.28) | copy-start | bytes 1540
  272.9 32.0 %copy-start.45 = (f32[512]{0:T(512)S(1)}, f32[512]{0:T(512)}, u32[]{:S(2)}) copy-start(f32[512]{0:T(512)} %get-tuple-element.591) | copy-start | bytes 6148
  272.9 64.4 %copy-start.14 = (bf16[128,512]{1,0:T(8,128)(2,1)S(1)}, bf16[128,512]{1,0:T(8,128)(2,1)}, u32[]{:S(2)}) copy-start(bf16[128,512]{1,0:T(8,128)(2,1)} %copy-done.13) | copy-start | bytes 393220
  301.2 3.2 copy-start.33
  (16 other events, 20.5 us)
Sparse Core Ops, SparseCore 0:
  12.1 87.5 all-reduce.4
  218.7 82.4 all-reduce.6
  305.4 58.9 reduce-scatter.6
  369.1 60.6 reduce-scatter.10
  434.0 65.1 reduce-scatter.4
  503.4 71.2 reduce-scatter.8
where the time goes:
time: 584 us; the launch traced here: 582 us
  waiting for transfers between devices  290 us (50%)
  blocking collectives  115 us (20%)
  matrix products  55.9 us (10%)
  local copies, waits for them, and re-layouts  51.9 us (9%)
  other arithmetic  27.5 us (5%)
  starting transfers between devices  22 us (4%)
  between operations  16 us (3%)
    reduce_scatter x1, waiting for transfers between devices, on_device(): lax.psum_scatter(grad_in_local, 'seq', scatter_dimension=0, tiled=True)  75.6 us
    reduce_scatter x1, waiting for transfers between devices, on_device(): lax.psum_scatter(grad_qkv_local, 'seq', scatter_dimension=0, tiled=True)  69.4 us
    reduce_scatter x1, waiting for transfers between devices, on_device(): lax.psum_scatter(grad_down_local, 'seq', scatter_dimension=0, tiled=True)  65.3 us
    unnamed x2, blocking collectives  44.3 us
    psum x1, blocking collectives, on_device(): totals, counts = lax.psum((part_sums, part_count), 'seq')  31.4 us
    psum x1, waiting for transfers between devices, on_device(): virtual_node_gradient = lax.psum(vn_part, 'seq')  28.3 us
    reduce_scatter x1, waiting for transfers between devices, on_device(): lax.psum_scatter(grad_out_local, 'seq', scatter_dimension=0, tiled=True)  26.3 us
    all_gather x1, blocking collectives, on_device(): lax.all_gather(tile_lists, 'seq', axis=0, tiled=True)  24.6 us
  transfers between devices with their start and end apart: 11, of which 9 were waited for; matrix products, arithmetic and copies ran while one was open for 8% of the time, Pallas kernels for 0%

commit v1 on v0

v1 whole, which is shorter than its diff:
```python
import functools
import math

import jax
import jax.numpy as jnp
from jax import lax
from jax.experimental import pallas as pl
from jax.experimental.pallas import tpu as pltpu
from jax.sharding import PartitionSpec as P

HEADS = 16
KT = 4
VN_DEV = 2
CAP = 30.0
EPS = 1e-06
HIGH_PRECISION = lax.Precision.HIGHEST
VMEM_BYTES = 48 * 1024 * 1024


def rms_parts(values):
    inverse = lax.rsqrt(jnp.mean(values * values, axis=-1, keepdims=True) + EPS)
    return (inverse, values * inverse)


def dot_tn(a, b):
    return lax.dot_general(a, b, (((0,), (0,)), ((), ())), preferred_element_type=jnp.float32)


def dot_nt(a, b):
    return lax.dot_general(a, b, (((1,), (1,)), ((), ())), preferred_element_type=jnp.float32)


def dot_nn(a, b):
    return jnp.dot(a, b, preferred_element_type=jnp.float32)


def tile_weights(lists_ref, qkv_ref, virt_ref, t, head_dim):
    count = lists_ref[t, KT]
    query = qkv_ref[lists_ref[t, 0], 0:head_dim, :]
    scale = 1.0 / (math.sqrt(head_dim) * CAP)
    tanhs, weights = [], []
    for j in range(KT):
        keys = qkv_ref[lists_ref[t, j], head_dim : 2 * head_dim, :]
        th = jnp.tanh(dot_tn(keys, query) * scale)
        w = jnp.exp(CAP * th)
        if j:
            w = w * jnp.where(j < count, 1.0, 0.0)
        tanhs.append(th)
        weights.append(w)
    th = jnp.tanh(dot_tn(virt_ref[0], query) * scale)
    tanhs.append(th)
    weights.append(jnp.exp(CAP * th))
    total = jnp.sum(weights[0], axis=0, keepdims=True)
    for w in weights[1:]:
        total = total + jnp.sum(w, axis=0, keepdims=True)
    inverse = 1.0 / total
    return query, tanhs, [w * inverse for w in weights]


def forward_kernel(head_dim, lists_ref, qkv_ref, virt_ref, out_ref):
    def body(t, carry):
        _, _, probs = tile_weights(lists_ref, qkv_ref, virt_ref, t, head_dim)
        out = dot_nn(virt_ref[1], probs[KT].astype(jnp.bfloat16))
        for j in range(KT):
            values = qkv_ref[lists_ref[t, j], 2 * head_dim : 3 * head_dim, :]
            out = out + dot_nn(values, probs[j].astype(jnp.bfloat16))
        out_ref[t] = out.astype(jnp.bfloat16)
        return carry

    lax.fori_loop(0, out_ref.shape[0], body, 0, unroll=2)


def backward_kernel(
    head_dim, lists_ref, qkv_ref, virt_ref, grad_ref, dq_ref, dkv_ref, dvirt_ref, acc_ref
):
    scale = 1.0 / math.sqrt(head_dim)
    acc_ref[...] = jnp.zeros_like(acc_ref)
    dvirt_ref[...] = jnp.zeros_like(dvirt_ref)

    def body(t, carry):
        query, tanhs, probs = tile_weights(lists_ref, qkv_ref, virt_ref, t, head_dim)
        grad = grad_ref[t]
        dps = []
        for j in range(KT):
            values = qkv_ref[lists_ref[t, j], 2 * head_dim : 3 * head_dim, :]
            dps.append(dot_tn(values, grad))
        dps.append(dot_tn(virt_ref[1], grad))
        inner = jnp.sum(probs[0] * dps[0], axis=0, keepdims=True)
        for j in range(1, KT + 1):
            inner = inner + jnp.sum(probs[j] * dps[j], axis=0, keepdims=True)
        ds = [
            (p * (dp - inner) * (1.0 - th * th) * scale).astype(jnp.bfloat16)
            for p, dp, th in zip(probs, dps, tanhs)
        ]
        pb = [p.astype(jnp.bfloat16) for p in probs]
        dq = dot_nn(virt_ref[0], ds[KT])
        for j in range(KT):
            dq = dq + dot_nn(qkv_ref[lists_ref[t, j], head_dim : 2 * head_dim, :], ds[j])
        dq_ref[t] = dq.astype(jnp.bfloat16)
        for j in range(KT):
            target = lists_ref[t, j]
            acc_ref[target, 0:head_dim, :] += dot_nt(query, ds[j])
            acc_ref[target, head_dim : 2 * head_dim, :] += dot_nt(grad, pb[j])
        dvirt_ref[0:head_dim, :] += dot_nt(query, ds[KT])
        dvirt_ref[head_dim : 2 * head_dim, :] += dot_nt(grad, pb[KT])
        return carry

    lax.fori_loop(0, grad_ref.shape[0], body, 0)
    dkv_ref[...] = acc_ref[...].astype(jnp.bfloat16)


def attention_forward(lists, qkv_all, virt, head_dim):
    tiles_here = lists.shape[0]
    rows = qkv_all.shape[2]
    pairs = tiles_here * rows * (KT * rows + virt.shape[2])
    vmem = pl.BlockSpec(memory_space=pltpu.VMEM)
    return pl.pallas_call(
        functools.partial(forward_kernel, head_dim),
        out_shape=jax.ShapeDtypeStruct((tiles_here, head_dim, rows), jnp.bfloat16),
        in_specs=[pl.BlockSpec(memory_space=pltpu.SMEM), vmem, vmem],
        out_specs=vmem,
        compiler_params=pltpu.CompilerParams(vmem_limit_bytes=VMEM_BYTES),
        cost_estimate=pl.CostEstimate(
            flops=4 * pairs * head_dim, bytes_accessed=2 * qkv_all.size, transcendentals=2 * pairs
        ),
    )(lists, qkv_all, virt)


def attention_backward(lists, qkv_all, virt, grads, head_dim):
    tiles_here, _, rows = grads.shape
    tiles = qkv_all.shape[0]
    parts = virt.shape[2]
    pairs = tiles_here * rows * (KT * rows + parts)
    vmem = pl.BlockSpec(memory_space=pltpu.VMEM)
    return pl.pallas_call(
        functools.partial(backward_kernel, head_dim),
        out_shape=(
            jax.ShapeDtypeStruct((tiles_here, head_dim, rows), jnp.bfloat16),
            jax.ShapeDtypeStruct((tiles, 2 * head_dim, rows), jnp.bfloat16),
            jax.ShapeDtypeStruct((2 * head_dim, parts), jnp.float32),
        ),
        in_specs=[pl.BlockSpec(memory_space=pltpu.SMEM), vmem, vmem, vmem],
        out_specs=(vmem, vmem, vmem),
        scratch_shapes=[pltpu.VMEM((tiles, 2 * head_dim, rows), jnp.float32)],
        compiler_params=pltpu.CompilerParams(vmem_limit_bytes=VMEM_BYTES),
        cost_estimate=pl.CostEstimate(
            flops=10 * pairs * head_dim, bytes_accessed=6 * qkv_all.size, transcendentals=2 * pairs
        ),
    )(lists, qkv_all, virt, grads)


def all_to_all(blocks):
    return lax.all_to_all(blocks, "seq", split_axis=0, concat_axis=0, tiled=True)


def reduce_scatter(blocks):
    size, rows, columns = blocks.shape
    me = lax.axis_index("seq")

    def halve(held, bit):
        mine = (me // bit) % 2
        split = held.reshape(held.shape[0] // 2, 2, rows, columns)
        keep = lax.dynamic_index_in_dim(split, mine, 1, keepdims=False)
        send = lax.dynamic_index_in_dim(split, 1 - mine, 1, keepdims=False)
        got = lax.ppermute(send, "seq", [(i, i ^ bit) for i in range(size)])
        return (keep.astype(jnp.float32) + got.astype(jnp.float32)).astype(jnp.bfloat16)

    held = halve(halve(blocks, 1), 2)
    count = size // 4
    if count > 4:
        groups = [[j + 4 * m for m in range(count)] for j in range(4)]
        got = lax.all_to_all(
            held, "seq", split_axis=0, concat_axis=0, axis_index_groups=groups, tiled=True
        )
        return jnp.sum(got.astype(jnp.float32), axis=0)
    mine = me // 4
    total = lax.dynamic_index_in_dim(held, mine, 0, keepdims=False).astype(jnp.float32)
    for k in range(1, count):
        send = lax.dynamic_index_in_dim(held, (mine + k) % count, 0, keepdims=False)
        perm = [(i, ((i // 4 + k) % count) * 4 + i % 4) for i in range(size)]
        total = total + lax.ppermute(send, "seq", perm).astype(jnp.float32)
    return total


def on_device(
    features,
    gain_attn,
    gain_ffn,
    query_key_value_weight,
    w_out,
    w_in,
    w_down,
    tile_lists,
    tile_count,
    partition,
    grad_out,
):
    rows, width = features.shape
    head_dim = width // HEADS
    hidden_units = w_down.shape[0]
    seq_size = lax.axis_size("seq")
    me = lax.axis_index("seq")
    parts = VN_DEV * seq_size
    slices = seq_size // HEADS
    my_head = me // slices
    my_slice = me % slices
    tiles_here = seq_size // slices
    slice_of_me = me // tiles_here

    x_f = features.astype(jnp.float32)
    inv_attn, unit_attn = rms_parts(x_f)
    normed = (unit_attn * gain_attn).astype(jnp.bfloat16)
    member = (partition[:, None] == jnp.arange(parts, dtype=jnp.int32)[None, :]).astype(
        jnp.bfloat16
    )
    extended = jnp.concatenate([normed, jnp.ones((rows, 128), jnp.bfloat16)], axis=1)
    part_sums = jnp.einsum("rp,rd->pd", member, extended, preferred_element_type=jnp.float32)
    wide = width + 128
    list_row = jnp.concatenate([tile_lists[0], tile_count]).astype(jnp.float32)
    list_row = jnp.pad(list_row, (0, wide - KT - 1))
    first_send = jnp.concatenate(
        [
            part_sums.reshape(seq_size, VN_DEV, wide),
            jnp.broadcast_to(list_row, (seq_size, 1, wide)),
        ],
        axis=1,
    )
    first = all_to_all(first_send)
    own_sums = jnp.sum(first[:, :VN_DEV], axis=0)
    lists_all = first[:, VN_DEV, : KT + 1].astype(jnp.int32)
    second = all_to_all(jnp.broadcast_to(own_sums, (seq_size, VN_DEV, wide)))
    second = second.reshape(parts, wide)
    totals = second[:, :width]
    counts = second[:, width : width + 1]
    part_mean = totals / counts
    inv_vn, unit_vn = rms_parts(part_mean)
    virtual = unit_vn.astype(jnp.bfloat16)

    qkv_t = jnp.einsum(
        "dc,rd->cr", query_key_value_weight, normed, preferred_element_type=jnp.float32
    ).astype(jnp.bfloat16)
    qkv_heads = jnp.transpose(qkv_t.reshape(3, HEADS, head_dim, rows), (1, 0, 2, 3)).reshape(
        HEADS, 1, 3 * head_dim, rows
    )
    qkv_all = all_to_all(
        jnp.broadcast_to(qkv_heads, (HEADS, slices, 3 * head_dim, rows)).reshape(
            seq_size, 3 * head_dim, rows
        )
    )
    lists = lax.dynamic_slice_in_dim(lists_all, my_slice * tiles_here, tiles_here, 0)
    weight_heads = query_key_value_weight.reshape(width, 3, HEADS, head_dim)
    my_columns = lax.dynamic_index_in_dim(weight_heads, my_head, 2, keepdims=False)[:, 1:]
    virt = jnp.einsum(
        "dke,pd->kep", my_columns, virtual, preferred_element_type=jnp.float32
    ).astype(jnp.bfloat16)

    def spread(local):
        if slices == 1:
            return local
        empty = jnp.zeros((seq_size,) + local.shape[1:], local.dtype)
        return lax.dynamic_update_slice_in_dim(empty, local, my_slice * tiles_here, 0)

    def pick_slice(received):
        split = received.reshape((HEADS, slices) + received.shape[1:])
        return lax.dynamic_index_in_dim(split, slice_of_me, 1, keepdims=False)

    out_heads = attention_forward(lists, qkv_all, virt, head_dim)
    attn_out_t = pick_slice(all_to_all(spread(out_heads))).reshape(width, rows)

    mixed = jnp.einsum("dr,de->re", attn_out_t, w_out, preferred_element_type=jnp.float32)
    resid = (x_f + mixed).astype(jnp.bfloat16)
    res_f = resid.astype(jnp.float32)
    inv_ffn, unit_ffn = rms_parts(res_f)
    normed_ffn = (unit_ffn * gain_ffn).astype(jnp.bfloat16)
    gate_up = jnp.dot(normed_ffn, w_in, preferred_element_type=jnp.float32)
    gate_proj = gate_up[:, :hidden_units]
    up_proj = gate_up[:, hidden_units:]
    sigmoid_gate = jax.nn.sigmoid(gate_proj)
    activated = gate_proj * sigmoid_gate
    hidden = (activated * up_proj).astype(jnp.bfloat16)
    layer_out = (res_f + jnp.dot(hidden, w_down, preferred_element_type=jnp.float32)).astype(
        jnp.bfloat16
    )
    d_hidden = jnp.einsum("rd,fd->rf", grad_out, w_down, preferred_element_type=jnp.float32)
    d_gate = d_hidden * up_proj * sigmoid_gate * (1.0 + gate_proj * (1.0 - sigmoid_gate))
    d_up = d_hidden * activated
    d_both = jnp.concatenate([d_gate, d_up], axis=1).astype(jnp.bfloat16)
    d_normed_ffn = jnp.einsum("rf,df->rd", d_both, w_in, preferred_element_type=jnp.float32)
    scaled_ffn = d_normed_ffn * gain_ffn
    d_resid = (
        grad_out.astype(jnp.float32)
        + inv_ffn
        * (scaled_ffn - unit_ffn * jnp.mean(scaled_ffn * unit_ffn, axis=-1, keepdims=True))
    ).astype(jnp.bfloat16)
    d_attn_t = jnp.einsum("de,re->dr", w_out, d_resid, preferred_element_type=jnp.float32).astype(
        jnp.bfloat16
    )
    d_heads = jnp.broadcast_to(
        d_attn_t.reshape(HEADS, 1, head_dim, rows), (HEADS, slices, head_dim, rows)
    ).reshape(seq_size, head_dim, rows)
    grads = lax.dynamic_slice_in_dim(all_to_all(d_heads), my_slice * tiles_here, tiles_here, 0)

    share = width // seq_size
    grad_out_local = jnp.einsum("dr,re->de", attn_out_t, d_resid, preferred_element_type=jnp.float32)
    grad_in_local = jnp.einsum("rd,rf->df", normed_ffn, d_both, preferred_element_type=jnp.float32)
    grad_down_local = jnp.einsum("rf,rd->fd", hidden, grad_out, preferred_element_type=jnp.float32)
    down_blocks = grad_down_local.astype(jnp.bfloat16).reshape(seq_size, -1, share, width)
    early = jnp.concatenate(
        [
            grad_out_local.astype(jnp.bfloat16).reshape(seq_size, share, -1),
            grad_in_local.astype(jnp.bfloat16).reshape(seq_size, share, -1),
        ]
        + [down_blocks[:, i] for i in range(down_blocks.shape[1])],
        axis=2,
    )
    early_sum = reduce_scatter(early)
    grad_w_out = early_sum[:, :width]
    in_end = width + 2 * hidden_units
    grad_w_in = early_sum[:, width:in_end]
    grad_w_down = jnp.concatenate(
        [early_sum[:, c : c + width] for c in range(in_end, early_sum.shape[1], width)], axis=0
    )

    dq, dkv, dvirt = attention_backward(lists, qkv_all, virt, grads, head_dim)
    virt_rows = 2 * head_dim * parts // rows
    back_send = jnp.concatenate(
        [
            spread(dq),
            dkv,
            jnp.broadcast_to(
                dvirt.astype(jnp.bfloat16).reshape(virt_rows, rows), (seq_size, virt_rows, rows)
            ),
        ],
        axis=1,
    )
    back = all_to_all(back_send)
    dq_t = pick_slice(back[:, :head_dim])
    rest = back[:, head_dim:]
    if slices > 1:
        rest = jnp.sum(
            rest.reshape(HEADS, slices, -1, rows).astype(jnp.float32), axis=1
        ).astype(jnp.bfloat16)
    d_qkv_t = jnp.concatenate(
        [dq_t, rest[:, :head_dim], rest[:, head_dim : 2 * head_dim]], axis=0
    ).reshape(3 * width, rows)
    d_virt = (
        rest[:, 2 * head_dim :]
        .reshape(HEADS, 2, head_dim, parts)
        .transpose(1, 0, 2, 3)
        .reshape(2 * width, parts)
    )
    d_virtual = jnp.einsum(
        "sp,ds->pd", d_virt, query_key_value_weight[:, width:], preferred_element_type=jnp.float32
    )
    inner_vn = jnp.mean(d_virtual * unit_vn, axis=-1, keepdims=True)
    per_part = inv_vn * (d_virtual - unit_vn * inner_vn) / counts
    d_normed = jnp.einsum(
        "cr,dc->rd", d_qkv_t, query_key_value_weight, preferred_element_type=jnp.float32
    )
    d_normed = d_normed + jnp.dot(member.astype(jnp.float32), per_part, precision=HIGH_PRECISION)
    scaled_attn = d_normed * gain_attn
    d_features = (
        d_resid.astype(jnp.float32)
        + inv_attn
        * (scaled_attn - unit_attn * jnp.mean(scaled_attn * unit_attn, axis=-1, keepdims=True))
    ).astype(jnp.bfloat16)
    grad_qkv_local = jnp.einsum("rd,cr->dc", normed, d_qkv_t, preferred_element_type=jnp.float32)
    gain_local = jnp.concatenate(
        [jnp.sum(d_normed * unit_attn, axis=0), jnp.sum(d_normed_ffn * unit_ffn, axis=0)]
    )
    gain_share = 2 * width // seq_size
    gain_block = jnp.pad(
        gain_local.astype(jnp.bfloat16).reshape(seq_size, 1, gain_share),
        ((0, 0), (0, share - 1), (0, 128 - gain_share)),
    )
    late = jnp.concatenate(
        [grad_qkv_local.astype(jnp.bfloat16).reshape(seq_size, share, -1), gain_block], axis=2
    )
    late_sum = reduce_scatter(late)
    my_virtual = lax.dynamic_slice_in_dim(virtual, me * share, share, 1)
    virtual_grad = jnp.einsum("pd,sp->ds", my_virtual, d_virt, preferred_element_type=jnp.float32)
    grad_qkv = jnp.concatenate(
        [late_sum[:, :width], late_sum[:, width : 3 * width] + virtual_grad], axis=1
    )
    grad_gains = late_sum[0, 3 * width : 3 * width + gain_share]
    return (layer_out, d_features, grad_qkv, grad_w_out, grad_w_in, grad_w_down, grad_gains)


def solution(mesh):
    node = P(("groups", "seq"), None)
    flat = P(("groups", "seq"))
    return jax.shard_map(
        on_device,
        mesh=mesh,
        in_specs=(node, P(), P(), P(), P(), P(), P(), node, flat, flat, node),
        out_specs=(node, node, node, node, node, node, flat),
        check_vma=False,
    )
```

time: 584 us -> 202 us (0.35)
  waiting for transfers between devices: 290 us -> 86.6 us
  blocking collectives: 115 us -> 0 us
  matrix products: 55.9 us -> 21.9 us
  local copies, waits for them, and re-layouts: 51.9 us -> 22.4 us
  Pallas kernels: 0 us -> 18.8 us
  other arithmetic: 27.5 us -> 13.2 us
  starting transfers between devices: 22 us -> 36.3 us
  between operations: 16 us -> 2.03 us
    reduce_scatter x4 -> x0, waiting for transfers between devices: 237 us -> none  [the longest x1 75.6 us: on_device(): lax.psum_scatter(grad_in_local, 'seq', scatter_dimension=0, tiled=True)]
    ppermute x0 -> x10, waiting for transfers between devices: none -> 45.8 us  [the longest x6 25.3 us: reduce_scatter(): total = total + lax.ppermute(send, 'seq', perm).astype(jnp.float32)]
    unnamed x2 -> x0, blocking collectives: 44.3 us -> none
    dot_general x42 -> x11, matrix products: 45 us -> 12.7 us  [the longest x1 1.83 us: on_device(): jnp.einsum('rd,cr->dc', normed, d_qkv_t, preferred_element_type=jnp.float32)]
    psum x1 -> x0, blocking collectives: 31.4 us -> none  [on_device(): totals, counts = lax.psum((part_sums, part_count), 'seq')]
    psum x2 -> x0, waiting for transfers between devices: 30.1 us -> none  [the longest x1 28.3 us: on_device(): virtual_node_gradient = lax.psum(vn_part, 'seq')]
    all_gather x1 -> x0, blocking collectives: 24.6 us -> none  [on_device(): lax.all_gather(tile_lists, 'seq', axis=0, tiled=True)]
    pallas_call x0 -> x2, Pallas kernels: none -> 18.8 us  [the longest x1 11.8 us: attention_backward(): pl.pallas_call(functools.partial(backward_kernel, head_dim), out_shape=(j...]
  transfers between devices with their start and end apart: 11 -> 16, of which waited for: 9 -> 13; matrix products, arithmetic and copies ran while one was open for 8% -> 17% of each run, Pallas kernels for 0% -> 0%
where the time goes in v1:
time: 202 us; the launch traced here: 201 us
  waiting for transfers between devices  86.6 us (43%)
  starting transfers between devices  36.3 us (18%)
  local copies, waits for them, and re-layouts  22.4 us (11%)
  matrix products  21.9 us (11%)
  Pallas kernels  18.8 us (9%)
  other arithmetic  13.2 us (7%)
  between operations  2.03 us (1%)
    all_to_all x6, waiting for transfers between devices, all_to_all(): lax.all_to_all(blocks, 'seq', split_axis=0, concat_axis=0, tiled=True)  40.8 us
    all_to_all x6, starting transfers between devices, all_to_all(): lax.all_to_all(blocks, 'seq', split_axis=0, concat_axis=0, tiled=True)  25.7 us
    ppermute x6, waiting for transfers between devices, reduce_scatter(): total = total + lax.ppermute(send, 'seq', perm).astype(jnp.float32)  25.3 us
    ppermute x4, waiting for transfers between devices, halve(): got = lax.ppermute(send, 'seq', [(i, i ^ bit) for i in range(size)])  20.5 us
    pallas_call x1, Pallas kernels, attention_backward(): pl.pallas_call(functools.partial(backward_kernel, head_dim), out_shape=(j...  11.8 us
    unnamed x61, local copies, waits for them, and re-layouts  9.75 us
    ppermute x6, starting transfers between devices, reduce_scatter(): total = total + lax.ppermute(send, 'seq', perm).astype(jnp.float32)  8.78 us
    pallas_call x1, Pallas kernels, attention_forward(): pl.pallas_call(functools.partial(forward_kernel, head_dim), out_shape=jax...  6.98 us
  transfers between devices with their start and end apart: 16, of which 13 were waited for; matrix products, arithmetic and copies ran while one was open for 17% of the time, Pallas kernels for 0%

profile of v1, /device:TPU:0, one launch (start us, length us, event | category | flops | bytes accessed | tf_op | source)
XLA Modules:
  0.0 201.2 jit_solution(484278821508811236)
XLA Ops:
  1.4 1.0 fusion.26
  3.0 1.0 fusion.19
  4.0 0.9 fusion.34
  5.0 0.7 add_convert_fusion.1
  5.8 0.7 pad_maximum_fusion.7
  6.5 7.4 %all-to-all-start = ((f32[16,3,640]{2,1,0:T(4,128)}), f32[16,3,640]{2,1,0:T(4,128)S(1)}, u32[]{:S(2)}, u32[]{:S(2)}) async-start(f32[16,3,640]{2,1,0:T(4,128)} %pad_maximum_fusion.7), calls=%async_computation | async-start | bytes 327680 | tf_op jit(solution)/shard_map/all_to_all | solution.py:153
  13.9 2.6 %copy.76 = bf16[512,1536]{0,1:T(8,128)(2,1)} copy(bf16[512,1536]{1,0:T(8,128)(2,1)} %param.14) | data formatting | bytes 3145728 | tf_op args[3]
  16.5 1.8 fusion.1
  18.5 0.8 copy.75
  19.3 3.0 %all-to-all-done = f32[16,3,640]{2,1,0:T(4,128)S(1)} async-done(((f32[16,3,640]{2,1,0:T(4,128)}), f32[16,3,640]{2,1,0:T(4,128)S(1)}, u32[]{:S(2)}, u32[]{:S(2)}) %all-to-all-start) | async-done | bytes 122912 | tf_op jit(solution)/shard_map/all_to_all | solution.py:153
  23.1 3.5 %all-to-all-start.2 = ((f32[16,2,640]{2,1,0:T(2,128)}), f32[16,2,640]{2,1,0:T(2,128)S(1)}, u32[]{:S(2)}, u32[]{:S(2)}) async-start(f32[16,2,640]{2,1,0:T(2,128)} %broadcast_in_dim.7), calls=%async_computation.2 | async-start | bytes 163840 | tf_op jit(solution)/shard_map/all_to_all | solution.py:153
  26.7 7.0 %all-to-all-done.2 = f32[16,2,640]{2,1,0:T(2,128)S(1)} async-done(((f32[16,2,640]{2,1,0:T(2,128)}), f32[16,2,640]{2,1,0:T(2,128)S(1)}, u32[]{:S(2)}, u32[]{:S(2)}) %all-to-all-start.2) | async-done | bytes 81952 | tf_op jit(solution)/shard_map/all_to_all | solution.py:153
  33.7 3.6 %all-to-all-start.1 = ((bf16[16,96,128]{2,1,0:T(8,128)(2,1)}), bf16[16,96,128]{2,1,0:T(8,128)(2,1)S(1)}, u32[]{:S(2)}, u32[]{:S(2)}) async-start(bf16[16,96,128]{2,1,0:T(8,128)(2,1)} %bitcast.5), calls=%async_computation.1 | async-start | bytes 786432 | tf_op jit(solution)/shard_map/all_to_all | solution.py:153
  38.3 1.0 convolution_convert_fusion.6.virt_ref
  39.3 10.2 %all-to-all-done.1.qkv_ref = bf16[16,96,128]{2,1,0:T(8,128)(2,1)S(1)} async-done(((bf16[16,96,128]{2,1,0:T(8,128)(2,1)}), bf16[16,96,128]{2,1,0:T(8,128)(2,1)S(1)}, u32[]{:S(2)}, u32[]{:S(2)}) %all-to-all-start.1) | async-done | bytes 393248 | tf_op jit(solution)/shard_map/all_to_all | solution.py:153
  49.5 7.0 %shard_map.162 = bf16[16,32,128]{2,1,0:T(8,128)(2,1)} custom-call(s32[16,5]{1,0:T(8,128)S(1)} %copy.77.lists_ref, bf16[16,96,128]{2,1,0:T(8,128)(2,1)S(1)} %all-to-all-done.1.qkv_ref, bf16[2,32,32]{2,1,0:T(8,128)(2,1)S(1)} %convolution_convert_fusion.6.virt_ref), custom_call_target="tpu_custom_call" | custom-call | flops 142606336 | bytes 393216 | tf_op jit(solution)/shard_map/pallas_call | solution.py:117
  56.4 3.5 %all-to-all-start.3 = ((bf16[16,32,128]{2,1,0:T(8,128)(2,1)}), bf16[16,32,128]{2,1,0:T(8,128)(2,1)S(1)}, u32[]{:S(2)}, u32[]{:S(2)}) async-start(bf16[16,32,128]{2,1,0:T(8,128)(2,1)} %shard_map.162), calls=%async_computation.3 | async-start | bytes 262144 | tf_op jit(solution)/shard_map/all_to_all | solution.py:153
  60.0 7.9 %all-to-all-done.3 = bf16[16,32,128]{2,1,0:T(8,128)(2,1)S(1)} async-done(((bf16[16,32,128]{2,1,0:T(8,128)(2,1)}), bf16[16,32,128]{2,1,0:T(8,128)(2,1)S(1)}, u32[]{:S(2)}, u32[]{:S(2)}) %all-to-all-start.3) | async-done | bytes 131104 | tf_op jit(solution)/shard_map/all_to_all | solution.py:153
  68.5 1.3 multiply_reduce_fusion.2
  70.4 0.7 copy-done.14
  71.1 1.3 multiply_convert_fusion.1
  72.3 1.4 multiply_reduce_fusion
  73.7 2.2 %convolution_convert_fusion = bf16[512,2048]{1,0:T(8,128)(2,1)} fusion(bf16[128,1024]{1,0:T(8,128)(2,1)S(1)} %get-tuple-element.18, bf16[128,1024]{1,0:T(8,128)(2,1)S(1)} %get-tuple-element.17, f32[128,512]{1,0:T(8,128)S(1)} %get-tuple-element.35, f32[512]{0:T(512)S(1)} %copy-done.20, f32[128]{0:T(128)S(1)} %add_rsqrt_fusion), kind=kOutput, calls=%fused_computation.3 | convolution fusion | flops 270729216 | bytes 2886144 | tf_op jit(solution)/shard_map/rd,rf->df/dot_general | solution.py:305
  76.7 1.0 fusion.7
  77.7 1.7 copy.78
  79.3 3.5 %all-to-all-start.4 = ((bf16[16,32,128]{2,1,0:T(8,128)(2,1)}), bf16[16,32,128]{2,1,0:T(8,128)(2,1)S(1)}, u32[]{:S(2)}, u32[]{:S(2)}) async-start(bf16[16,32,128]{2,1,0:T(8,128)(2,1)} %bitcast.11), calls=%async_computation.4 | async-start | bytes 262144 | tf_op jit(solution)/shard_map/all_to_all | solution.py:153
  82.9 1.5 convolution_convert_fusion.3
  84.4 1.1 fusion.60
  85.5 1.1 convolution_convert_fusion.4
  86.6 4.1 %all-to-all-done.4.grad_ref = bf16[16,32,128]{2,1,0:T(8,128)(2,1)S(1)} async-done(((bf16[16,32,128]{2,1,0:T(8,128)(2,1)}), bf16[16,32,128]{2,1,0:T(8,128)(2,1)S(1)}, u32[]{:S(2)}, u32[]{:S(2)}) %all-to-all-start.4) | async-done | bytes 131104 | tf_op jit(solution)/shard_map/all_to_all | solution.py:153
  90.7 11.8 %shard_map.163 = (bf16[16,32,128]{2,1,0:T(8,128)(2,1)S(1)}, bf16[16,64,128]{2,1,0:T(8,128)(2,1)S(1)}, f32[64,32]{1,0:T(8,128)S(1)}) custom-call(s32[16,5]{1,0:T(8,128)S(1)} %copy.77.lists_ref, bf16[16,96,128]{2,1,0:T(8,128)(2,1)S(1)} %all-to-all-done.1.qkv_ref, bf16[2,32,32]{2,1,0:T(8,128)(2,1)S(1)} %convolution_convert_fusion.6.virt_ref, ...), custom_call_target="tpu_custom_call" | custom-call | flops 356515840 | bytes 1179648 | tf_op jit(solution)/shard_map/pallas_call | solution.py:135
  102.7 0.8 pad_maximum_fusion.2
  103.5 4.2 %all-to-all-start.5 = ((bf16[16,112,128]{2,1,0:T(8,128)(2,1)}), bf16[16,112,128]{2,1,0:T(8,128)(2,1)}, u32[]{:S(2)}, u32[]{:S(2)}) async-start(bf16[16,112,128]{2,1,0:T(8,128)(2,1)} %pad_maximum_fusion.2), calls=%async_computation.5 | async-start | bytes 917504 | tf_op jit(solution)/shard_map/all_to_all | solution.py:153
  107.8 2.1 %pad_maximum_fusion = bf16[8,2,32,3584]{3,2,1,0:T(8,128)(2,1)S(1)} fusion(bf16[8,2,32,512]{3,2,1,0:T(8,128)(2,1)} %bitcast.118, bf16[8,2,32,512]{3,2,1,0:T(8,128)(2,1)} %bitcast.117, bf16[8,2,32,2048]{3,2,1,0:T(8,128)(2,1)} %bitcast.107, bf16[8,2,32,512]{3,2,1,0:T(8,128)(2,1)S(1)} %bitcast.116), kind=kLoop, calls=%fused_computation | loop fusion | flops 14680064 | bytes 7340032 | tf_op jit(solution)/shard_map/concatenate | solution.py:308
  109.8 1.6 dynamic-slice_bitcast_fusion
  111.4 0.8 copy-done.1
  112.4 8.6 %all-to-all-done.5 = bf16[16,112,128]{2,1,0:T(8,128)(2,1)} async-done(((bf16[16,112,128]{2,1,0:T(8,128)(2,1)}), bf16[16,112,128]{2,1,0:T(8,128)(2,1)}, u32[]{:S(2)}, u32[]{:S(2)}) %all-to-all-start.5) | async-done | bytes 458784 | tf_op jit(solution)/shard_map/all_to_all | solution.py:153
  121.0 1.2 fusion.62
  122.6 1.4 fusion.63
  124.0 1.8 convolution_convert_fusion.1
  125.9 0.9 slice.97
  127.6 1.8 multiply_reduce_fusion.3
  130.1 1.5 copy_dynamic-update-slice_fusion
  131.7 1.3 copy-done.4
  133.0 1.0 dynamic-slice_bitcast_fusion.2
  134.1 2.3 %fusion.6 = bf16[128,512]{1,0:T(8,128)(2,1)} fusion(f32[128,512]{1,0:T(8,128)S(1)} %get-tuple-element.35, bf16[128,1024]{1,0:T(8,128)(2,1)S(1)} %copy-done.15, bf16[1024,512]{1,0:T(8,128)(2,1)} %param.17), kind=kOutput, calls=%fused_computation.21 | convolution fusion | flops 134348800 | bytes 1703936 | tf_op jit(solution)/shard_map/dot_general | solution.py:281
  136.4 0.8 fusion.24
  137.2 1.7 fusion.3
  139.0 1.1 collective-permute-start.1
  140.0 2.0 fusion
  142.0 9.2 %collective-permute-done.1 = bf16[4,32,1664]{2,1,0:T(8,128)(2,1)S(1)} collective-permute-done((bf16[4,32,1664]{2,1,0:T(8,128)(2,1)S(1)}, bf16[4,32,1664]{2,1,0:T(8,128)(2,1)S(1)}, u32[]{:S(2)}, u32[]{:S(2)}) %collective-permute-start.1) | collective-permute-done | bytes 426016 | tf_op jit(solution)/shard_map/ppermute | solution.py:165
  151.3 1.1 collective-permute-start.2
  152.4 2.8 %collective-permute-start.4 = (bf16[32,1664]{1,0:T(8,128)(2,1)S(1)}, bf16[32,1664]{1,0:T(8,128)(2,1)S(1)}, u32[]{:S(2)}, u32[]{:S(2)}) collective-permute-start(bf16[32,1664]{1,0:T(8,128)(2,1)S(1)} %get-tuple-element.32), channel_id=1, source_target_pairs={{0,12},{1,13},{2,14},{3,15},{4,0},{5,1},{6,2},{7,3},{8,4},{9,5},{1... | collective-permute-start | bytes 319496 | tf_op jit(solution)/shard_map/ppermute | solution.py:181
  155.9 3.2 %collective-permute-done.2 = bf16[32,1664]{1,0:T(8,128)(2,1)S(1)} collective-permute-done((bf16[32,1664]{1,0:T(8,128)(2,1)S(1)}, bf16[32,1664]{1,0:T(8,128)(2,1)S(1)}, u32[]{:S(2)}, u32[]{:S(2)}) %collective-permute-start.2) | collective-permute-done | bytes 106528 | tf_op jit(solution)/shard_map/ppermute | solution.py:181
  159.1 5.4 %collective-permute-done.3 = bf16[32,1664]{1,0:T(8,128)(2,1)S(1)} collective-permute-done((bf16[32,1664]{1,0:T(8,128)(2,1)S(1)}, bf16[32,1664]{1,0:T(8,128)(2,1)S(1)}, u32[]{:S(2)}, u32[]{:S(2)}) %collective-permute-start.3) | collective-permute-done | bytes 106528 | tf_op jit(solution)/shard_map/ppermute | solution.py:181
  165.4 11.3 %collective-permute-done.6 = bf16[4,32,3584]{2,1,0:T(8,128)(2,1)S(1)} collective-permute-done((bf16[4,32,3584]{2,1,0:T(8,128)(2,1)S(1)}, bf16[4,32,3584]{2,1,0:T(8,128)(2,1)S(1)}, u32[]{:S(2)}, u32[]{:S(2)}) %collective-permute-start.6) | collective-permute-done | bytes 917536 | tf_op jit(solution)/shard_map/ppermute | solution.py:165
  177.6 3.3 %collective-permute-start.9 = (bf16[32,3584]{1,0:T(8,128)(2,1)S(1)}, bf16[32,3584]{1,0:T(8,128)(2,1)S(1)}, u32[]{:S(2)}, u32[]{:S(2)}) collective-permute-start(bf16[32,3584]{1,0:T(8,128)(2,1)S(1)} %get-tuple-element.23), channel_id=1, source_target_pairs={{0,12},{1,13},{2,14},{3,15},{4,0},{5,1},{6,2},{7,3},{8,4},{9,5},{1... | collective-permute-start | bytes 688136 | tf_op jit(solution)/shard_map/ppermute | solution.py:181
  180.9 0.8 collective-permute-start.8
  181.7 0.7 pad_maximum_fusion.6
  182.4 5.1 %collective-permute-done.7 = bf16[32,3584]{1,0:T(8,128)(2,1)S(1)} collective-permute-done((bf16[32,3584]{1,0:T(8,128)(2,1)S(1)}, bf16[32,3584]{1,0:T(8,128)(2,1)S(1)}, u32[]{:S(2)}, u32[]{:S(2)}) %collective-permute-start.7) | collective-permute-done | bytes 229408 | tf_op jit(solution)/shard_map/ppermute | solution.py:181
  187.5 1.0 collective-permute-done.9
  188.5 10.5 %collective-permute-done.8 = bf16[32,3584]{1,0:T(8,128)(2,1)S(1)} collective-permute-done((bf16[32,3584]{1,0:T(8,128)(2,1)S(1)}, bf16[32,3584]{1,0:T(8,128)(2,1)S(1)}, u32[]{:S(2)}, u32[]{:S(2)}) %collective-permute-start.8) | collective-permute-done | bytes 229408 | tf_op jit(solution)/shard_map/ppermute | solution.py:181
  199.8 0.7 slice.103
  200.6 0.7 pad_maximum_fusion.8
  (109 shorter events, 10.6 us)
Async XLA Ops:
  0.6 69.2 %copy-start = (bf16[512,2048]{1,0:T(8,128)(2,1)S(1)}, bf16[512,2048]{1,0:T(8,128)(2,1)}, u32[]{:S(2)}) copy-start(bf16[512,2048]{1,0:T(8,128)(2,1)} %param.16) | copy-start | bytes 6291460
  2.5 0.5 copy-start.22
  6.5 15.8 %all-to-all-start = ((f32[16,3,640]{2,1,0:T(4,128)}), f32[16,3,640]{2,1,0:T(4,128)S(1)}, u32[]{:S(2)}, u32[]{:S(2)}) async-start(f32[16,3,640]{2,1,0:T(4,128)} %pad_maximum_fusion.7), calls=%async_computation | async-start | bytes 327680 | tf_op jit(solution)/shard_map/all_to_all | solution.py:153
  23.1 10.6 %all-to-all-start.2 = ((f32[16,2,640]{2,1,0:T(2,128)}), f32[16,2,640]{2,1,0:T(2,128)S(1)}, u32[]{:S(2)}, u32[]{:S(2)}) async-start(f32[16,2,640]{2,1,0:T(2,128)} %broadcast_in_dim.7), calls=%async_computation.2 | async-start | bytes 163840 | tf_op jit(solution)/shard_map/all_to_all | solution.py:153
  33.7 15.7 %all-to-all-start.1 = ((bf16[16,96,128]{2,1,0:T(8,128)(2,1)}), bf16[16,96,128]{2,1,0:T(8,128)(2,1)S(1)}, u32[]{:S(2)}, u32[]{:S(2)}) async-start(bf16[16,96,128]{2,1,0:T(8,128)(2,1)} %bitcast.5), calls=%async_computation.1 | async-start | bytes 786432 | tf_op jit(solution)/shard_map/all_to_all | solution.py:153
  37.7 0.6 copy-start.26
  39.2 29.3 %copy-start.7 = (bf16[512,512]{1,0:T(8,128)(2,1)S(1)}, bf16[512,512]{1,0:T(8,128)(2,1)}, u32[]{:S(2)}) copy-start(bf16[512,512]{1,0:T(8,128)(2,1)} %param.15) | copy-start | bytes 1572868
  39.3 30.6 %copy-start.20 = (f32[512]{0:T(512)S(1)}, f32[512]{0:T(512)}, u32[]{:S(2)}) copy-start(f32[512]{0:T(512)} %param.13) | copy-start | bytes 6148
  56.4 11.4 %all-to-all-start.3 = ((bf16[16,32,128]{2,1,0:T(8,128)(2,1)}), bf16[16,32,128]{2,1,0:T(8,128)(2,1)S(1)}, u32[]{:S(2)}, u32[]{:S(2)}) async-start(bf16[16,32,128]{2,1,0:T(8,128)(2,1)} %shard_map.162), calls=%async_computation.3 | async-start | bytes 262144 | tf_op jit(solution)/shard_map/all_to_all | solution.py:153
  67.9 0.7 copy-start.12
  69.8 1.2 copy-start.14
  69.8 1.2 copy-start.16
  76.0 0.7 copy-start.9
  79.3 11.4 %all-to-all-start.4 = ((bf16[16,32,128]{2,1,0:T(8,128)(2,1)}), bf16[16,32,128]{2,1,0:T(8,128)(2,1)S(1)}, u32[]{:S(2)}, u32[]{:S(2)}) async-start(bf16[16,32,128]{2,1,0:T(8,128)(2,1)} %bitcast.11), calls=%async_computation.4 | async-start | bytes 262144 | tf_op jit(solution)/shard_map/all_to_all | solution.py:153
  82.8 2.6 %copy-start.24 = (bf16[512]{0:T(512)(128)(2,1)S(1)}, bf16[512]{0:T(512)(128)(2,1)}, u32[]{:S(2)}) copy-start(bf16[512]{0:T(512)(128)(2,1)} %get-tuple-element.13) | copy-start | bytes 3076
  82.9 2.7 %copy-start.10 = (bf16[128,512]{1,0:T(8,128)(2,1)S(1)}, bf16[128,512]{1,0:T(8,128)(2,1)}, u32[]{:S(2)}) copy-start(bf16[128,512]{1,0:T(8,128)(2,1)} %copy-done.9) | copy-start | bytes 393220
  82.9 2.7 %copy-start.13 = (bf16[16,32,128]{2,1,0:T(8,128)(2,1)S(1)}, bf16[16,32,128]{2,1,0:T(8,128)(2,1)}, u32[]{:S(2)}) copy-start(bf16[16,32,128]{2,1,0:T(8,128)(2,1)} %copy-done.12) | copy-start | bytes 393220
  102.6 5.2 %copy-start.6 = (bf16[512,512]{1,0:T(8,128)(2,1)S(1)}, bf16[512,512]{1,0:T(8,128)(2,1)}, u32[]{:S(2)}) copy-start(bf16[512,512]{1,0:T(8,128)(2,1)} %convolution_convert_fusion.4) | copy-start | bytes 1572868
  103.5 17.5 %all-to-all-start.5 = ((bf16[16,112,128]{2,1,0:T(8,128)(2,1)}), bf16[16,112,128]{2,1,0:T(8,128)(2,1)}, u32[]{:S(2)}, u32[]{:S(2)}) async-start(bf16[16,112,128]{2,1,0:T(8,128)(2,1)} %pad_maximum_fusion.2), calls=%async_computation.5 | async-start | bytes 917504 | tf_op jit(solution)/shard_map/all_to_all | solution.py:153
  109.8 2.3 %copy-start.1 = (bf16[8,2,32,3584]{3,2,1,0:T(8,128)(2,1)}, bf16[8,2,32,3584]{3,2,1,0:T(8,128)(2,1)S(1)}, u32[]{:S(2)}) copy-start(bf16[8,2,32,3584]{3,2,1,0:T(8,128)(2,1)S(1)} %pad_maximum_fusion) | copy-start | bytes 11010052
  112.2 27.9 %collective-permute-start.5 = (bf16[8,32,3584]{2,1,0:T(8,128)(2,1)}, bf16[8,32,3584]{2,1,0:T(8,128)(2,1)}, u32[]{:S(2)}, u32[]{:S(2)}) collective-permute-start(bf16[8,32,3584]{2,1,0:T(8,128)(2,1)} %dynamic-slice_bitcast_fusion), channel_id=1, source_target_pairs={{0,1},{1,0},{2,3},{3,2},{4,5},{5,4},{6,7},{7,6},{8,9},{9,8},{10,11... | collective-permute-start | bytes 5505032 | tf_op jit(solution)/shard_map/ppermute | solution.py:165
  121.0 1.6 copy-start.3
  124.0 3.6 %copy-start.27 = (f32[32]{0:T(128)S(1)}, f32[32]{0:T(128)}, u32[]{:S(2)}) copy-start(f32[32]{0:T(128)} %copy-done.26) | copy-start | bytes 388
  125.8 3.6 %copy-start.8 = (bf16[128,512]{1,0:T(8,128)(2,1)S(1)}, bf16[128,512]{1,0:T(8,128)(2,1)}, u32[]{:S(2)}) copy-start(bf16[128,512]{1,0:T(8,128)(2,1)} %param.11) | copy-start | bytes 393220
  125.8 3.6 %copy-start.17 = (f32[128,512]{1,0:T(8,128)S(1)}, f32[128,512]{1,0:T(8,128)}, u32[]{:S(2)}) copy-start(f32[128,512]{1,0:T(8,128)} %fusion.63) | copy-start | bytes 786436
  125.8 3.7 %copy-start.21 = (f32[512]{0:T(512)S(1)}, f32[512]{0:T(512)}, u32[]{:S(2)}) copy-start(f32[512]{0:T(512)} %param.12) | copy-start | bytes 6148
  125.8 3.7 %copy-start.23 = (f32[128]{0:T(128)S(1)}, f32[128]{0:T(128)}, u32[]{:S(2)}) copy-start(f32[128]{0:T(128)} %copy-done.22) | copy-start | bytes 1540
  125.8 3.7 %copy-start.25 = (s32[128]{0:T(128)S(1)}, s32[128]{0:T(128)}, u32[]{:S(2)}) copy-start(s32[128]{0:T(128)} %param.20) | copy-start | bytes 1540
  125.8 3.7 %copy-start.28 = (f32[32]{0:T(128)S(1)}, f32[32]{0:T(128)}, u32[]{:S(2)}) copy-start(f32[32]{0:T(128)} %copy-done.26) | copy-start | bytes 388
  127.6 1.8 copy-start.18
  131.6 2.5 %copy-start.15 = (bf16[128,1024]{1,0:T(8,128)(2,1)S(1)}, bf16[128,1024]{1,0:T(8,128)(2,1)}, u32[]{:S(2)}) copy-start(bf16[128,1024]{1,0:T(8,128)(2,1)} %get-tuple-element.21) | copy-start | bytes 786436
  131.7 1.3 copy-start.4
  133.0 3.4 %copy-start.11 = (bf16[128,512]{1,0:T(8,128)(2,1)S(1)}, bf16[128,512]{1,0:T(8,128)(2,1)}, u32[]{:S(2)}) copy-start(bf16[128,512]{1,0:T(8,128)(2,1)} %copy-done.9) | copy-start | bytes 393220
  134.0 3.3 %collective-permute-start = (bf16[8,32,1664]{2,1,0:T(8,128)(2,1)}, bf16[8,32,1664]{2,1,0:T(8,128)(2,1)}, u32[]{:S(2)}, u32[]{:S(2)}) collective-permute-start(bf16[8,32,1664]{2,1,0:T(8,128)(2,1)} %dynamic-slice_bitcast_fusion.2), channel_id=1, source_target_pairs={{0,1},{1,0},{2,3},{3,2},{4,5},{5,4},{6,7},{7,6},{8,9},{9,8},{10,11... | collective-permute-start | bytes 2555912 | tf_op jit(solution)/shard_map/ppermute | solution.py:165
  134.1 3.1 %copy-start.5 = (bf16[8,2,32,1664]{3,2,0,1:T(8,128)(2,1)S(1)}, bf16[8,2,32,1664]{3,2,0,1:T(8,128)(2,1)}, u32[]{:S(2)}) copy-start(bf16[8,2,32,1664]{3,2,0,1:T(8,128)(2,1)} %copy-done.4) | copy-start | bytes 5111812
  136.4 3.6 %copy-start.2 = (bf16[8,2,32,3584]{3,2,1,0:T(8,128)(2,1)S(1)}, bf16[8,2,32,3584]{3,2,1,0:T(8,128)(2,1)}, u32[]{:S(2)}) copy-start(bf16[8,2,32,3584]{3,2,1,0:T(8,128)(2,1)} %copy-done.1) | copy-start | bytes 11010052
  139.0 12.2 %collective-permute-start.1 = (bf16[4,32,1664]{2,1,0:T(8,128)(2,1)S(1)}, bf16[4,32,1664]{2,1,0:T(8,128)(2,1)S(1)}, u32[]{:S(2)}, u32[]{:S(2)}) collective-permute-start(bf16[4,32,1664]{2,1,0:T(8,128)(2,1)S(1)} %dynamic-slice_bitcast_fusion.3), channel_id=1, source_target_pairs={{0,2},{1,3},{2,0},{3,1},{4,6},{5,7},{6,4},{7,5},{8,10},{9,11},{10,... | collective-permute-start | bytes 1277960 | tf_op jit(solution)/shard_map/ppermute | solution.py:165
  151.3 13.9 %copy-start.19 = (bf16[1024,32]{0,1:T(8,128)(2,1)S(1)}, bf16[1024,32]{0,1:T(8,128)(2,1)}, u32[]{:S(2)}) copy-start(bf16[1024,32]{0,1:T(8,128)(2,1)} %copy-done.18) | copy-start | bytes 196612
  151.3 7.8 %collective-permute-start.2 = (bf16[32,1664]{1,0:T(8,128)(2,1)S(1)}, bf16[32,1664]{1,0:T(8,128)(2,1)S(1)}, u32[]{:S(2)}, u32[]{:S(2)}) collective-permute-start(bf16[32,1664]{1,0:T(8,128)(2,1)S(1)} %get-tuple-element.31), channel_id=1, source_target_pairs={{0,4},{1,5},{2,6},{3,7},{4,8},{5,9},{6,10},{7,11},{8,12},{9,13},{1... | collective-permute-start | bytes 319496 | tf_op jit(solution)/shard_map/ppermute | solution.py:181
  152.4 6.7 %collective-permute-start.4 = (bf16[32,1664]{1,0:T(8,128)(2,1)S(1)}, bf16[32,1664]{1,0:T(8,128)(2,1)S(1)}, u32[]{:S(2)}, u32[]{:S(2)}) collective-permute-start(bf16[32,1664]{1,0:T(8,128)(2,1)S(1)} %get-tuple-element.32), channel_id=1, source_target_pairs={{0,12},{1,13},{2,14},{3,15},{4,0},{5,1},{6,2},{7,3},{8,4},{9,5},{1... | collective-permute-start | bytes 319496 | tf_op jit(solution)/shard_map/ppermute | solution.py:181
  155.2 9.3 %collective-permute-start.3 = (bf16[32,1664]{1,0:T(8,128)(2,1)S(1)}, bf16[32,1664]{1,0:T(8,128)(2,1)S(1)}, u32[]{:S(2)}, u32[]{:S(2)}) collective-permute-start(bf16[32,1664]{1,0:T(8,128)(2,1)S(1)} %get-tuple-element.33), channel_id=1, source_target_pairs={{0,8},{1,9},{2,10},{3,11},{4,12},{5,13},{6,14},{7,15},{8,0},{9,1},... | collective-permute-start | bytes 319496 | tf_op jit(solution)/shard_map/ppermute | solution.py:181
  155.5 21.2 %collective-permute-start.6 = (bf16[4,32,3584]{2,1,0:T(8,128)(2,1)S(1)}, bf16[4,32,3584]{2,1,0:T(8,128)(2,1)S(1)}, u32[]{:S(2)}, u32[]{:S(2)}) collective-permute-start(bf16[4,32,3584]{2,1,0:T(8,128)(2,1)S(1)} %dynamic-slice_bitcast_fusion.1), channel_id=1, source_target_pairs={{0,2},{1,3},{2,0},{3,1},{4,6},{5,7},{6,4},{7,5},{8,10},{9,11},{10,... | collective-permute-start | bytes 2752520 | tf_op jit(solution)/shard_map/ppermute | solution.py:165
  177.0 10.5 %collective-permute-start.7 = (bf16[32,3584]{1,0:T(8,128)(2,1)S(1)}, bf16[32,3584]{1,0:T(8,128)(2,1)S(1)}, u32[]{:S(2)}, u32[]{:S(2)}) collective-permute-start(bf16[32,3584]{1,0:T(8,128)(2,1)S(1)} %get-tuple-element.22), channel_id=1, source_target_pairs={{0,4},{1,5},{2,6},{3,7},{4,8},{5,9},{6,10},{7,11},{8,12},{9,13},{1... | collective-permute-start | bytes 688136 | tf_op jit(solution)/shard_map/ppermute | solution.py:181
  177.6 10.9 %collective-permute-start.9 = (bf16[32,3584]{1,0:T(8,128)(2,1)S(1)}, bf16[32,3584]{1,0:T(8,128)(2,1)S(1)}, u32[]{:S(2)}, u32[]{:S(2)}) collective-permute-start(bf16[32,3584]{1,0:T(8,128)(2,1)S(1)} %get-tuple-element.23), channel_id=1, source_target_pairs={{0,12},{1,13},{2,14},{3,15},{4,0},{5,1},{6,2},{7,3},{8,4},{9,5},{1... | collective-permute-start | bytes 688136 | tf_op jit(solution)/shard_map/ppermute | solution.py:181
  180.9 18.2 %collective-permute-start.8 = (bf16[32,3584]{1,0:T(8,128)(2,1)S(1)}, bf16[32,3584]{1,0:T(8,128)(2,1)S(1)}, u32[]{:S(2)}, u32[]{:S(2)}) collective-permute-start(bf16[32,3584]{1,0:T(8,128)(2,1)S(1)} %get-tuple-element.24), channel_id=1, source_target_pairs={{0,8},{1,9},{2,10},{3,11},{4,12},{5,13},{6,14},{7,15},{8,0},{9,1},... | collective-permute-start | bytes 688136 | tf_op jit(solution)/shard_map/ppermute | solution.py:181

commit v2 on v1

--- a/solution.py
+++ b/solution.py
@@ -153,19 +153,18 @@
     return lax.all_to_all(blocks, "seq", split_axis=0, concat_axis=0, tiled=True)
 
 
-def reduce_scatter(blocks):
-    size, rows, columns = blocks.shape
-    me = lax.axis_index("seq")
-
-    def halve(held, bit):
-        mine = (me // bit) % 2
-        split = held.reshape(held.shape[0] // 2, 2, rows, columns)
-        keep = lax.dynamic_index_in_dim(split, mine, 1, keepdims=False)
-        send = lax.dynamic_index_in_dim(split, 1 - mine, 1, keepdims=False)
-        got = lax.ppermute(send, "seq", [(i, i ^ bit) for i in range(size)])
-        return (keep.astype(jnp.float32) + got.astype(jnp.float32)).astype(jnp.bfloat16)
-
-    held = halve(halve(blocks, 1), 2)
+def halve(held, bit):
+    size = lax.axis_size("seq")
+    mine = (lax.axis_index("seq") // bit) % 2
+    split = held.reshape((held.shape[0] // 2, 2) + held.shape[1:])
+    keep = lax.dynamic_index_in_dim(split, mine, 1, keepdims=False)
+    send = lax.dynamic_index_in_dim(split, 1 - mine, 1, keepdims=False)
+    got = lax.ppermute(send, "seq", [(i, i ^ bit) for i in range(size)])
+    return (keep.astype(jnp.float32) + got.astype(jnp.float32)).astype(jnp.bfloat16)
+
+
+def finish(held):
+    size = lax.axis_size("seq")
     count = size // 4
     if count > 4:
         groups = [[j + 4 * m for m in range(count)] for j in range(4)]
@@ -173,7 +172,7 @@
             held, "seq", split_axis=0, concat_axis=0, axis_index_groups=groups, tiled=True
         )
         return jnp.sum(got.astype(jnp.float32), axis=0)
-    mine = me // 4
+    mine = lax.axis_index("seq") // 4
     total = lax.dynamic_index_in_dim(held, mine, 0, keepdims=False).astype(jnp.float32)
     for k in range(1, count):
         send = lax.dynamic_index_in_dim(held, (mine + k) % count, 0, keepdims=False)
@@ -313,15 +312,13 @@
         + [down_blocks[:, i] for i in range(down_blocks.shape[1])],
         axis=2,
     )
-    early_sum = reduce_scatter(early)
-    grad_w_out = early_sum[:, :width]
-    in_end = width + 2 * hidden_units
-    grad_w_in = early_sum[:, width:in_end]
-    grad_w_down = jnp.concatenate(
-        [early_sum[:, c : c + width] for c in range(in_end, early_sum.shape[1], width)], axis=0
-    )
+    early = halve(early, 1)
+    grads, early = lax.optimization_barrier((grads, early))
+    early = halve(early, 2)
 
     dq, dkv, dvirt = attention_backward(lists, qkv_all, virt, grads, head_dim)
+    dq, early = lax.optimization_barrier((dq, early))
+    early_sum = finish(early)
     virt_rows = 2 * head_dim * parts // rows
     back_send = jnp.concatenate(
         [
@@ -334,6 +331,7 @@
         axis=1,
     )
     back = all_to_all(back_send)
+    back, early_sum = lax.optimization_barrier((back, early_sum))
     dq_t = pick_slice(back[:, :head_dim])
     rest = back[:, head_dim:]
     if slices > 1:
@@ -376,7 +374,13 @@
     late = jnp.concatenate(
         [grad_qkv_local.astype(jnp.bfloat16).reshape(seq_size, share, -1), gain_block], axis=2
     )
-    late_sum = reduce_scatter(late)
+    late_sum = finish(halve(halve(late, 1), 2))
+    grad_w_out = early_sum[:, :width]
+    in_end = width + 2 * hidden_units
+    grad_w_in = early_sum[:, width:in_end]
+    grad_w_down = jnp.concatenate(
+        [early_sum[:, c : c + width] for c in range(in_end, early_sum.shape[1], width)], axis=0
+    )
     my_virtual = lax.dynamic_slice_in_dim(virtual, me * share, share, 1)
     virtual_grad = jnp.einsum("pd,sp->ds", my_virtual, d_virt, preferred_element_type=jnp.float32)
     grad_qkv = jnp.concatenate(

time: 202 us -> 198 us (0.980)
  waiting for transfers between devices: 86.6 us -> 78.4 us
  local copies, waits for them, and re-layouts: 22.4 us -> 25.6 us
  other arithmetic: 13.2 us -> 16.2 us
  matrix products: 21.9 us -> 19.3 us
    all_to_all x6, waiting for transfers between devices: 40.8 us -> 32 us  [all_to_all(): lax.all_to_all(blocks, 'seq', split_axis=0, concat_axis=0, tiled=True)]
    squeeze x4, local copies, waits for them, and re-layouts: 2.64 us -> 5.9 us  [halve(): send = lax.dynamic_index_in_dim(split, 1 - mine, 1, keepdims=False)]
    convert_element_type x4, other arithmetic: 4.01 us -> 6.72 us  [halve(): (keep.astype(jnp.float32) + got.astype(jnp.float32)).astype(jnp.bfloat16)]
    unnamed x61 -> x57, local copies, waits for them, and re-layouts: 9.75 us -> 10.6 us
  transfers between devices with their start and end apart: 16 -> 16, of which waited for: 13 -> 10; matrix products, arithmetic and copies ran while one was open for 17% -> 11% of each run, Pallas kernels for 0% -> 6%
where the time goes in v2:
time: 198 us; the launch traced here: 197 us
  waiting for transfers between devices  78.4 us (40%)
  starting transfers between devices  36.7 us (19%)
  local copies, waits for them, and re-layouts  25.6 us (13%)
  matrix products  19.3 us (10%)
  Pallas kernels  18.8 us (9%)
  other arithmetic  16.2 us (8%)
  between operations  2 us (1%)
    all_to_all x6, waiting for transfers between devices, all_to_all(): lax.all_to_all(blocks, 'seq', split_axis=0, concat_axis=0, tiled=True)  32 us
    ppermute x6, waiting for transfers between devices, finish(): total = total + lax.ppermute(send, 'seq', perm).astype(jnp.float32)  27.1 us
    all_to_all x6, starting transfers between devices, all_to_all(): lax.all_to_all(blocks, 'seq', split_axis=0, concat_axis=0, tiled=True)  25.9 us
    ppermute x4, waiting for transfers between devices, halve(): got = lax.ppermute(send, 'seq', [(i, i ^ bit) for i in range(size)])  19.3 us
    pallas_call x1, Pallas kernels, attention_backward(): pl.pallas_call(functools.partial(backward_kernel, head_dim), out_shape=(j...  11.8 us
    unnamed x57, local copies, waits for them, and re-layouts  10.6 us
    ppermute x6, starting transfers between devices, finish(): total = total + lax.ppermute(send, 'seq', perm).astype(jnp.float32)  8.51 us
    pallas_call x1, Pallas kernels, attention_forward(): pl.pallas_call(functools.partial(forward_kernel, head_dim), out_shape=jax...  6.99 us
  transfers between devices with their start and end apart: 16, of which 10 were waited for; matrix products, arithmetic and copies ran while one was open for 11% of the time, Pallas kernels for 6%

profile of v2, /device:TPU:0, one launch (start us, length us, event | category | flops | bytes accessed | tf_op | source)
XLA Modules:
  0.0 197.1 jit_solution(8503483240661845610)
XLA Ops:
  1.4 1.0 fusion.26
  2.5 1.0 fusion.19
  3.5 0.9 fusion.34
  4.5 0.7 add_convert_fusion.1
  5.2 0.7 pad_maximum_fusion.7
  6.0 7.4 %all-to-all-start = ((f32[16,3,640]{2,1,0:T(4,128)}), f32[16,3,640]{2,1,0:T(4,128)S(1)}, u32[]{:S(2)}, u32[]{:S(2)}) async-start(f32[16,3,640]{2,1,0:T(4,128)} %pad_maximum_fusion.7), calls=%async_computation | async-start | bytes 327680 | tf_op jit(solution)/shard_map/all_to_all | solution.py:153
  13.4 2.7 %copy.76 = bf16[512,1536]{0,1:T(8,128)(2,1)} copy(bf16[512,1536]{1,0:T(8,128)(2,1)} %param.14) | data formatting | bytes 3145728 | tf_op args[3]
  16.0 1.8 fusion.1
  18.0 0.8 copy.75
  18.8 3.0 %all-to-all-done = f32[16,3,640]{2,1,0:T(4,128)S(1)} async-done(((f32[16,3,640]{2,1,0:T(4,128)}), f32[16,3,640]{2,1,0:T(4,128)S(1)}, u32[]{:S(2)}, u32[]{:S(2)}) %all-to-all-start) | async-done | bytes 122912 | tf_op jit(solution)/shard_map/all_to_all | solution.py:153
  21.9 0.7 broadcast_in_dim.7
  22.6 3.5 %all-to-all-start.2 = ((f32[16,2,640]{2,1,0:T(2,128)}), f32[16,2,640]{2,1,0:T(2,128)S(1)}, u32[]{:S(2)}, u32[]{:S(2)}) async-start(f32[16,2,640]{2,1,0:T(2,128)} %broadcast_in_dim.7), calls=%async_computation.2 | async-start | bytes 163840 | tf_op jit(solution)/shard_map/all_to_all | solution.py:153
  26.2 7.0 %all-to-all-done.2 = f32[16,2,640]{2,1,0:T(2,128)S(1)} async-done(((f32[16,2,640]{2,1,0:T(2,128)}), f32[16,2,640]{2,1,0:T(2,128)S(1)}, u32[]{:S(2)}, u32[]{:S(2)}) %all-to-all-start.2) | async-done | bytes 81952 | tf_op jit(solution)/shard_map/all_to_all | solution.py:153
  33.2 3.6 %all-to-all-start.1 = ((bf16[16,96,128]{2,1,0:T(8,128)(2,1)}), bf16[16,96,128]{2,1,0:T(8,128)(2,1)S(1)}, u32[]{:S(2)}, u32[]{:S(2)}) async-start(bf16[16,96,128]{2,1,0:T(8,128)(2,1)} %bitcast.5), calls=%async_computation.1 | async-start | bytes 786432 | tf_op jit(solution)/shard_map/all_to_all | solution.py:153
  37.9 1.0 convolution_convert_fusion.6.virt_ref
  38.9 10.0 %all-to-all-done.1.qkv_ref = bf16[16,96,128]{2,1,0:T(8,128)(2,1)S(1)} async-done(((bf16[16,96,128]{2,1,0:T(8,128)(2,1)}), bf16[16,96,128]{2,1,0:T(8,128)(2,1)S(1)}, u32[]{:S(2)}, u32[]{:S(2)}) %all-to-all-start.1) | async-done | bytes 393248 | tf_op jit(solution)/shard_map/all_to_all | solution.py:153
  48.9 7.0 %shard_map.162 = bf16[16,32,128]{2,1,0:T(8,128)(2,1)} custom-call(s32[16,5]{1,0:T(8,128)S(1)} %copy.77.lists_ref, bf16[16,96,128]{2,1,0:T(8,128)(2,1)S(1)} %all-to-all-done.1.qkv_ref, bf16[2,32,32]{2,1,0:T(8,128)(2,1)S(1)} %convolution_convert_fusion.6.virt_ref), custom_call_target="tpu_custom_call" | custom-call | flops 142606336 | bytes 393216 | tf_op jit(solution)/shard_map/pallas_call | solution.py:117
  55.9 3.5 %all-to-all-start.3 = ((bf16[16,32,128]{2,1,0:T(8,128)(2,1)}), bf16[16,32,128]{2,1,0:T(8,128)(2,1)S(1)}, u32[]{:S(2)}, u32[]{:S(2)}) async-start(bf16[16,32,128]{2,1,0:T(8,128)(2,1)} %shard_map.162), calls=%async_computation.3 | async-start | bytes 262144 | tf_op jit(solution)/shard_map/all_to_all | solution.py:153
  59.5 7.9 %all-to-all-done.3 = bf16[16,32,128]{2,1,0:T(8,128)(2,1)S(1)} async-done(((bf16[16,32,128]{2,1,0:T(8,128)(2,1)}), bf16[16,32,128]{2,1,0:T(8,128)(2,1)S(1)}, u32[]{:S(2)}, u32[]{:S(2)}) %all-to-all-start.3) | async-done | bytes 131104 | tf_op jit(solution)/shard_map/all_to_all | solution.py:153
  67.4 0.7 copy-done.11
  68.0 1.3 multiply_reduce_fusion.2
  69.9 0.7 copy-done.13
  71.1 1.4 multiply_reduce_fusion
  72.6 0.8 convolution_convert_fusion
  75.3 1.6 dynamic-slice_bitcast_fusion
  76.8 0.8 copy-done.1
  77.6 1.9 fusion.7
  79.5 1.7 copy.78
  81.2 3.5 %all-to-all-start.4 = ((bf16[16,32,128]{2,1,0:T(8,128)(2,1)}), bf16[16,32,128]{2,1,0:T(8,128)(2,1)S(1)}, u32[]{:S(2)}, u32[]{:S(2)}) async-start(bf16[16,32,128]{2,1,0:T(8,128)(2,1)} %bitcast.11), calls=%async_computation.4 | async-start | bytes 262144 | tf_op jit(solution)/shard_map/all_to_all | solution.py:153
  84.7 3.8 %fusion = bf16[8,32,3584]{2,1,0:T(8,128)(2,1)} fusion(bf16[8,32,3584]{2,1,0:T(8,128)(2,1)} %collective-permute-done, bf16[8,2,32,3584]{3,2,1,0:T(8,128)(2,1)} %copy-done.1, s32[]{:T(128)S(6)} %select_n.100), kind=kLoop, calls=%fused_computation.2 | loop fusion | flops 3670016 | bytes 5505028 | tf_op jit(solution)/shard_map/convert_element_type | solution.py:163
  88.5 4.1 %all-to-all-done.4.grad_ref = bf16[16,32,128]{2,1,0:T(8,128)(2,1)S(1)} async-done(((bf16[16,32,128]{2,1,0:T(8,128)(2,1)}), bf16[16,32,128]{2,1,0:T(8,128)(2,1)S(1)}, u32[]{:S(2)}, u32[]{:S(2)}) %all-to-all-start.4) | async-done | bytes 131104 | tf_op jit(solution)/shard_map/all_to_all | solution.py:153
  92.6 2.2 %dynamic-slice_bitcast_fusion.1 = bf16[4,32,3584]{2,1,0:T(8,128)(2,1)} fusion(bf16[4,2,32,3584]{3,2,1,0:T(8,128)(2,1)} %bitcast.108, s32[]{:T(128)S(6)} %select_n.105), kind=kLoop, calls=%fused_computation.26 | loop fusion | bytes 1835012 | tf_op jit(solution)/shard_map/jit(dynamic_index_in_dim)/squeeze | solution.py:161
  94.8 11.8 %shard_map.163 = (bf16[16,32,128]{2,1,0:T(8,128)(2,1)S(1)}, bf16[16,64,128]{2,1,0:T(8,128)(2,1)S(1)}, f32[64,32]{1,0:T(8,128)S(1)}) custom-call(s32[16,5]{1,0:T(8,128)S(1)} %copy.77.lists_ref, bf16[16,96,128]{2,1,0:T(8,128)(2,1)S(1)} %all-to-all-done.1.qkv_ref, bf16[2,32,32]{2,1,0:T(8,128)(2,1)S(1)} %convolution_convert_fusion.6.virt_ref, ...), custom_call_target="tpu_custom_call" | custom-call | flops 356515840 | bytes 1179648 | tf_op jit(solution)/shard_map/pallas_call | solution.py:135
  106.6 10.1 %collective-permute-done.1 = bf16[4,32,3584]{2,1,0:T(8,128)(2,1)} collective-permute-done((bf16[4,32,3584]{2,1,0:T(8,128)(2,1)}, bf16[4,32,3584]{2,1,0:T(8,128)(2,1)}, u32[]{:S(2)}, u32[]{:S(2)}) %collective-permute-start.1) | collective-permute-done | bytes 917536 | tf_op jit(solution)/shard_map/ppermute | solution.py:162
  116.7 1.5 fusion.2
  118.1 0.9 copy-done.5
  119.1 0.9 dynamic-slice_bitcast_fusion.6
  120.0 1.5 collective-permute-start.4
  122.1 1.0 collective-permute-start.2
  123.3 0.8 pad_maximum_fusion.2
  124.1 4.4 %all-to-all-start.5 = ((bf16[16,112,128]{2,1,0:T(8,128)(2,1)}), bf16[16,112,128]{2,1,0:T(8,128)(2,1)S(1)}, u32[]{:S(2)}, u32[]{:S(2)}) async-start(bf16[16,112,128]{2,1,0:T(8,128)(2,1)} %pad_maximum_fusion.2), calls=%async_computation.5 | async-start | bytes 917504 | tf_op jit(solution)/shard_map/all_to_all | solution.py:153
  128.5 20.1 %collective-permute-done.3 = bf16[32,3584]{1,0:T(8,128)(2,1)} collective-permute-done((bf16[32,3584]{1,0:T(8,128)(2,1)}, bf16[32,3584]{1,0:T(8,128)(2,1)}, u32[]{:S(2)}, u32[]{:S(2)}) %collective-permute-start.3) | collective-permute-done | bytes 229408 | tf_op jit(solution)/shard_map/ppermute | solution.py:180
  148.6 2.0 %fusion.13 = f32[32,3584]{1,0:T(8,128)} fusion(bf16[32,3584]{1,0:T(8,128)(2,1)S(1)} %collective-permute-done.4, bf16[32,3584]{1,0:T(8,128)(2,1)} %collective-permute-done.3, bf16[32,3584]{1,0:T(8,128)(2,1)} %collective-permute-done.2, bf16[4,32,3584]{2,1,0:T(8,128)(2,1)} %copy-done.5, s32[]{:T(128)S(6)} %select_n.107), kind=kLoop, calls=%fused_computation.39 | loop fusion | flops 802816 | bytes 1376260 | tf_op jit(solution)/shard_map/add | solution.py:180
  151.4 0.7 copy-done.2
  152.1 0.6 fusion.63
  152.7 1.8 convolution_convert_fusion.1
  155.4 1.8 multiply_reduce_fusion.3
  157.2 2.8 %copy_dynamic-update-slice_fusion = bf16[8,2,32,1664]{3,2,0,1:T(8,128)(2,1)} fusion(bf16[8,2,32,1536]{3,2,1,0:T(8,128)(2,1)} %bitcast.110), kind=kLoop, calls=%fused_computation.12 | loop fusion | bytes 3145728
  160.0 1.1 fusion.25
  161.2 0.7 copy_dynamic-update-slice_fusion.1
  162.0 2.1 %dynamic-slice_bitcast_fusion.2 = bf16[8,32,1664]{2,1,0:T(8,128)(2,1)} fusion(bf16[8,2,32,1664]{3,2,0,1:T(8,128)(2,1)} %copy_dynamic-update-slice_fusion.1, s32[]{:T(128)S(6)} %select_n.101), kind=kLoop, calls=%fused_computation.29 | loop fusion | bytes 1703940 | tf_op jit(solution)/shard_map/jit(dynamic_index_in_dim)/squeeze | solution.py:161
  164.6 2.3 %fusion.6 = bf16[128,512]{1,0:T(8,128)(2,1)} fusion(f32[128,512]{1,0:T(8,128)S(1)} %get-tuple-element.47, bf16[128,1024]{1,0:T(8,128)(2,1)S(1)} %copy-done.15, bf16[1024,512]{1,0:T(8,128)(2,1)} %param.17), kind=kOutput, calls=%fused_computation.21 | convolution fusion | flops 134348800 | bytes 1703936 | tf_op jit(solution)/shard_map/dot_general | solution.py:280
  167.0 0.7 slice.84
  168.3 1.4 fusion.3
  169.8 1.8 collective-permute-start.6
  171.5 0.8 fusion.24
  172.4 9.2 %collective-permute-done.6 = bf16[4,32,1664]{2,1,0:T(8,128)(2,1)S(1)} collective-permute-done((bf16[4,32,1664]{2,1,0:T(8,128)(2,1)S(1)}, bf16[4,32,1664]{2,1,0:T(8,128)(2,1)S(1)}, u32[]{:S(2)}, u32[]{:S(2)}) %collective-permute-start.6) | collective-permute-done | bytes 426016 | tf_op jit(solution)/shard_map/ppermute | solution.py:162
  181.7 3.5 %collective-permute-start.9 = (bf16[32,1664]{1,0:T(8,128)(2,1)S(1)}, bf16[32,1664]{1,0:T(8,128)(2,1)S(1)}, u32[]{:S(2)}, u32[]{:S(2)}) collective-permute-start(bf16[32,1664]{1,0:T(8,128)(2,1)S(1)} %get-tuple-element.44), channel_id=1, source_target_pairs={{0,12},{1,13},{2,14},{3,15},{4,0},{5,1},{6,2},{7,3},{8,4},{9,5},{1... | collective-permute-start | bytes 319496 | tf_op jit(solution)/shard_map/ppermute | solution.py:180
  185.3 1.9 collective-permute-start.7
  187.1 0.7 pad_maximum_fusion.8
  187.8 0.9 collective-permute-done.9
  188.7 6.1 %collective-permute-done.8 = bf16[32,1664]{1,0:T(8,128)(2,1)S(1)} collective-permute-done((bf16[32,1664]{1,0:T(8,128)(2,1)S(1)}, bf16[32,1664]{1,0:T(8,128)(2,1)S(1)}, u32[]{:S(2)}, u32[]{:S(2)}) %collective-permute-start.8) | collective-permute-done | bytes 106528 | tf_op jit(solution)/shard_map/ppermute | solution.py:180
  195.4 1.0 slice_add_fusion
  196.4 0.7 pad_maximum_fusion.6
  (105 shorter events, 9.1 us)
Async XLA Ops:
  0.6 68.7 %copy-start = (bf16[512,2048]{1,0:T(8,128)(2,1)S(1)}, bf16[512,2048]{1,0:T(8,128)(2,1)}, u32[]{:S(2)}) copy-start(bf16[512,2048]{1,0:T(8,128)(2,1)} %param.16) | copy-start | bytes 6291460
  6.0 15.8 %all-to-all-start = ((f32[16,3,640]{2,1,0:T(4,128)}), f32[16,3,640]{2,1,0:T(4,128)S(1)}, u32[]{:S(2)}, u32[]{:S(2)}) async-start(f32[16,3,640]{2,1,0:T(4,128)} %pad_maximum_fusion.7), calls=%async_computation | async-start | bytes 327680 | tf_op jit(solution)/shard_map/all_to_all | solution.py:153
  22.6 10.6 %all-to-all-start.2 = ((f32[16,2,640]{2,1,0:T(2,128)}), f32[16,2,640]{2,1,0:T(2,128)S(1)}, u32[]{:S(2)}, u32[]{:S(2)}) async-start(f32[16,2,640]{2,1,0:T(2,128)} %broadcast_in_dim.7), calls=%async_computation.2 | async-start | bytes 163840 | tf_op jit(solution)/shard_map/all_to_all | solution.py:153
  33.2 15.7 %all-to-all-start.1 = ((bf16[16,96,128]{2,1,0:T(8,128)(2,1)}), bf16[16,96,128]{2,1,0:T(8,128)(2,1)S(1)}, u32[]{:S(2)}, u32[]{:S(2)}) async-start(bf16[16,96,128]{2,1,0:T(8,128)(2,1)} %bitcast.5), calls=%async_computation.1 | async-start | bytes 786432 | tf_op jit(solution)/shard_map/all_to_all | solution.py:153
  37.2 1.7 copy-start.24
  37.3 0.6 copy-start.19
  38.9 29.1 %copy-start.6 = (bf16[512,512]{1,0:T(8,128)(2,1)S(1)}, bf16[512,512]{1,0:T(8,128)(2,1)}, u32[]{:S(2)}) copy-start(bf16[512,512]{1,0:T(8,128)(2,1)} %param.15) | copy-start | bytes 1572868
  38.9 30.5 %copy-start.20 = (f32[512]{0:T(512)S(1)}, f32[512]{0:T(512)}, u32[]{:S(2)}) copy-start(f32[512]{0:T(512)} %param.13) | copy-start | bytes 6148
  55.9 11.4 %all-to-all-start.3 = ((bf16[16,32,128]{2,1,0:T(8,128)(2,1)}), bf16[16,32,128]{2,1,0:T(8,128)(2,1)S(1)}, u32[]{:S(2)}, u32[]{:S(2)}) async-start(bf16[16,32,128]{2,1,0:T(8,128)(2,1)} %shard_map.162), calls=%async_computation.3 | async-start | bytes 262144 | tf_op jit(solution)/shard_map/all_to_all | solution.py:153
  67.4 0.7 copy-start.11
  69.3 1.2 copy-start.13
  69.3 1.2 copy-start.16
  71.1 2.3 %copy-start.14 = (bf16[128,1024]{1,0:T(8,128)(2,1)}, bf16[128,1024]{1,0:T(8,128)(2,1)S(1)}, u32[]{:S(2)}) copy-start(bf16[128,1024]{1,0:T(8,128)(2,1)S(1)} %get-tuple-element.33) | copy-start | bytes 786436
  73.4 0.9 copy-start.12
  74.3 0.7 copy-start.8
  75.3 2.4 %copy-start.1 = (bf16[8,2,32,3584]{3,2,1,0:T(8,128)(2,1)}, bf16[8,2,32,3584]{3,2,1,0:T(8,128)(2,1)S(1)}, u32[]{:S(2)}) copy-start(bf16[8,2,32,3584]{3,2,1,0:T(8,128)(2,1)S(1)} %pad_maximum_fusion) | copy-start | bytes 11010052
  77.6 7.1 %collective-permute-start = (bf16[8,32,3584]{2,1,0:T(8,128)(2,1)}, bf16[8,32,3584]{2,1,0:T(8,128)(2,1)}, u32[]{:S(2)}, u32[]{:S(2)}) collective-permute-start(bf16[8,32,3584]{2,1,0:T(8,128)(2,1)} %dynamic-slice_bitcast_fusion), channel_id=1, source_target_pairs={{0,1},{1,0},{2,3},{3,2},{4,5},{5,4},{6,7},{7,6},{8,9},{9,8},{10,11... | collective-permute-start | bytes 5505032 | tf_op jit(solution)/shard_map/ppermute | solution.py:162
  81.2 11.4 %all-to-all-start.4 = ((bf16[16,32,128]{2,1,0:T(8,128)(2,1)}), bf16[16,32,128]{2,1,0:T(8,128)(2,1)S(1)}, u32[]{:S(2)}, u32[]{:S(2)}) async-start(bf16[16,32,128]{2,1,0:T(8,128)(2,1)} %bitcast.11), calls=%async_computation.4 | async-start | bytes 262144 | tf_op jit(solution)/shard_map/all_to_all | solution.py:153
  94.7 21.9 %collective-permute-start.1 = (bf16[4,32,3584]{2,1,0:T(8,128)(2,1)}, bf16[4,32,3584]{2,1,0:T(8,128)(2,1)}, u32[]{:S(2)}, u32[]{:S(2)}) collective-permute-start(bf16[4,32,3584]{2,1,0:T(8,128)(2,1)} %dynamic-slice_bitcast_fusion.1), channel_id=1, source_target_pairs={{0,2},{1,3},{2,0},{3,1},{4,6},{5,7},{6,4},{7,5},{8,10},{9,11},{10,... | collective-permute-start | bytes 2752520 | tf_op jit(solution)/shard_map/ppermute | solution.py:162
  94.8 21.9 %copy-start.3 = (bf16[8,32,3584]{2,1,0:T(8,128)(2,1)S(1)}, bf16[8,32,3584]{2,1,0:T(8,128)(2,1)}, u32[]{:S(2)}) copy-start(bf16[8,32,3584]{2,1,0:T(8,128)(2,1)} %fusion) | copy-start | bytes 5505028
  106.6 16.5 %copy-start.22 = (bf16[512]{0:T(512)(128)(2,1)S(1)}, bf16[512]{0:T(512)(128)(2,1)}, u32[]{:S(2)}) copy-start(bf16[512]{0:T(512)(128)(2,1)} %get-tuple-element.25) | copy-start | bytes 3076
  118.1 1.0 copy-start.5
  120.0 8.6 %collective-permute-start.4 = (bf16[32,3584]{1,0:T(8,128)(2,1)}, bf16[32,3584]{1,0:T(8,128)(2,1)S(1)}, u32[]{:S(2)}, u32[]{:S(2)}) collective-permute-start(bf16[32,3584]{1,0:T(8,128)(2,1)} %get-tuple-element.35), channel_id=1, source_target_pairs={{0,12},{1,13},{2,14},{3,15},{4,0},{5,1},{6,2},{7,3},{8,4},{9,5},{1... | collective-permute-start | bytes 688136 | tf_op jit(solution)/shard_map/ppermute | solution.py:180
  121.5 27.1 %collective-permute-start.3 = (bf16[32,3584]{1,0:T(8,128)(2,1)}, bf16[32,3584]{1,0:T(8,128)(2,1)}, u32[]{:S(2)}, u32[]{:S(2)}) collective-permute-start(bf16[32,3584]{1,0:T(8,128)(2,1)} %get-tuple-element.36), channel_id=1, source_target_pairs={{0,8},{1,9},{2,10},{3,11},{4,12},{5,13},{6,14},{7,15},{8,0},{9,1},... | collective-permute-start | bytes 688136 | tf_op jit(solution)/shard_map/ppermute | solution.py:180
  122.1 26.5 %collective-permute-start.2 = (bf16[32,3584]{1,0:T(8,128)(2,1)}, bf16[32,3584]{1,0:T(8,128)(2,1)}, u32[]{:S(2)}, u32[]{:S(2)}) collective-permute-start(bf16[32,3584]{1,0:T(8,128)(2,1)} %get-tuple-element.34), channel_id=1, source_target_pairs={{0,4},{1,5},{2,6},{3,7},{4,8},{5,9},{6,10},{7,11},{8,12},{9,13},{1... | collective-permute-start | bytes 688136 | tf_op jit(solution)/shard_map/ppermute | solution.py:180
  124.1 26.5 %all-to-all-start.5 = ((bf16[16,112,128]{2,1,0:T(8,128)(2,1)}), bf16[16,112,128]{2,1,0:T(8,128)(2,1)S(1)}, u32[]{:S(2)}, u32[]{:S(2)}) async-start(bf16[16,112,128]{2,1,0:T(8,128)(2,1)} %pad_maximum_fusion.2), calls=%async_computation.5 | async-start | bytes 917504 | tf_op jit(solution)/shard_map/all_to_all | solution.py:153
  150.6 1.4 copy-start.2
  152.1 2.4 %copy-start.18 = (bf16[16,16,128]{2,1,0:T(8,128)(2,1)S(1)}, bf16[16,16,128]{2,1,0:T(8,128)(2,1)}, u32[]{:S(2)}) copy-start(bf16[16,16,128]{2,1,0:T(8,128)(2,1)} %slice.79) | copy-start | bytes 196612
  152.7 2.7 %copy-start.25 = (f32[32]{0:T(128)S(1)}, f32[32]{0:T(128)}, u32[]{:S(2)}) copy-start(f32[32]{0:T(128)} %copy-done.24) | copy-start | bytes 388
  157.1 2.9 %copy-start.7 = (bf16[128,512]{1,0:T(8,128)(2,1)S(1)}, bf16[128,512]{1,0:T(8,128)(2,1)}, u32[]{:S(2)}) copy-start(bf16[128,512]{1,0:T(8,128)(2,1)} %param.11) | copy-start | bytes 393220
  157.2 2.8 %copy-start.21 = (f32[512]{0:T(512)S(1)}, f32[512]{0:T(512)}, u32[]{:S(2)}) copy-start(f32[512]{0:T(512)} %param.12) | copy-start | bytes 6148
  157.2 2.8 %copy-start.23 = (s32[128]{0:T(128)S(1)}, s32[128]{0:T(128)}, u32[]{:S(2)}) copy-start(s32[128]{0:T(128)} %param.20) | copy-start | bytes 1540
  157.2 2.8 %copy-start.26 = (f32[32]{0:T(128)S(1)}, f32[32]{0:T(128)}, u32[]{:S(2)}) copy-start(f32[32]{0:T(128)} %copy-done.24) | copy-start | bytes 388
  160.0 4.6 %copy-start.15 = (bf16[128,1024]{1,0:T(8,128)(2,1)S(1)}, bf16[128,1024]{1,0:T(8,128)(2,1)}, u32[]{:S(2)}) copy-start(bf16[128,1024]{1,0:T(8,128)(2,1)} %copy-done.14) | copy-start | bytes 786436
  161.2 5.7 %copy-start.10 = (f32[32,3584]{1,0:T(8,128)S(1)}, f32[32,3584]{1,0:T(8,128)}, u32[]{:S(2)}) copy-start(f32[32,3584]{1,0:T(8,128)} %fusion.13) | copy-start | bytes 1376260
  164.1 4.2 %collective-permute-start.5 = (bf16[8,32,1664]{2,1,0:T(8,128)(2,1)}, bf16[8,32,1664]{2,1,0:T(8,128)(2,1)}, u32[]{:S(2)}, u32[]{:S(2)}) collective-permute-start(bf16[8,32,1664]{2,1,0:T(8,128)(2,1)} %dynamic-slice_bitcast_fusion.2), channel_id=1, source_target_pairs={{0,1},{1,0},{2,3},{3,2},{4,5},{5,4},{6,7},{7,6},{8,9},{9,8},{10,11... | collective-permute-start | bytes 2555912 | tf_op jit(solution)/shard_map/ppermute | solution.py:162
  164.6 3.7 %copy-start.4 = (bf16[8,2,32,1664]{3,2,0,1:T(8,128)(2,1)S(1)}, bf16[8,2,32,1664]{3,2,0,1:T(8,128)(2,1)}, u32[]{:S(2)}) copy-start(bf16[8,2,32,1664]{3,2,0,1:T(8,128)(2,1)} %copy_dynamic-update-slice_fusion.1) | copy-start | bytes 5111812
  167.7 3.9 %copy-start.9 = (bf16[128,512]{1,0:T(8,128)(2,1)S(1)}, bf16[128,512]{1,0:T(8,128)(2,1)}, u32[]{:S(2)}) copy-start(bf16[128,512]{1,0:T(8,128)(2,1)} %copy-done.8) | copy-start | bytes 393220
  167.7 3.9 %copy-start.17 = (f32[128,512]{1,0:T(8,128)S(1)}, f32[128,512]{1,0:T(8,128)}, u32[]{:S(2)}) copy-start(f32[128,512]{1,0:T(8,128)} %get-tuple-element.51) | copy-start | bytes 786436
  169.8 11.8 %collective-permute-start.6 = (bf16[4,32,1664]{2,1,0:T(8,128)(2,1)S(1)}, bf16[4,32,1664]{2,1,0:T(8,128)(2,1)S(1)}, u32[]{:S(2)}, u32[]{:S(2)}) collective-permute-start(bf16[4,32,1664]{2,1,0:T(8,128)(2,1)S(1)} %dynamic-slice_bitcast_fusion.3), channel_id=1, source_target_pairs={{0,2},{1,3},{2,0},{3,1},{4,6},{5,7},{6,4},{7,5},{8,10},{9,11},{10,... | collective-permute-start | bytes 1277960 | tf_op jit(solution)/shard_map/ppermute | solution.py:162
  181.7 7.0 %collective-permute-start.9 = (bf16[32,1664]{1,0:T(8,128)(2,1)S(1)}, bf16[32,1664]{1,0:T(8,128)(2,1)S(1)}, u32[]{:S(2)}, u32[]{:S(2)}) collective-permute-start(bf16[32,1664]{1,0:T(8,128)(2,1)S(1)} %get-tuple-element.44), channel_id=1, source_target_pairs={{0,12},{1,13},{2,14},{3,15},{4,0},{5,1},{6,2},{7,3},{8,4},{9,5},{1... | collective-permute-start | bytes 319496 | tf_op jit(solution)/shard_map/ppermute | solution.py:180
  185.2 9.6 %collective-permute-start.8 = (bf16[32,1664]{1,0:T(8,128)(2,1)S(1)}, bf16[32,1664]{1,0:T(8,128)(2,1)S(1)}, u32[]{:S(2)}, u32[]{:S(2)}) collective-permute-start(bf16[32,1664]{1,0:T(8,128)(2,1)S(1)} %get-tuple-element.45), channel_id=1, source_target_pairs={{0,8},{1,9},{2,10},{3,11},{4,12},{5,13},{6,14},{7,15},{8,0},{9,1},... | collective-permute-start | bytes 319496 | tf_op jit(solution)/shard_map/ppermute | solution.py:180
  185.3 9.6 %collective-permute-start.7 = (bf16[32,1664]{1,0:T(8,128)(2,1)S(1)}, bf16[32,1664]{1,0:T(8,128)(2,1)S(1)}, u32[]{:S(2)}, u32[]{:S(2)}) collective-permute-start(bf16[32,1664]{1,0:T(8,128)(2,1)S(1)} %get-tuple-element.43), channel_id=1, source_target_pairs={{0,4},{1,5},{2,6},{3,7},{4,8},{5,9},{6,10},{7,11},{8,12},{9,13},{1... | collective-permute-start | bytes 319496 | tf_op jit(solution)/shard_map/ppermute | solution.py:180

commit v3 on v2

--- a/solution.py
+++ b/solution.py
@@ -153,32 +153,111 @@
     return lax.all_to_all(blocks, "seq", split_axis=0, concat_axis=0, tiled=True)
 
 
-def halve(held, bit):
+def as_bits(blocks):
+    bits = blocks.shape[0].bit_length() - 1
+    return blocks.reshape((2,) * bits + blocks.shape[1:]), list(range(bits - 1, -1, -1))
+
+
+def halve(held, left, bit, last=False):
     size = lax.axis_size("seq")
-    mine = (lax.axis_index("seq") // bit) % 2
-    split = held.reshape((held.shape[0] // 2, 2) + held.shape[1:])
-    keep = lax.dynamic_index_in_dim(split, mine, 1, keepdims=False)
-    send = lax.dynamic_index_in_dim(split, 1 - mine, 1, keepdims=False)
-    got = lax.ppermute(send, "seq", [(i, i ^ bit) for i in range(size)])
-    return (keep.astype(jnp.float32) + got.astype(jnp.float32)).astype(jnp.bfloat16)
-
-
-def finish(held):
-    size = lax.axis_size("seq")
-    count = size // 4
-    if count > 4:
-        groups = [[j + 4 * m for m in range(count)] for j in range(4)]
-        got = lax.all_to_all(
-            held, "seq", split_axis=0, concat_axis=0, axis_index_groups=groups, tiled=True
+    mine = (lax.axis_index("seq") // (1 << bit)) % 2
+    axis = left.index(bit)
+    keep = lax.dynamic_index_in_dim(held, mine, axis, keepdims=False)
+    send = lax.dynamic_index_in_dim(held, 1 - mine, axis, keepdims=False)
+    got = lax.ppermute(send, "seq", [(i, i ^ (1 << bit)) for i in range(size)])
+    total = keep.astype(jnp.float32) + got.astype(jnp.float32)
+    rest = [b for b in left if b != bit]
+    return (total if not rest else total.astype(jnp.bfloat16)), rest
+
+
+def reduce_in_order(blocks, order):
+    held, left = as_bits(blocks)
+    for bit in order:
+        held, left = halve(held, left, bit)
+    return held
+
+
+def exchange_kernel(
+    slices, sums_ref, list_ref, qkv_ref, qkv_all_ref, second_ref, first_ref, own_ref, send, recv
+):
+    size = qkv_all_ref.shape[0]
+    me = lax.axis_index("seq")
+
+    def peer(k):
+        return lax.rem(me + k, size)
+
+    def each(step):
+        def body(k, carry):
+            step(k, peer(k))
+            return carry
+
+        lax.fori_loop(1, size, body, 0)
+
+    def remote(src, dst, which, k, to):
+        return pltpu.make_async_remote_copy(
+            src_ref=src,
+            dst_ref=dst,
+            send_sem=send.at[which, k],
+            recv_sem=recv.at[which, k],
+            device_id={"seq": to},
+            device_id_type=pl.DeviceIdType.MESH,
         )
-        return jnp.sum(got.astype(jnp.float32), axis=0)
-    mine = lax.axis_index("seq") // 4
-    total = lax.dynamic_index_in_dim(held, mine, 0, keepdims=False).astype(jnp.float32)
-    for k in range(1, count):
-        send = lax.dynamic_index_in_dim(held, (mine + k) % count, 0, keepdims=False)
-        perm = [(i, ((i // 4 + k) % count) * 4 + i % 4) for i in range(size)]
-        total = total + lax.ppermute(send, "seq", perm).astype(jnp.float32)
-    return total
+
+    def first_copy(k, to):
+        return remote(sums_ref.at[to], first_ref.at[me], 0, k, to)
+
+    def second_copy(k, to):
+        return remote(own_ref, second_ref.at[me], 1, k, to)
+
+    def head_copy(k, to):
+        return remote(qkv_ref.at[to // slices], qkv_all_ref.at[me], 2, k, to)
+
+    barrier = pltpu.get_barrier_semaphore()
+    each(
+        lambda k, to: pl.semaphore_signal(
+            barrier, inc=1, device_id={"seq": to}, device_id_type=pl.DeviceIdType.MESH
+        )
+    )
+    first_ref[me] = sums_ref[me]
+    qkv_all_ref[me] = qkv_ref[me // slices]
+    pl.semaphore_wait(barrier, size - 1)
+    each(lambda k, to: first_copy(k, to).start())
+    each(lambda k, to: head_copy(k, to).start())
+    each(lambda k, to: first_copy(k, to).wait_recv())
+    own_ref[...] = list_ref[...] + jnp.sum(first_ref[...], axis=0)
+    each(lambda k, to: second_copy(k, to).start())
+    second_ref[me] = own_ref[...]
+    each(lambda k, to: second_copy(k, to).wait_recv())
+    each(lambda k, to: head_copy(k, to).wait_recv())
+    each(lambda k, to: first_copy(k, to).wait_send())
+    each(lambda k, to: second_copy(k, to).wait_send())
+    each(lambda k, to: head_copy(k, to).wait_send())
+
+
+def exchange(sums, list_rows, qkv_heads, slices):
+    size = sums.shape[0]
+    vmem = pl.BlockSpec(memory_space=pltpu.VMEM)
+    return pl.pallas_call(
+        functools.partial(exchange_kernel, slices),
+        out_shape=(
+            jax.ShapeDtypeStruct((size,) + qkv_heads.shape[1:], qkv_heads.dtype),
+            jax.ShapeDtypeStruct(sums.shape, sums.dtype),
+        ),
+        in_specs=[vmem, vmem, vmem],
+        out_specs=(vmem, vmem),
+        scratch_shapes=[
+            pltpu.VMEM(sums.shape, sums.dtype),
+            pltpu.VMEM(sums.shape[1:], sums.dtype),
+            pltpu.SemaphoreType.DMA((3, size)),
+            pltpu.SemaphoreType.DMA((3, size)),
+        ],
+        compiler_params=pltpu.CompilerParams(
+            vmem_limit_bytes=VMEM_BYTES, collective_id=0, has_side_effects=True
+        ),
+        cost_estimate=pl.CostEstimate(
+            flops=sums.size, bytes_accessed=4 * size * qkv_heads[0].size, transcendentals=0
+        ),
+    )(sums, list_rows, qkv_heads)
 
 
 def on_device(
@@ -212,40 +291,40 @@
     member = (partition[:, None] == jnp.arange(parts, dtype=jnp.int32)[None, :]).astype(
         jnp.bfloat16
     )
-    extended = jnp.concatenate([normed, jnp.ones((rows, 128), jnp.bfloat16)], axis=1)
-    part_sums = jnp.einsum("rp,rd->pd", member, extended, preferred_element_type=jnp.float32)
-    wide = width + 128
-    list_row = jnp.concatenate([tile_lists[0], tile_count]).astype(jnp.float32)
-    list_row = jnp.pad(list_row, (0, wide - KT - 1))
-    first_send = jnp.concatenate(
+    part_sums = jnp.einsum("rp,rd->pd", member, normed, preferred_element_type=jnp.float32)
+    part_counts = jnp.sum(member.astype(jnp.float32), axis=0)
+    lanes = 128
+    sum_rows = VN_DEV * width // lanes
+    list_at = sum_rows + VN_DEV
+    block_rows = -(-(list_at + 1) // 8) * 8
+    sums = jnp.concatenate(
         [
-            part_sums.reshape(seq_size, VN_DEV, wide),
-            jnp.broadcast_to(list_row, (seq_size, 1, wide)),
+            part_sums.reshape(seq_size, sum_rows, lanes),
+            jnp.broadcast_to(
+                part_counts.reshape(seq_size, VN_DEV, 1), (seq_size, VN_DEV, lanes)
+            ),
+            jnp.zeros((seq_size, block_rows - list_at, lanes), jnp.float32),
         ],
         axis=1,
     )
-    first = all_to_all(first_send)
-    own_sums = jnp.sum(first[:, :VN_DEV], axis=0)
-    lists_all = first[:, VN_DEV, : KT + 1].astype(jnp.int32)
-    second = all_to_all(jnp.broadcast_to(own_sums, (seq_size, VN_DEV, wide)))
-    second = second.reshape(parts, wide)
-    totals = second[:, :width]
-    counts = second[:, width : width + 1]
-    part_mean = totals / counts
-    inv_vn, unit_vn = rms_parts(part_mean)
-    virtual = unit_vn.astype(jnp.bfloat16)
-
+    list_rows = jnp.pad(
+        jnp.concatenate([tile_lists[0], tile_count]).astype(jnp.float32)[None],
+        ((list_at, block_rows - list_at - 1), (0, lanes - KT - 1)),
+    )
     qkv_t = jnp.einsum(
         "dc,rd->cr", query_key_value_weight, normed, preferred_element_type=jnp.float32
     ).astype(jnp.bfloat16)
     qkv_heads = jnp.transpose(qkv_t.reshape(3, HEADS, head_dim, rows), (1, 0, 2, 3)).reshape(
-        HEADS, 1, 3 * head_dim, rows
-    )
-    qkv_all = all_to_all(
-        jnp.broadcast_to(qkv_heads, (HEADS, slices, 3 * head_dim, rows)).reshape(
-            seq_size, 3 * head_dim, rows
-        )
-    )
+        HEADS, 3 * head_dim, rows
+    )
+    qkv_all, second = exchange(sums, list_rows, qkv_heads, slices)
+    totals = second[:, :sum_rows].reshape(parts, width)
+    counts = second[:, sum_rows:list_at, :1].reshape(parts, 1)
+    lists_all = second[:, list_at, : KT + 1].astype(jnp.int32)
+    part_mean = totals / counts
+    inv_vn, unit_vn = rms_parts(part_mean)
+    virtual = unit_vn.astype(jnp.bfloat16)
+
     lists = lax.dynamic_slice_in_dim(lists_all, my_slice * tiles_here, tiles_here, 0)
     weight_heads = query_key_value_weight.reshape(width, 3, HEADS, head_dim)
     my_columns = lax.dynamic_index_in_dim(weight_heads, my_head, 2, keepdims=False)[:, 1:]
@@ -304,21 +383,28 @@
     grad_in_local = jnp.einsum("rd,rf->df", normed_ffn, d_both, preferred_element_type=jnp.float32)
     grad_down_local = jnp.einsum("rf,rd->fd", hidden, grad_out, preferred_element_type=jnp.float32)
     down_blocks = grad_down_local.astype(jnp.bfloat16).reshape(seq_size, -1, share, width)
-    early = jnp.concatenate(
-        [
-            grad_out_local.astype(jnp.bfloat16).reshape(seq_size, share, -1),
-            grad_in_local.astype(jnp.bfloat16).reshape(seq_size, share, -1),
-        ]
-        + [down_blocks[:, i] for i in range(down_blocks.shape[1])],
-        axis=2,
-    )
-    early = halve(early, 1)
-    grads, early = lax.optimization_barrier((grads, early))
-    early = halve(early, 2)
+    bits = seq_size.bit_length() - 1
+    outer = list(range(2, bits))
+    one, one_left = as_bits(grad_in_local.astype(jnp.bfloat16).reshape(seq_size, share, -1))
+    two, two_left = as_bits(
+        jnp.concatenate(
+            [grad_out_local.astype(jnp.bfloat16).reshape(seq_size, share, -1)]
+            + [down_blocks[:, i] for i in range(down_blocks.shape[1])],
+            axis=2,
+        )
+    )
+    one, one_left = halve(one, one_left, 0)
+    two, two_left = halve(two, two_left, 0)
+    grads, one, two = lax.optimization_barrier((grads, one, two))
+    one, one_left = halve(one, one_left, 1)
+    two, two_left = halve(two, two_left, outer[0])
 
     dq, dkv, dvirt = attention_backward(lists, qkv_all, virt, grads, head_dim)
-    dq, early = lax.optimization_barrier((dq, early))
-    early_sum = finish(early)
+    dq, one, two = lax.optimization_barrier((dq, one, two))
+    for bit in outer:
+        one, one_left = halve(one, one_left, bit)
+    for bit in outer[1:] + [1]:
+        two, two_left = halve(two, two_left, bit)
     virt_rows = 2 * head_dim * parts // rows
     back_send = jnp.concatenate(
         [
@@ -331,7 +417,6 @@
         axis=1,
     )
     back = all_to_all(back_send)
-    back, early_sum = lax.optimization_barrier((back, early_sum))
     dq_t = pick_slice(back[:, :head_dim])
     rest = back[:, head_dim:]
     if slices > 1:
@@ -374,12 +459,11 @@
     late = jnp.concatenate(
         [grad_qkv_local.astype(jnp.bfloat16).reshape(seq_size, share, -1), gain_block], axis=2
     )
-    late_sum = finish(halve(halve(late, 1), 2))
-    grad_w_out = early_sum[:, :width]
-    in_end = width + 2 * hidden_units
-    grad_w_in = early_sum[:, width:in_end]
+    late_sum = reduce_in_order(late, [0, 1] + outer)
+    grad_w_in = one
+    grad_w_out = two[:, :width]
     grad_w_down = jnp.concatenate(
-        [early_sum[:, c : c + width] for c in range(in_end, early_sum.shape[1], width)], axis=0
+        [two[:, c : c + width] for c in range(width, two.shape[1], width)], axis=0
     )
     my_virtual = lax.dynamic_slice_in_dim(virtual, me * share, share, 1)
     virtual_grad = jnp.einsum("pd,sp->ds", my_virtual, d_virt, preferred_element_type=jnp.float32)

time: 198 us -> 173 us (0.87)
  waiting for transfers between devices: 78.4 us -> 47.4 us
  Pallas kernels: 18.8 us -> 40.8 us
  starting transfers between devices: 36.7 us -> 25.4 us
  matrix products: 19.3 us -> 16.2 us
  local copies, waits for them, and re-layouts: 25.6 us -> 23.5 us
    pallas_call x0 -> x1, Pallas kernels: none -> 22 us  [exchange(): pl.pallas_call(functools.partial(exchange_kernel, slices), out_shape=(jax...]
    all_to_all x6 -> x3, waiting for transfers between devices: 32 us -> 10.7 us  [all_to_all(): lax.all_to_all(blocks, 'seq', split_axis=0, concat_axis=0, tiled=True)]
    all_to_all x6 -> x3, starting transfers between devices: 25.9 us -> 13.6 us  [all_to_all(): lax.all_to_all(blocks, 'seq', split_axis=0, concat_axis=0, tiled=True)]
    ppermute x10 -> x12, waiting for transfers between devices: 46.4 us -> 36.6 us  [halve(): got = lax.ppermute(send, 'seq', [(i, i ^ 1 << bit) for i in range(size)])]
    unnamed x57 -> x44, local copies, waits for them, and re-layouts: 10.6 us -> 6.53 us
    dynamic_slice x0 -> x2, local copies, waits for them, and re-layouts: none -> 2.17 us  [the longest x1 1.12 us: halve(): keep = lax.dynamic_index_in_dim(held, mine, axis, keepdims=False)]
    convert_element_type x7 -> x11, other arithmetic: 8.47 us -> 9.71 us  [the longest x9 9.62 us: halve(): return (total if not rest else total.astype(jnp.bfloat16), rest)]
    squeeze x6 -> x11, local copies, waits for them, and re-layouts: 6.82 us -> 7.96 us  [halve(): send = lax.dynamic_index_in_dim(held, 1 - mine, axis, keepdims=False)]
  transfers between devices with their start and end apart: 16 -> 15, of which waited for: 10 -> 7; matrix products, arithmetic and copies ran while one was open for 11% -> 19% of each run, Pallas kernels for 6% -> 7%
where the time goes in v3:
time: 173 us; the launch traced here: 172 us
  waiting for transfers between devices  47.4 us (27%)
  Pallas kernels  40.8 us (24%)
  starting transfers between devices  25.4 us (15%)
  local copies, waits for them, and re-layouts  23.5 us (14%)
  other arithmetic  17.1 us (10%)
  matrix products  16.2 us (9%)
  between operations  1.93 us (1%)
    ppermute x12, waiting for transfers between devices, halve(): got = lax.ppermute(send, 'seq', [(i, i ^ 1 << bit) for i in range(size)])  36.6 us
    pallas_call x1, Pallas kernels, exchange(): pl.pallas_call(functools.partial(exchange_kernel, slices), out_shape=(jax...  22 us
    all_to_all x3, starting transfers between devices, all_to_all(): lax.all_to_all(blocks, 'seq', split_axis=0, concat_axis=0, tiled=True)  13.6 us
    pallas_call x1, Pallas kernels, attention_backward(): pl.pallas_call(functools.partial(backward_kernel, head_dim), out_shape=(j...  11.8 us
    ppermute x12, starting transfers between devices, halve(): got = lax.ppermute(send, 'seq', [(i, i ^ 1 << bit) for i in range(size)])  11.7 us
    all_to_all x3, waiting for transfers between devices, all_to_all(): lax.all_to_all(blocks, 'seq', split_axis=0, concat_axis=0, tiled=True)  10.7 us
    convert_element_type x9, other arithmetic, halve(): return (total if not rest else total.astype(jnp.bfloat16), rest)  9.62 us
    squeeze x11, local copies, waits for them, and re-layouts, halve(): send = lax.dynamic_index_in_dim(held, 1 - mine, axis, keepdims=False)  7.96 us
  transfers between devices with their start and end apart: 15, of which 7 were waited for; matrix products, arithmetic and copies ran while one was open for 19% of the time, Pallas kernels for 7%

profile of v3, /device:TPU:0, one launch (start us, length us, event | category | flops | bytes accessed | tf_op | source)
XLA Modules:
  0.0 172.3 jit_solution(6778351723570237803)
XLA Ops:
  0.6 0.9 convert_reduce_fusion
  1.6 1.0 fusion.29
  2.6 1.1 fusion.47
  3.7 1.9 %fusion = bf16[1536,128]{0,1:T(8,128)(2,1)S(1)} fusion(bf16[512,1536]{1,0:T(8,128)(2,1)} %param.14, bf16[128,512]{1,0:T(8,128)(2,1)} %param.11, f32[512]{0:T(512)} %param.12, f32[128]{0:T(128)S(1)} %add_rsqrt_fusion.2), kind=kOutput, calls=%fused_computation.3 | convolution fusion | flops 201785344 | bytes 2099712 | tf_op jit(solution)/shard_map/dc,rd->cr/dot_general | solution.py:314
  5.7 2.6 %copy.67 = bf16[512,1536]{0,1:T(8,128)(2,1)} copy(bf16[512,1536]{1,0:T(8,128)(2,1)} %param.14) | data formatting | bytes 3145728 | tf_op args[3]
  9.6 22.0 %shard_map.162 = (bf16[16,96,128]{2,1,0:T(8,128)(2,1)S(1)}, f32[16,16,128]{2,1,0:T(8,128)S(1)}) custom-call(f32[16,16,128]{2,1,0:T(8,128)S(1)} %maximum_maximum_fusion.sums_ref, f32[16,128]{1,0:T(8,128)S(1)} %pad.8.list_ref, bf16[16,96,128]{2,1,0:T(8,128)(2,1)S(1)} %bitcast.128), custom_call_target="tpu_custom_call" | custom-call | flops 32768 | bytes 786432 | tf_op jit(solution)/shard_map/pallas_call | solution.py:240
  32.5 1.0 convolution_convert_fusion.6.virt_ref
  33.5 7.0 %shard_map.163 = bf16[16,32,128]{2,1,0:T(8,128)(2,1)} custom-call(s32[16,5]{1,0:T(8,128)S(1)} %bitcast.129, bf16[16,96,128]{2,1,0:T(8,128)(2,1)S(1)} %get-tuple-element.19.qkv_ref, bf16[2,32,32]{2,1,0:T(8,128)(2,1)S(1)} %convolution_convert_fusion.6.virt_ref), custom_call_target="tpu_custom_call" | custom-call | flops 142606336 | bytes 393216 | tf_op jit(solution)/shard_map/pallas_call | solution.py:117
  40.5 5.5 %all-to-all-start = ((bf16[16,32,128]{2,1,0:T(8,128)(2,1)}), bf16[16,32,128]{2,1,0:T(8,128)(2,1)S(1)}, u32[]{:S(2)}, u32[]{:S(2)}) async-start(bf16[16,32,128]{2,1,0:T(8,128)(2,1)} %shard_map.163), calls=%async_computation | async-start | bytes 262144 | tf_op jit(solution)/shard_map/all_to_all | solution.py:153
  46.1 7.9 %all-to-all-done = bf16[16,32,128]{2,1,0:T(8,128)(2,1)S(1)} async-done(((bf16[16,32,128]{2,1,0:T(8,128)(2,1)}), bf16[16,32,128]{2,1,0:T(8,128)(2,1)S(1)}, u32[]{:S(2)}, u32[]{:S(2)}) %all-to-all-start) | async-done | bytes 131104 | tf_op jit(solution)/shard_map/all_to_all | solution.py:153
  54.0 1.4 multiply_reduce_fusion.2
  55.4 0.5 fusion.58
  55.9 0.7 copy-done.8
  56.6 0.5 multiply_convert_fusion.1
  57.2 1.0 multiply_reduce_fusion
  58.2 0.8 convolution_convert_fusion
  60.1 1.1 dynamic-slice_bitcast_fusion.1
  61.2 1.1 constant_dynamic-slice_fusion.1
  62.3 1.0 copy.94
  63.4 0.5 collective-permute-start
  63.9 1.3 fusion.7
  65.2 0.8 copy.71
  66.0 3.5 %all-to-all-start.1 = ((bf16[16,32,128]{2,1,0:T(8,128)(2,1)}), bf16[16,32,128]{2,1,0:T(8,128)(2,1)S(1)}, u32[]{:S(2)}, u32[]{:S(2)}) async-start(bf16[16,32,128]{2,1,0:T(8,128)(2,1)} %bitcast.15), calls=%async_computation.1 | async-start | bytes 262144 | tf_op jit(solution)/shard_map/all_to_all | solution.py:153
  69.5 2.6 %fusion.3 = bf16[2,2,2,32,1536]{4,3,2,1,0:T(8,128)(2,1)} fusion(bf16[2,2,2,32,1536]{4,3,2,1,0:T(8,128)(2,1)} %collective-permute-done.1, bf16[2,2,2,2,32,1536]{5,4,3,2,1,0:T(8,128)(2,1)} %copy-done.3, s32[]{:T(128)S(6)} %select_n.124), kind=kLoop, calls=%fused_computation.10 | loop fusion | flops 1572864 | bytes 2359300 | tf_op jit(solution)/shard_map/convert_element_type | solution.py:170
  72.1 2.5 %fusion.1 = bf16[2,2,2,32,2048]{4,3,0,1,2:T(8,128)(2,1)} fusion(bf16[2,2,2,32,2048]{4,3,0,1,2:T(8,128)(2,1)} %collective-permute-done, bf16[2,2,2,1,32,2048]{5,4,3,2,1,0:T(8,128)(2,1)S(1)} %copy-done.4), kind=kLoop, calls=%fused_computation.5 | loop fusion | flops 2097152 | bytes 3145728 | tf_op jit(solution)/shard_map/convert_element_type | solution.py:170
  74.6 2.8 %all-to-all-done.1.grad_ref = bf16[16,32,128]{2,1,0:T(8,128)(2,1)S(1)} async-done(((bf16[16,32,128]{2,1,0:T(8,128)(2,1)}), bf16[16,32,128]{2,1,0:T(8,128)(2,1)S(1)}, u32[]{:S(2)}, u32[]{:S(2)}) %all-to-all-start.1) | async-done | bytes 131104 | tf_op jit(solution)/shard_map/all_to_all | solution.py:153
  77.4 1.9 %dynamic-slice_bitcast_fusion.4 = bf16[2,2,32,1536]{3,2,1,0:T(8,128)(2,1)} fusion(bf16[2,2,2,32,1536]{4,3,2,1,0:T(8,128)(2,1)} %fusion.3, s32[]{:T(128)S(6)} %select_n.133), kind=kLoop, calls=%fused_computation.51 | loop fusion | bytes 786436 | tf_op jit(solution)/shard_map/jit(dynamic_index_in_dim)/squeeze | solution.py:166
  79.3 1.9 %dynamic-slice_bitcast_fusion.2 = bf16[2,2,32,2048]{3,2,0,1:T(8,128)(2,1)} fusion(bf16[2,2,2,32,2048]{4,3,0,1,2:T(8,128)(2,1)} %fusion.1, s32[]{:T(128)S(6)} %select_n.129), kind=kLoop, calls=%fused_computation.38 | loop fusion | bytes 1048580 | tf_op jit(solution)/shard_map/jit(dynamic_index_in_dim)/squeeze | solution.py:166
  81.2 0.5 collective-permute-start.2
  81.7 1.0 fusion.6
  82.8 11.8 %shard_map.164 = (bf16[16,32,128]{2,1,0:T(8,128)(2,1)S(1)}, bf16[16,64,128]{2,1,0:T(8,128)(2,1)S(1)}, f32[64,32]{1,0:T(8,128)S(1)}) custom-call(s32[16,5]{1,0:T(8,128)S(1)} %bitcast.130, bf16[16,96,128]{2,1,0:T(8,128)(2,1)S(1)} %get-tuple-element.19.qkv_ref, bf16[2,32,32]{2,1,0:T(8,128)(2,1)S(1)} %convolution_convert_fusion.6.virt_ref, ...), custom_call_target="tpu_custom_call" | custom-call | flops 356515840 | bytes 1179648 | tf_op jit(solution)/shard_map/pallas_call | solution.py:135
  94.7 1.2 fusion.12
  95.9 2.2 %fusion.8 = bf16[2,2,32,2048]{3,2,0,1:T(8,128)(2,1)} fusion(bf16[2,2,32,2048]{3,2,0,1:T(8,128)(2,1)} %collective-permute-done.2, bf16[2,2,2,32,2048]{4,3,0,1,2:T(8,128)(2,1)} %fusion.1, s32[]{:T(128)S(6)} %select_n.128), kind=kLoop, calls=%fused_computation.25 | loop fusion | flops 1048576 | bytes 1572868 | tf_op jit(solution)/shard_map/convert_element_type | solution.py:170
  98.1 0.8 pad_maximum_fusion.2
  98.9 4.6 %all-to-all-start.2 = ((bf16[16,112,128]{2,1,0:T(8,128)(2,1)}), bf16[16,112,128]{2,1,0:T(8,128)(2,1)}, u32[]{:S(2)}, u32[]{:S(2)}) async-start(bf16[16,112,128]{2,1,0:T(8,128)(2,1)} %pad_maximum_fusion.2), calls=%async_computation.2 | async-start | bytes 917504 | tf_op jit(solution)/shard_map/all_to_all | solution.py:153
  103.5 2.8 %collective-permute-start.8 = (bf16[2,32,1536]{2,1,0:T(8,128)(2,1)S(1)}, bf16[2,32,1536]{2,1,0:T(8,128)(2,1)S(1)}, u32[]{:S(2)}, u32[]{:S(2)}) collective-permute-start(bf16[2,32,1536]{2,1,0:T(8,128)(2,1)S(1)} %dynamic-slice_bitcast_fusion.7), channel_id=1, source_target_pairs={{0,8},{1,9},{2,10},{3,11},{4,12},{5,13},{6,14},{7,15},{8,0},{9,1},... | collective-permute-start | bytes 589832 | tf_op jit(solution)/shard_map/ppermute | solution.py:167
  106.3 1.0 dynamic-slice_bitcast_fusion.5
  107.3 1.5 collective-permute-start.10
  108.8 16.9 %collective-permute-done.8 = bf16[2,32,1536]{2,1,0:T(8,128)(2,1)S(1)} collective-permute-done((bf16[2,32,1536]{2,1,0:T(8,128)(2,1)S(1)}, bf16[2,32,1536]{2,1,0:T(8,128)(2,1)S(1)}, u32[]{:S(2)}, u32[]{:S(2)}) %collective-permute-start.8) | collective-permute-done | bytes 196640 | tf_op jit(solution)/shard_map/ppermute | solution.py:167
  125.8 0.7 dynamic-slice_bitcast_fusion.10
  126.4 1.5 collective-permute-start.9
  127.9 0.8 fusion.13
  128.7 1.2 fusion.64
  130.3 0.6 fusion.67
  130.9 1.8 %convolution_convert_fusion.1 = bf16[512,1536]{1,0:T(8,128)(2,1)} fusion(bf16[1536,128]{1,0:T(8,128)(2,1)S(1)} %bitcast.135, bf16[128,512]{1,0:T(8,128)(2,1)S(1)} %copy-done.5, f32[512]{0:T(512)S(1)} %copy-done.18, f32[128]{0:T(128)S(1)} %add_rsqrt_fusion.2), kind=kOutput, calls=%fused_computation.1 | convolution fusion | flops 202375168 | bytes 2099712 | tf_op jit(solution)/shard_map/rd,cr->dc/dot_general | solution.py:450
  132.7 0.8 slice.87
  134.5 1.8 %multiply_reduce_fusion.3 = (f32[32]{0:T(128)S(1)}, f32[32,512]{1,0:T(8,128)S(1)}) fusion(f32[32]{0:T(128)S(1)} %add_rsqrt_fusion.1, f32[32,512]{1,0:T(8,128)} %copy-done.13, f32[32]{0:T(128)S(1)} %div.82, bf16[1024,32]{0,1:T(8,128)(2,1)S(1)} %reshape.208, bf16[512,1536]{1,0:T(8,128)(2,1)} %param.14), kind=kOutput, calls=%fused_computation.100 | convolution fusion | flops 33619936 | bytes 1245568 | tf_op jit(solution)/shard_map/sp,ds->pd/dot_general | solution.py:435
  136.3 2.8 %copy_dynamic-update-slice_fusion = bf16[2,2,2,2,32,1664]{5,4,0,1,2,3:T(8,128)(2,1)} fusion(bf16[2,2,2,2,32,1536]{5,4,3,2,1,0:T(8,128)(2,1)} %bitcast.132), kind=kLoop, calls=%fused_computation.11 | loop fusion | bytes 3145728
  139.7 0.7 copy_dynamic-update-slice_fusion.1
  140.4 1.3 dynamic-slice_bitcast_fusion
  141.9 0.9 convert_add_fusion.11
  142.9 0.6 fusion.65
  143.5 0.7 pad_maximum_fusion.7
  144.5 0.6 collective-permute-start.5
  145.1 5.2 %collective-permute-done.11 = bf16[32,2048]{1,0:T(8,128)(2,1)S(1)} collective-permute-done((bf16[32,2048]{1,0:T(8,128)(2,1)S(1)}, bf16[32,2048]{1,0:T(8,128)(2,1)S(1)}, u32[]{:S(2)}, u32[]{:S(2)}) %collective-permute-start.11) | collective-permute-done | bytes 131104 | tf_op jit(solution)/shard_map/ppermute | solution.py:167
  150.3 0.7 convert_add_fusion.9
  151.1 5.7 %collective-permute-done.5 = bf16[2,2,32,1664]{3,2,0,1:T(8,128)(2,1)S(1)} collective-permute-done((bf16[2,2,32,1664]{3,2,0,1:T(8,128)(2,1)S(1)}, bf16[2,2,32,1664]{3,2,0,1:T(8,128)(2,1)S(1)}, u32[]{:S(2)}, u32[]{:S(2)}) %collective-permute-start.5) | collective-permute-done | bytes 426016 | tf_op jit(solution)/shard_map/ppermute | solution.py:167
  156.9 1.8 %collective-permute-start.6 = (bf16[2,32,1664]{2,1,0:T(8,128)(2,1)S(1)}, bf16[2,32,1664]{2,1,0:T(8,128)(2,1)S(1)}, u32[]{:S(2)}, u32[]{:S(2)}) collective-permute-start(bf16[2,32,1664]{2,1,0:T(8,128)(2,1)S(1)} %dynamic-slice_bitcast_fusion.6), channel_id=1, source_target_pairs={{0,4},{1,5},{2,6},{3,7},{4,0},{5,1},{6,2},{7,3},{8,12},{9,13},{10,... | collective-permute-start | bytes 638984 | tf_op jit(solution)/shard_map/ppermute | solution.py:167
  158.7 5.1 %collective-permute-done.6 = bf16[2,32,1664]{2,1,0:T(8,128)(2,1)S(1)} collective-permute-done((bf16[2,32,1664]{2,1,0:T(8,128)(2,1)S(1)}, bf16[2,32,1664]{2,1,0:T(8,128)(2,1)S(1)}, u32[]{:S(2)}, u32[]{:S(2)}) %collective-permute-start.6) | collective-permute-done | bytes 213024 | tf_op jit(solution)/shard_map/ppermute | solution.py:167
  163.9 2.4 %collective-permute-start.7 = (bf16[32,1664]{1,0:T(8,128)(2,1)S(1)}, bf16[32,1664]{1,0:T(8,128)(2,1)S(1)}, u32[]{:S(2)}, u32[]{:S(2)}) collective-permute-start(bf16[32,1664]{1,0:T(8,128)(2,1)S(1)} %dynamic-slice_bitcast_fusion.9), channel_id=1, source_target_pairs={{0,8},{1,9},{2,10},{3,11},{4,12},{5,13},{6,14},{7,15},{8,0},{9,1},... | collective-permute-start | bytes 319496 | tf_op jit(solution)/shard_map/ppermute | solution.py:167
  166.2 0.8 fusion.27
  167.0 3.7 %collective-permute-done.7 = bf16[32,1664]{1,0:T(8,128)(2,1)S(1)} collective-permute-done((bf16[32,1664]{1,0:T(8,128)(2,1)S(1)}, bf16[32,1664]{1,0:T(8,128)(2,1)S(1)}, u32[]{:S(2)}, u32[]{:S(2)}) %collective-permute-start.7) | collective-permute-done | bytes 106528 | tf_op jit(solution)/shard_map/ppermute | solution.py:167
  170.8 0.5 slice_bitcast_fusion
  171.6 0.7 pad_maximum_fusion.6
  (108 shorter events, 5.7 us)
Async XLA Ops:
  0.6 54.8 %copy-start = (bf16[512,2048]{1,0:T(8,128)(2,1)S(1)}, bf16[512,2048]{1,0:T(8,128)(2,1)}, u32[]{:S(2)}) copy-start(bf16[512,2048]{1,0:T(8,128)(2,1)} %param.16) | copy-start | bytes 6291460
  5.7 3.6 %copy-start.19 = (s32[1,4]{1,0:T(1,128)S(1)}, s32[1,4]{1,0:T(1,128)}, u32[]{:S(2)}) copy-start(s32[1,4]{1,0:T(1,128)} %param.18) | copy-start | bytes 52
  32.3 8.2 %copy-start.13 = (f32[32,512]{1,0:T(8,128)}, f32[32,512]{1,0:T(8,128)S(1)}, u32[]{:S(2)}) copy-start(f32[32,512]{1,0:T(8,128)S(1)} %reshape.202) | copy-start | bytes 196612
  33.5 20.5 %copy-start.5 = (bf16[128,512]{1,0:T(8,128)(2,1)S(1)}, bf16[128,512]{1,0:T(8,128)(2,1)}, u32[]{:S(2)}) copy-start(bf16[128,512]{1,0:T(8,128)(2,1)} %param.11) | copy-start | bytes 393220
  33.5 21.9 %copy-start.17 = (f32[512]{0:T(512)S(1)}, f32[512]{0:T(512)}, u32[]{:S(2)}) copy-start(f32[512]{0:T(512)} %param.13) | copy-start | bytes 6148
  40.5 13.5 %all-to-all-start = ((bf16[16,32,128]{2,1,0:T(8,128)(2,1)}), bf16[16,32,128]{2,1,0:T(8,128)(2,1)S(1)}, u32[]{:S(2)}, u32[]{:S(2)}) async-start(bf16[16,32,128]{2,1,0:T(8,128)(2,1)} %shard_map.163), calls=%async_computation | async-start | bytes 262144 | tf_op jit(solution)/shard_map/all_to_all | solution.py:153
  55.4 1.2 copy-start.8
  55.4 1.2 copy-start.12
  57.2 1.8 %copy-start.10 = (bf16[128,1024]{1,0:T(8,128)(2,1)}, bf16[128,1024]{1,0:T(8,128)(2,1)S(1)}, u32[]{:S(2)}) copy-start(bf16[128,1024]{1,0:T(8,128)(2,1)S(1)} %get-tuple-element.39) | copy-start | bytes 786436
  60.1 2.2 %copy-start.3 = (bf16[2,2,2,2,32,1536]{5,4,3,2,1,0:T(8,128)(2,1)}, bf16[2,2,2,2,32,1536]{5,4,3,2,1,0:T(8,128)(2,1)S(1)}, u32[]{:S(2)}) copy-start(bf16[2,2,2,2,32,1536]{5,4,3,2,1,0:T(8,128)(2,1)S(1)} %pad_maximum_fusion) | copy-start | bytes 4718596
  61.2 8.3 %collective-permute-start.1 = (bf16[2,2,2,32,1536]{4,3,2,1,0:T(8,128)(2,1)}, bf16[2,2,2,32,1536]{4,3,2,1,0:T(8,128)(2,1)}, u32[]{:S(2)}, u32[]{:S(2)}) collective-permute-start(bf16[2,2,2,32,1536]{4,3,2,1,0:T(8,128)(2,1)} %dynamic-slice_bitcast_fusion.1), channel_id=1, source_target_pairs={{0,1},{1,0},{2,3},{3,2},{4,5},{5,4},{6,7},{7,6},{8,9},{9,8},{10,11... | collective-permute-start | bytes 2359304 | tf_op jit(solution)/shard_map/ppermute | solution.py:167
  63.4 8.7 %collective-permute-start = (bf16[2,2,2,32,2048]{4,3,0,1,2:T(8,128)(2,1)}, bf16[2,2,2,32,2048]{4,3,0,1,2:T(8,128)(2,1)}, u32[]{:S(2)}, u32[]{:S(2)}) collective-permute-start(bf16[2,2,2,32,2048]{4,3,0,1,2:T(8,128)(2,1)} %bitcast.126), channel_id=1, source_target_pairs={{0,1},{1,0},{2,3},{3,2},{4,5},{5,4},{6,7},{7,6},{8,9},{9,8},{10,11... | collective-permute-start | bytes 3145736 | tf_op jit(solution)/shard_map/ppermute | solution.py:167
  66.0 11.4 %all-to-all-start.1 = ((bf16[16,32,128]{2,1,0:T(8,128)(2,1)}), bf16[16,32,128]{2,1,0:T(8,128)(2,1)S(1)}, u32[]{:S(2)}, u32[]{:S(2)}) async-start(bf16[16,32,128]{2,1,0:T(8,128)(2,1)} %bitcast.15), calls=%async_computation.1 | async-start | bytes 262144 | tf_op jit(solution)/shard_map/all_to_all | solution.py:153
  69.5 2.6 %copy-start.4 = (bf16[2,2,2,1,32,2048]{5,4,3,2,1,0:T(8,128)(2,1)S(1)}, bf16[2,2,2,1,32,2048]{5,4,3,2,1,0:T(8,128)(2,1)}, u32[]{:S(2)}) copy-start(bf16[2,2,2,1,32,2048]{5,4,3,2,1,0:T(8,128)(2,1)} %get-tuple-element.33) | copy-start | bytes 3145732
  77.4 4.3 %copy-start.9 = (bf16[1024,512]{1,0:T(8,128)(2,1)S(1)}, bf16[1024,512]{1,0:T(8,128)(2,1)}, u32[]{:S(2)}) copy-start(bf16[1024,512]{1,0:T(8,128)(2,1)} %param.17) | copy-start | bytes 3145732
  77.4 4.3 %copy-start.11 = (bf16[128,1024]{1,0:T(8,128)(2,1)S(1)}, bf16[128,1024]{1,0:T(8,128)(2,1)}, u32[]{:S(2)}) copy-start(bf16[128,1024]{1,0:T(8,128)(2,1)} %copy-done.10) | copy-start | bytes 786436
  79.3 15.4 %collective-permute-start.3 = (bf16[2,2,32,1536]{3,2,1,0:T(8,128)(2,1)}, bf16[2,2,32,1536]{3,2,1,0:T(8,128)(2,1)}, u32[]{:S(2)}, u32[]{:S(2)}) collective-permute-start(bf16[2,2,32,1536]{3,2,1,0:T(8,128)(2,1)} %dynamic-slice_bitcast_fusion.4), channel_id=1, source_target_pairs={{0,4},{1,5},{2,6},{3,7},{4,0},{5,1},{6,2},{7,3},{8,12},{9,13},{10,... | collective-permute-start | bytes 1179656 | tf_op jit(solution)/shard_map/ppermute | solution.py:167
  81.2 14.7 %collective-permute-start.2 = (bf16[2,2,32,2048]{3,2,0,1:T(8,128)(2,1)}, bf16[2,2,32,2048]{3,2,0,1:T(8,128)(2,1)}, u32[]{:S(2)}, u32[]{:S(2)}) collective-permute-start(bf16[2,2,32,2048]{3,2,0,1:T(8,128)(2,1)} %dynamic-slice_bitcast_fusion.2), channel_id=1, source_target_pairs={{0,2},{1,3},{2,0},{3,1},{4,6},{5,7},{6,4},{7,5},{8,10},{9,11},{10,... | collective-permute-start | bytes 1572872 | tf_op jit(solution)/shard_map/ppermute | solution.py:167
  98.9 29.0 %copy-start.6 = (bf16[2,2,32,2048]{3,2,0,1:T(8,128)(2,1)S(1)}, bf16[2,2,32,2048]{3,2,0,1:T(8,128)(2,1)}, u32[]{:S(2)}) copy-start(bf16[2,2,32,2048]{3,2,0,1:T(8,128)(2,1)} %fusion.8) | copy-start | bytes 1572868
  98.9 29.8 %all-to-all-start.2 = ((bf16[16,112,128]{2,1,0:T(8,128)(2,1)}), bf16[16,112,128]{2,1,0:T(8,128)(2,1)}, u32[]{:S(2)}, u32[]{:S(2)}) async-start(bf16[16,112,128]{2,1,0:T(8,128)(2,1)} %pad_maximum_fusion.2), calls=%async_computation.2 | async-start | bytes 917504 | tf_op jit(solution)/shard_map/all_to_all | solution.py:153
  103.5 22.2 %collective-permute-start.8 = (bf16[2,32,1536]{2,1,0:T(8,128)(2,1)S(1)}, bf16[2,32,1536]{2,1,0:T(8,128)(2,1)S(1)}, u32[]{:S(2)}, u32[]{:S(2)}) collective-permute-start(bf16[2,32,1536]{2,1,0:T(8,128)(2,1)S(1)} %dynamic-slice_bitcast_fusion.7), channel_id=1, source_target_pairs={{0,8},{1,9},{2,10},{3,11},{4,12},{5,13},{6,14},{7,15},{8,0},{9,1},... | collective-permute-start | bytes 589832 | tf_op jit(solution)/shard_map/ppermute | solution.py:167
  107.3 20.6 %collective-permute-start.10 = (bf16[2,32,2048]{2,1,0:T(8,128)(2,1)S(1)}, bf16[2,32,2048]{2,1,0:T(8,128)(2,1)S(1)}, u32[]{:S(2)}, u32[]{:S(2)}) collective-permute-start(bf16[2,32,2048]{2,1,0:T(8,128)(2,1)S(1)} %dynamic-slice_bitcast_fusion.5), channel_id=1, source_target_pairs={{0,4},{1,5},{2,6},{3,7},{4,0},{5,1},{6,2},{7,3},{8,12},{9,13},{10,... | collective-permute-start | bytes 786440 | tf_op jit(solution)/shard_map/ppermute | solution.py:167
  126.4 15.5 %collective-permute-start.9 = (bf16[32,1536]{1,0:T(8,128)(2,1)}, bf16[32,1536]{1,0:T(8,128)(2,1)}, u32[]{:S(2)}, u32[]{:S(2)}) collective-permute-start(bf16[32,1536]{1,0:T(8,128)(2,1)} %dynamic-slice_bitcast_fusion.10), channel_id=1, source_target_pairs={{0,2},{1,3},{2,0},{3,1},{4,6},{5,7},{6,4},{7,5},{8,10},{9,11},{10,... | collective-permute-start | bytes 294920 | tf_op jit(solution)/shard_map/ppermute | solution.py:167
  128.7 1.6 copy-start.1
  129.8 1.1 copy-start.18
  134.5 1.8 %copy-start.15 = (bf16[1024,32]{0,1:T(8,128)(2,1)}, bf16[1024,32]{0,1:T(8,128)(2,1)S(1)}, u32[]{:S(2)}) copy-start(bf16[1024,32]{0,1:T(8,128)(2,1)S(1)} %reshape.208) | copy-start | bytes 196612
  136.3 2.8 %copy-start.14 = (f32[32,512]{1,0:T(8,128)S(1)}, f32[32,512]{1,0:T(8,128)}, u32[]{:S(2)}) copy-start(f32[32,512]{1,0:T(8,128)} %copy-done.13) | copy-start | bytes 196612
  136.3 2.8 %copy-start.20 = (s32[128]{0:T(128)S(1)}, s32[128]{0:T(128)}, u32[]{:S(2)}) copy-start(s32[128]{0:T(128)} %param.20) | copy-start | bytes 1540
  139.1 2.7 %copy-start.7 = (bf16[2,32,2048]{2,1,0:T(8,128)(2,1)S(1)}, bf16[2,32,2048]{2,1,0:T(8,128)(2,1)}, u32[]{:S(2)}) copy-start(bf16[2,32,2048]{2,1,0:T(8,128)(2,1)} %fusion.13) | copy-start | bytes 786436
  140.4 3.8 %copy-start.2 = (bf16[2,2,2,2,32,1664]{5,4,0,1,2,3:T(8,128)(2,1)S(1)}, bf16[2,2,2,2,32,1664]{5,4,0,1,2,3:T(8,128)(2,1)}, u32[]{:S(2)}) copy-start(bf16[2,2,2,2,32,1664]{5,4,0,1,2,3:T(8,128)(2,1)} %copy_dynamic-update-slice_fusion.1) | copy-start | bytes 5111812
  141.7 2.4 %collective-permute-start.4 = (bf16[2,2,2,32,1664]{4,3,0,1,2:T(8,128)(2,1)S(1)}, bf16[2,2,2,32,1664]{4,3,0,1,2:T(8,128)(2,1)S(1)}, u32[]{:S(2)}, u32[]{:S(2)}) collective-permute-start(bf16[2,2,2,32,1664]{4,3,0,1,2:T(8,128)(2,1)S(1)} %dynamic-slice_bitcast_fusion), channel_id=1, source_target_pairs={{0,1},{1,0},{2,3},{3,2},{4,5},{5,4},{6,7},{7,6},{8,9},{9,8},{10,11... | collective-permute-start | bytes 2555912 | tf_op jit(solution)/shard_map/ppermute | solution.py:167
  141.9 8.5 %collective-permute-start.11 = (bf16[32,2048]{1,0:T(8,128)(2,1)S(1)}, bf16[32,2048]{1,0:T(8,128)(2,1)S(1)}, u32[]{:S(2)}, u32[]{:S(2)}) collective-permute-start(bf16[32,2048]{1,0:T(8,128)(2,1)S(1)} %dynamic-slice_bitcast_fusion.8), channel_id=1, source_target_pairs={{0,8},{1,9},{2,10},{3,11},{4,12},{5,13},{6,14},{7,15},{8,0},{9,1},... | collective-permute-start | bytes 393224 | tf_op jit(solution)/shard_map/ppermute | solution.py:167
  144.5 12.3 %collective-permute-start.5 = (bf16[2,2,32,1664]{3,2,0,1:T(8,128)(2,1)S(1)}, bf16[2,2,32,1664]{3,2,0,1:T(8,128)(2,1)S(1)}, u32[]{:S(2)}, u32[]{:S(2)}) collective-permute-start(bf16[2,2,32,1664]{3,2,0,1:T(8,128)(2,1)S(1)} %dynamic-slice_bitcast_fusion.3), channel_id=1, source_target_pairs={{0,2},{1,3},{2,0},{3,1},{4,6},{5,7},{6,4},{7,5},{8,10},{9,11},{10,... | collective-permute-start | bytes 1277960 | tf_op jit(solution)/shard_map/ppermute | solution.py:167
  151.1 20.3 %copy-start.16 = (bf16[1024,32]{0,1:T(8,128)(2,1)S(1)}, bf16[1024,32]{0,1:T(8,128)(2,1)}, u32[]{:S(2)}) copy-start(bf16[1024,32]{0,1:T(8,128)(2,1)} %copy-done.15) | copy-start | bytes 196612
  156.9 6.9 %collective-permute-start.6 = (bf16[2,32,1664]{2,1,0:T(8,128)(2,1)S(1)}, bf16[2,32,1664]{2,1,0:T(8,128)(2,1)S(1)}, u32[]{:S(2)}, u32[]{:S(2)}) collective-permute-start(bf16[2,32,1664]{2,1,0:T(8,128)(2,1)S(1)} %dynamic-slice_bitcast_fusion.6), channel_id=1, source_target_pairs={{0,4},{1,5},{2,6},{3,7},{4,0},{5,1},{6,2},{7,3},{8,12},{9,13},{10,... | collective-permute-start | bytes 638984 | tf_op jit(solution)/shard_map/ppermute | solution.py:167
  163.9 6.9 %collective-permute-start.7 = (bf16[32,1664]{1,0:T(8,128)(2,1)S(1)}, bf16[32,1664]{1,0:T(8,128)(2,1)S(1)}, u32[]{:S(2)}, u32[]{:S(2)}) collective-permute-start(bf16[32,1664]{1,0:T(8,128)(2,1)S(1)} %dynamic-slice_bitcast_fusion.9), channel_id=1, source_target_pairs={{0,8},{1,9},{2,10},{3,11},{4,12},{5,13},{6,14},{7,15},{8,0},{9,1},... | collective-permute-start | bytes 319496 | tf_op jit(solution)/shard_map/ppermute | solution.py:167

commit v4 on v3

--- a/solution.py
+++ b/solution.py
@@ -57,17 +57,84 @@
     return query, tanhs, [w * inverse for w in weights]
 
 
-def forward_kernel(head_dim, lists_ref, qkv_ref, virt_ref, out_ref):
-    def body(t, carry):
+def forward_kernel(
+    head_dim, slices, size, lists_ref, qkv_ref, virt_ref, heads_ref, out_ref, send, recv
+):
+    me = lax.axis_index("seq")
+    tiles_here = size // slices
+    my_head = me // slices
+    my_slice = me % slices
+    from_slice = me // tiles_here
+
+    def copy(t, head, to):
+        return pltpu.make_async_remote_copy(
+            src_ref=out_ref.at[t],
+            dst_ref=heads_ref.at[head],
+            send_sem=send.at[t],
+            recv_sem=recv.at[head],
+            device_id={"seq": to},
+            device_id_type=pl.DeviceIdType.MESH,
+        )
+
+    def tile_rows(t):
         _, _, probs = tile_weights(lists_ref, qkv_ref, virt_ref, t, head_dim)
         out = dot_nn(virt_ref[1], probs[KT].astype(jnp.bfloat16))
         for j in range(KT):
             values = qkv_ref[lists_ref[t, j], 2 * head_dim : 3 * head_dim, :]
             out = out + dot_nn(values, probs[j].astype(jnp.bfloat16))
-        out_ref[t] = out.astype(jnp.bfloat16)
+        return out.astype(jnp.bfloat16)
+
+    barrier = pltpu.get_barrier_semaphore()
+
+    def greet(k, carry):
+        pl.semaphore_signal(
+            barrier,
+            inc=1,
+            device_id={"seq": lax.rem(me + k, size)},
+            device_id_type=pl.DeviceIdType.MESH,
+        )
         return carry
 
-    lax.fori_loop(0, out_ref.shape[0], body, 0, unroll=2)
+    lax.fori_loop(1, size, greet, 0)
+    pl.semaphore_wait(barrier, size - 1)
+
+    def body(k, carry):
+        pair = [lax.rem(me + 2 * k + 1 + u, tiles_here) for u in range(2)]
+        rows = [tile_rows(t) for t in pair]
+        for t, values in zip(pair, rows):
+            out_ref[t] = values
+        for t in pair:
+            to = my_slice * tiles_here + t
+
+            @pl.when(to != me)
+            def _():
+                copy(t, my_head, to).start()
+
+            @pl.when(to == me)
+            def _():
+                heads_ref[my_head] = out_ref[t]
+
+        return carry
+
+    lax.fori_loop(0, tiles_here // 2, body, 0)
+
+    def arrive(head, carry):
+        @pl.when(head * slices + from_slice != me)
+        def _():
+            copy(0, head, me).wait_recv()
+
+        return carry
+
+    lax.fori_loop(0, HEADS, arrive, 0)
+
+    def leave(t, carry):
+        @pl.when(my_slice * tiles_here + t != me)
+        def _():
+            copy(t, my_head, me).wait_send()
+
+        return carry
+
+    lax.fori_loop(0, tiles_here, leave, 0)
 
 
 def backward_kernel(
@@ -109,17 +176,24 @@
     dkv_ref[...] = acc_ref[...].astype(jnp.bfloat16)
 
 
-def attention_forward(lists, qkv_all, virt, head_dim):
+def attention_forward(lists, qkv_all, virt, head_dim, slices):
     tiles_here = lists.shape[0]
-    rows = qkv_all.shape[2]
+    size, _, rows = qkv_all.shape
     pairs = tiles_here * rows * (KT * rows + virt.shape[2])
     vmem = pl.BlockSpec(memory_space=pltpu.VMEM)
     return pl.pallas_call(
-        functools.partial(forward_kernel, head_dim),
-        out_shape=jax.ShapeDtypeStruct((tiles_here, head_dim, rows), jnp.bfloat16),
+        functools.partial(forward_kernel, head_dim, slices, size),
+        out_shape=jax.ShapeDtypeStruct((HEADS, head_dim, rows), jnp.bfloat16),
         in_specs=[pl.BlockSpec(memory_space=pltpu.SMEM), vmem, vmem],
         out_specs=vmem,
-        compiler_params=pltpu.CompilerParams(vmem_limit_bytes=VMEM_BYTES),
+        scratch_shapes=[
+            pltpu.VMEM((tiles_here, head_dim, rows), jnp.bfloat16),
+            pltpu.SemaphoreType.DMA((tiles_here,)),
+            pltpu.SemaphoreType.DMA((HEADS,)),
+        ],
+        compiler_params=pltpu.CompilerParams(
+            vmem_limit_bytes=VMEM_BYTES, collective_id=1, has_side_effects=True
+        ),
         cost_estimate=pl.CostEstimate(
             flops=4 * pairs * head_dim, bytes_accessed=2 * qkv_all.size, transcendentals=2 * pairs
         ),
@@ -158,23 +232,18 @@
     return blocks.reshape((2,) * bits + blocks.shape[1:]), list(range(bits - 1, -1, -1))
 
 
-def halve(held, left, bit, last=False):
+def halve(held, left, bit, after=None):
     size = lax.axis_size("seq")
     mine = (lax.axis_index("seq") // (1 << bit)) % 2
     axis = left.index(bit)
     keep = lax.dynamic_index_in_dim(held, mine, axis, keepdims=False)
     send = lax.dynamic_index_in_dim(held, 1 - mine, axis, keepdims=False)
     got = lax.ppermute(send, "seq", [(i, i ^ (1 << bit)) for i in range(size)])
+    if after is not None:
+        got, _ = lax.optimization_barrier((got, after))
     total = keep.astype(jnp.float32) + got.astype(jnp.float32)
     rest = [b for b in left if b != bit]
     return (total if not rest else total.astype(jnp.bfloat16)), rest
-
-
-def reduce_in_order(blocks, order):
-    held, left = as_bits(blocks)
-    for bit in order:
-        held, left = halve(held, left, bit)
-    return held
 
 
 def exchange_kernel(
@@ -224,7 +293,9 @@
     each(lambda k, to: first_copy(k, to).start())
     each(lambda k, to: head_copy(k, to).start())
     each(lambda k, to: first_copy(k, to).wait_recv())
-    own_ref[...] = list_ref[...] + jnp.sum(first_ref[...], axis=0)
+    own_ref[...] = (
+        list_ref[...] + jnp.sum(first_ref[...].astype(jnp.float32), axis=0)
+    ).astype(own_ref.dtype)
     each(lambda k, to: second_copy(k, to).start())
     second_ref[me] = own_ref[...]
     each(lambda k, to: second_copy(k, to).wait_recv())
@@ -296,7 +367,7 @@
     lanes = 128
     sum_rows = VN_DEV * width // lanes
     list_at = sum_rows + VN_DEV
-    block_rows = -(-(list_at + 1) // 8) * 8
+    block_rows = -(-(list_at + 1) // 16) * 16
     sums = jnp.concatenate(
         [
             part_sums.reshape(seq_size, sum_rows, lanes),
@@ -306,18 +377,18 @@
             jnp.zeros((seq_size, block_rows - list_at, lanes), jnp.float32),
         ],
         axis=1,
-    )
+    ).astype(jnp.bfloat16)
     list_rows = jnp.pad(
         jnp.concatenate([tile_lists[0], tile_count]).astype(jnp.float32)[None],
         ((list_at, block_rows - list_at - 1), (0, lanes - KT - 1)),
     )
-    qkv_t = jnp.einsum(
-        "dc,rd->cr", query_key_value_weight, normed, preferred_element_type=jnp.float32
-    ).astype(jnp.bfloat16)
+    qkv = jnp.dot(normed, query_key_value_weight, preferred_element_type=jnp.float32)
+    qkv_t = lax.optimization_barrier(qkv.astype(jnp.bfloat16)).T
     qkv_heads = jnp.transpose(qkv_t.reshape(3, HEADS, head_dim, rows), (1, 0, 2, 3)).reshape(
         HEADS, 3 * head_dim, rows
     )
     qkv_all, second = exchange(sums, list_rows, qkv_heads, slices)
+    second = second.astype(jnp.float32)
     totals = second[:, :sum_rows].reshape(parts, width)
     counts = second[:, sum_rows:list_at, :1].reshape(parts, 1)
     lists_all = second[:, list_at, : KT + 1].astype(jnp.int32)
@@ -342,8 +413,7 @@
         split = received.reshape((HEADS, slices) + received.shape[1:])
         return lax.dynamic_index_in_dim(split, slice_of_me, 1, keepdims=False)
 
-    out_heads = attention_forward(lists, qkv_all, virt, head_dim)
-    attn_out_t = pick_slice(all_to_all(spread(out_heads))).reshape(width, rows)
+    attn_out_t = attention_forward(lists, qkv_all, virt, head_dim, slices).reshape(width, rows)
 
     mixed = jnp.einsum("dr,de->re", attn_out_t, w_out, preferred_element_type=jnp.float32)
     resid = (x_f + mixed).astype(jnp.bfloat16)
@@ -398,13 +468,11 @@
     grads, one, two = lax.optimization_barrier((grads, one, two))
     one, one_left = halve(one, one_left, 1)
     two, two_left = halve(two, two_left, outer[0])
+    one_order = outer
+    two_order = outer[1:] + [1]
 
     dq, dkv, dvirt = attention_backward(lists, qkv_all, virt, grads, head_dim)
     dq, one, two = lax.optimization_barrier((dq, one, two))
-    for bit in outer:
-        one, one_left = halve(one, one_left, bit)
-    for bit in outer[1:] + [1]:
-        two, two_left = halve(two, two_left, bit)
     virt_rows = 2 * head_dim * parts // rows
     back_send = jnp.concatenate(
         [
@@ -437,6 +505,21 @@
     )
     inner_vn = jnp.mean(d_virtual * unit_vn, axis=-1, keepdims=True)
     per_part = inv_vn * (d_virtual - unit_vn * inner_vn) / counts
+    grad_qkv_local = jnp.einsum("rd,cr->dc", normed, d_qkv_t, preferred_element_type=jnp.float32)
+    late = grad_qkv_local.astype(jnp.bfloat16).reshape(seq_size, share, -1)
+    for step, bit in enumerate(one_order):
+        one, one_left = halve(one, one_left, bit, late if step == 0 else None)
+    for step, bit in enumerate(two_order):
+        two, two_left = halve(two, two_left, bit, late if step == 0 else None)
+    late, late_left = as_bits(late)
+    late, late_left = halve(late, late_left, 0)
+    middle = late.shape[-1] // 2
+    late_one, late_two = late[..., :middle], late[..., middle:]
+    one_left, two_left = late_left, late_left
+    for one_bit, two_bit in zip([1] + outer, outer + [1]):
+        late_one, one_left = halve(late_one, one_left, one_bit)
+        late_two, two_left = halve(late_two, two_left, two_bit)
+    late_sum = jnp.concatenate([late_one, late_two], axis=1)
     d_normed = jnp.einsum(
         "cr,dc->rd", d_qkv_t, query_key_value_weight, preferred_element_type=jnp.float32
     )
@@ -447,19 +530,11 @@
         + inv_attn
         * (scaled_attn - unit_attn * jnp.mean(scaled_attn * unit_attn, axis=-1, keepdims=True))
     ).astype(jnp.bfloat16)
-    grad_qkv_local = jnp.einsum("rd,cr->dc", normed, d_qkv_t, preferred_element_type=jnp.float32)
     gain_local = jnp.concatenate(
         [jnp.sum(d_normed * unit_attn, axis=0), jnp.sum(d_normed_ffn * unit_ffn, axis=0)]
     )
     gain_share = 2 * width // seq_size
-    gain_block = jnp.pad(
-        gain_local.astype(jnp.bfloat16).reshape(seq_size, 1, gain_share),
-        ((0, 0), (0, share - 1), (0, 128 - gain_share)),
-    )
-    late = jnp.concatenate(
-        [grad_qkv_local.astype(jnp.bfloat16).reshape(seq_size, share, -1), gain_block], axis=2
-    )
-    late_sum = reduce_in_order(late, [0, 1] + outer)
+    grad_gains = jnp.sum(all_to_all(gain_local.reshape(seq_size, gain_share)), axis=0)
     grad_w_in = one
     grad_w_out = two[:, :width]
     grad_w_down = jnp.concatenate(
@@ -470,7 +545,6 @@
     grad_qkv = jnp.concatenate(
         [late_sum[:, :width], late_sum[:, width : 3 * width] + virtual_grad], axis=1
     )
-    grad_gains = late_sum[0, 3 * width : 3 * width + gain_share]
     return (layer_out, d_features, grad_qkv, grad_w_out, grad_w_in, grad_w_down, grad_gains)
 
 

time: 173 us -> 175 us (1.012)
  waiting for transfers between devices: 47.4 us -> 26.3 us
  other arithmetic: 17.1 us -> 24 us
  starting transfers between devices: 25.4 us -> 31.7 us
  matrix products: 16.2 us -> 20.2 us
  local copies, waits for them, and re-layouts: 23.5 us -> 26.3 us
  Pallas kernels: 40.8 us -> 43.5 us
    ppermute x12 -> x15, waiting for transfers between devices: 36.6 us -> 13.3 us  [halve(): got = lax.ppermute(send, 'seq', [(i, i ^ 1 << bit) for i in range(size)])]
    ppermute x12 -> x15, starting transfers between devices: 11.7 us -> 17.1 us  [halve(): got = lax.ppermute(send, 'seq', [(i, i ^ 1 << bit) for i in range(size)])]
    pallas_call x1, Pallas kernels: 6.99 us -> 11.9 us  [attention_forward(): pl.pallas_call(functools.partial(forward_kernel, head_dim, slices, size),...]
    dynamic_slice x1 -> x2, local copies, waits for them, and re-layouts: 1.12 us -> 4.2 us  [halve(): keep = lax.dynamic_index_in_dim(held, mine, axis, keepdims=False)]
    convert_element_type x9 -> x11, other arithmetic: 9.62 us -> 12 us  [halve(): return (total if not rest else total.astype(jnp.bfloat16), rest)]
    all_to_all x3, waiting for transfers between devices: 10.7 us -> 13 us  [all_to_all(): lax.all_to_all(blocks, 'seq', split_axis=0, concat_axis=0, tiled=True)]
    pallas_call x1, Pallas kernels: 22 us -> 19.8 us  [exchange(): pl.pallas_call(functools.partial(exchange_kernel, slices), out_shape=(jax...]
    unnamed x44 -> x61, local copies, waits for them, and re-layouts: 6.53 us -> 4.97 us
  transfers between devices with their start and end apart: 15 -> 18, of which waited for: 7 -> 8; matrix products, arithmetic and copies ran while one was open for 19% -> 26% of each run, Pallas kernels for 7% -> 7%
where the time goes in v4:
time: 175 us; the launch traced here: 174 us
  Pallas kernels  43.5 us (25%)
  starting transfers between devices  31.7 us (18%)
  local copies, waits for them, and re-layouts  26.3 us (15%)
  waiting for transfers between devices  26.3 us (15%)
  other arithmetic  24 us (14%)
  matrix products  20.2 us (12%)
  between operations  2.07 us (1%)
    pallas_call x1, Pallas kernels, exchange(): pl.pallas_call(functools.partial(exchange_kernel, slices), out_shape=(jax...  19.8 us
    ppermute x15, starting transfers between devices, halve(): got = lax.ppermute(send, 'seq', [(i, i ^ 1 << bit) for i in range(size)])  17.1 us
    all_to_all x3, starting transfers between devices, all_to_all(): lax.all_to_all(blocks, 'seq', split_axis=0, concat_axis=0, tiled=True)  14.6 us
    ppermute x15, waiting for transfers between devices, halve(): got = lax.ppermute(send, 'seq', [(i, i ^ 1 << bit) for i in range(size)])  13.3 us
    all_to_all x3, waiting for transfers between devices, all_to_all(): lax.all_to_all(blocks, 'seq', split_axis=0, concat_axis=0, tiled=True)  13 us
    convert_element_type x11, other arithmetic, halve(): return (total if not rest else total.astype(jnp.bfloat16), rest)  12 us
    pallas_call x1, Pallas kernels, attention_forward(): pl.pallas_call(functools.partial(forward_kernel, head_dim, slices, size),...  11.9 us
    pallas_call x1, Pallas kernels, attention_backward(): pl.pallas_call(functools.partial(backward_kernel, head_dim), out_shape=(j...  11.8 us
  transfers between devices with their start and end apart: 18, of which 8 were waited for; matrix products, arithmetic and copies ran while one was open for 26% of the time, Pallas kernels for 7%

profile of v4, /device:TPU:0, one launch (start us, length us, event | category | flops | bytes accessed | tf_op | source)
XLA Modules:
  0.0 174.1 jit_solution(1340715334235097490)
XLA Ops:
  0.6 0.9 fusion.43
  1.6 1.0 fusion.28
  2.6 1.1 convolution_convert_fusion.6
  3.7 1.9 %convolution_convert_fusion.2 = bf16[128,1536]{1,0:T(8,128)(2,1)S(1)} fusion(bf16[512,1536]{1,0:T(8,128)(2,1)} %param.14, bf16[128,512]{1,0:T(8,128)(2,1)} %param.11, f32[512]{0:T(512)} %param.12, f32[128]{0:T(128)S(1)} %add_rsqrt_fusion.2), kind=kOutput, calls=%fused_computation.2 | convolution fusion | flops 201785344 | bytes 2099712 | tf_op jit(solution)/shard_map/dot_general | solution.py:385
  5.7 2.6 %copy.82 = bf16[512,1536]{0,1:T(8,128)(2,1)} copy(bf16[512,1536]{1,0:T(8,128)(2,1)} %param.14) | data formatting | bytes 3145728 | tf_op args[3]
  9.7 19.8 %shard_map.162 = (bf16[16,96,128]{2,1,0:T(8,128)(2,1)S(1)}, bf16[16,16,128]{2,1,0:T(8,128)(2,1)S(1)}) custom-call(bf16[16,16,128]{2,1,0:T(8,128)(2,1)S(1)} %maximum_maximum_fusion.sums_ref, f32[16,128]{1,0:T(8,128)S(1)} %pad.4.list_ref, bf16[16,96,128]{2,1,0:T(8,128)(2,1)S(1)} %bitcast.144), custom_call_target="tpu_custom_call" | custom-call | flops 32768 | bytes 786432 | tf_op jit(solution)/shard_map/pallas_call | solution.py:311
  30.5 1.0 convolution_convert_fusion.7.virt_ref
  31.5 11.9 %shard_map.163 = bf16[16,32,128]{2,1,0:T(8,128)(2,1)S(1)} custom-call(s32[16,5]{1,0:T(8,128)S(1)} %bitcast.147, bf16[16,96,128]{2,1,0:T(8,128)(2,1)S(1)} %get-tuple-element.21.qkv_ref, bf16[2,32,32]{2,1,0:T(8,128)(2,1)S(1)} %convolution_convert_fusion.7.virt_ref), custom_call_target="tpu_custom_call" | custom-call | flops 142606336 | bytes 393216 | tf_op jit(solution)/shard_map/pallas_call | solution.py:184
  44.3 0.7 copy-done.14
  45.6 1.5 multiply_reduce_fusion
  47.6 1.1 fusion.59
  48.9 1.1 convolution_convert_fusion.4
  50.0 1.5 pad_maximum_fusion
  51.5 1.1 copy-done.2
  52.6 1.0 dynamic-slice_bitcast_fusion
  54.1 2.1 %convolution_convert_fusion = bf16[512,2048]{1,0:T(8,128)(2,1)} fusion(bf16[128,1024]{1,0:T(8,128)(2,1)S(1)} %copy-done.25, bf16[128,1024]{1,0:T(8,128)(2,1)S(1)} %copy-done.23, f32[128,512]{1,0:T(8,128)S(1)} %get-tuple-element.55, f32[512]{0:T(512)S(1)} %copy-done.26, f32[128]{0:T(128)S(1)} %add_rsqrt_fusion), kind=kOutput, calls=%fused_computation | convolution fusion | flops 270729216 | bytes 2886144 | tf_op jit(solution)/shard_map/rd,rf->df/dot_general | solution.py:453
  56.3 2.7 %constant_dynamic-slice_fusion.3 = (bf16[2,2,2,1,32,2048]{5,4,3,2,1,0:T(8,128)(2,1)}, bf16[2,2,2,1,32,2048]{5,4,3,2,1,0:T(8,128)(2,1)S(1)}) fusion(bf16[2,2,2,2,32,2048]{5,4,3,2,1,0:T(8,128)(2,1)} %bitcast.149, s32[]{:T(128)S(6)} %select_n.139, s32[]{:T(128)S(6)} %select_n.140), kind=kLoop, calls=%fused_computation.118 | loop fusion | bytes 4194312 | tf_op jit(solution)/shard_map/jit(dynamic_index_in_dim)/dynamic_slice | solution.py:239
  59.0 1.1 copy.109
  60.3 1.0 fusion.6
  61.3 1.7 copy.86
  62.9 5.5 %all-to-all-start = ((bf16[16,32,128]{2,1,0:T(8,128)(2,1)}), bf16[16,32,128]{2,1,0:T(8,128)(2,1)S(1)}, u32[]{:S(2)}, u32[]{:S(2)}) async-start(bf16[16,32,128]{2,1,0:T(8,128)(2,1)} %bitcast.15), calls=%async_computation | async-start | bytes 262144 | tf_op jit(solution)/shard_map/all_to_all | solution.py:227
  68.5 2.6 %fusion.2 = bf16[2,2,2,32,1536]{4,3,2,1,0:T(8,128)(2,1)} fusion(bf16[2,2,2,32,1536]{4,3,2,1,0:T(8,128)(2,1)} %collective-permute-done.1, bf16[2,2,2,2,32,1536]{5,4,3,2,1,0:T(8,128)(2,1)} %copy-done.2, s32[]{:T(128)S(6)} %select_n.139), kind=kLoop, calls=%fused_computation.9 | loop fusion | flops 1572864 | bytes 2359300 | tf_op jit(solution)/shard_map/convert_element_type | solution.py:246
  71.1 2.6 %fusion = bf16[2,2,2,32,2048]{4,3,0,1,2:T(8,128)(2,1)} fusion(bf16[2,2,2,32,2048]{4,3,0,1,2:T(8,128)(2,1)} %collective-permute-done, bf16[2,2,2,1,32,2048]{5,4,3,2,1,0:T(8,128)(2,1)S(1)} %copy-done.3), kind=kLoop, calls=%fused_computation.4 | loop fusion | flops 2097152 | bytes 3145728 | tf_op jit(solution)/shard_map/convert_element_type | solution.py:246
  73.7 2.7 %all-to-all-done.grad_ref = bf16[16,32,128]{2,1,0:T(8,128)(2,1)S(1)} async-done(((bf16[16,32,128]{2,1,0:T(8,128)(2,1)}), bf16[16,32,128]{2,1,0:T(8,128)(2,1)S(1)}, u32[]{:S(2)}, u32[]{:S(2)}) %all-to-all-start) | async-done | bytes 131104 | tf_op jit(solution)/shard_map/all_to_all | solution.py:227
  76.4 1.8 %dynamic-slice_bitcast_fusion.2 = bf16[2,2,32,1536]{3,2,1,0:T(8,128)(2,1)} fusion(bf16[2,2,2,32,1536]{4,3,2,1,0:T(8,128)(2,1)} %fusion.2, s32[]{:T(128)S(6)} %select_n.148), kind=kLoop, calls=%fused_computation.50 | loop fusion | bytes 786436 | tf_op jit(solution)/shard_map/jit(dynamic_index_in_dim)/squeeze | solution.py:240
  78.2 1.9 %dynamic-slice_bitcast_fusion.1 = bf16[2,2,32,2048]{3,2,0,1:T(8,128)(2,1)} fusion(bf16[2,2,2,32,2048]{4,3,0,1,2:T(8,128)(2,1)} %fusion, s32[]{:T(128)S(6)} %select_n.144), kind=kLoop, calls=%fused_computation.36 | loop fusion | bytes 1048580 | tf_op jit(solution)/shard_map/jit(dynamic_index_in_dim)/squeeze | solution.py:240
  80.7 11.8 %shard_map.164 = (bf16[16,32,128]{2,1,0:T(8,128)(2,1)S(1)}, bf16[16,64,128]{2,1,0:T(8,128)(2,1)S(1)}, f32[64,32]{1,0:T(8,128)S(1)}) custom-call(s32[16,5]{1,0:T(8,128)S(1)} %bitcast.148, bf16[16,96,128]{2,1,0:T(8,128)(2,1)S(1)} %get-tuple-element.21.qkv_ref, bf16[2,32,32]{2,1,0:T(8,128)(2,1)S(1)} %convolution_convert_fusion.7.virt_ref, ...), custom_call_target="tpu_custom_call" | custom-call | flops 356515840 | bytes 1179648 | tf_op jit(solution)/shard_map/pallas_call | solution.py:209
  92.7 2.0 %fusion.10 = bf16[2,2,32,1536]{3,2,1,0:T(8,128)(2,1)} fusion(bf16[2,2,32,1536]{3,2,1,0:T(8,128)(2,1)} %collective-permute-done.3, bf16[2,2,2,32,1536]{4,3,2,1,0:T(8,128)(2,1)} %fusion.2, s32[]{:T(128)S(6)} %select_n.147), kind=kLoop, calls=%fused_computation.30 | loop fusion | flops 786432 | bytes 1179652 | tf_op jit(solution)/shard_map/convert_element_type | solution.py:246
  94.6 1.3 fusion.7
  96.0 0.9 pad_maximum_fusion.2
  96.9 4.5 %all-to-all-start.1 = ((bf16[16,112,128]{2,1,0:T(8,128)(2,1)}), bf16[16,112,128]{2,1,0:T(8,128)(2,1)}, u32[]{:S(2)}, u32[]{:S(2)}) async-start(bf16[16,112,128]{2,1,0:T(8,128)(2,1)} %pad_maximum_fusion.2), calls=%async_computation.1 | async-start | bytes 917504 | tf_op jit(solution)/shard_map/all_to_all | solution.py:227
  101.6 2.3 %fusion.5 = bf16[128,512]{1,0:T(8,128)(2,1)} fusion(f32[128,512]{1,0:T(8,128)S(1)} %get-tuple-element.55, bf16[128,1024]{1,0:T(8,128)(2,1)} %copy-done.15, bf16[1024,512]{1,0:T(8,128)(2,1)} %param.17), kind=kOutput, calls=%fused_computation.18 | convolution fusion | flops 134348800 | bytes 1703936 | tf_op jit(solution)/shard_map/dot_general | solution.py:429
  103.8 0.7 dynamic-slice_bitcast_fusion.4
  104.5 2.6 %collective-permute-start.11 = (bf16[2,32,1536]{2,1,0:T(8,128)(2,1)}, bf16[2,32,1536]{2,1,0:T(8,128)(2,1)}, u32[]{:S(2)}, u32[]{:S(2)}) collective-permute-start(bf16[2,32,1536]{2,1,0:T(8,128)(2,1)} %dynamic-slice_bitcast_fusion.4), channel_id=1, source_target_pairs={{0,8},{1,9},{2,10},{3,11},{4,12},{5,13},{6,14},{7,15},{8,0},{9,1},... | collective-permute-start | bytes 589832 | tf_op jit(solution)/shard_map/ppermute | solution.py:241
  107.1 0.7 dynamic-slice_bitcast_fusion.3
  107.8 1.5 collective-permute-start.13
  109.3 5.8 %all-to-all-done.1 = bf16[16,112,128]{2,1,0:T(8,128)(2,1)} async-done(((bf16[16,112,128]{2,1,0:T(8,128)(2,1)}), bf16[16,112,128]{2,1,0:T(8,128)(2,1)}, u32[]{:S(2)}, u32[]{:S(2)}) %all-to-all-start.1) | async-done | bytes 458784 | tf_op jit(solution)/shard_map/all_to_all | solution.py:227
  115.0 1.2 fusion.61
  116.6 1.4 fusion.63
  118.0 1.8 %convolution_convert_fusion.1 = bf16[512,1536]{1,0:T(8,128)(2,1)} fusion(bf16[1536,128]{1,0:T(8,128)(2,1)S(1)} %bitcast.153, bf16[128,512]{1,0:T(8,128)(2,1)S(1)} %copy-done.4, f32[512]{0:T(512)S(1)} %copy-done.27, f32[128]{0:T(128)S(1)} %add_rsqrt_fusion.2), kind=kOutput, calls=%fused_computation.1 | convolution fusion | flops 202375168 | bytes 2099712 | tf_op jit(solution)/shard_map/rd,cr->dc/dot_general | solution.py:508
  119.8 0.8 slice.94
  121.6 1.8 %multiply_reduce_fusion.3 = (f32[32]{0:T(128)S(1)}, f32[32,512]{1,0:T(8,128)S(1)}) fusion(f32[32]{0:T(128)S(1)} %add_rsqrt_fusion.1, f32[32,512]{1,0:T(8,128)S(1)} %copy-done.21, f32[32]{0:T(128)S(1)} %div.85, bf16[1024,32]{0,1:T(8,128)(2,1)S(1)} %reshape.182, bf16[512,1536]{1,0:T(8,128)(2,1)} %param.14), kind=kOutput, calls=%fused_computation.98 | convolution fusion | flops 33619936 | bytes 1245568 | tf_op jit(solution)/shard_map/sp,ds->pd/dot_general | solution.py:503
  123.3 1.5 constant_dynamic-slice_fusion.1
  124.9 0.9 copy.110
  125.8 3.4 %collective-permute-start.4 = (bf16[2,2,2,32,1536]{4,3,2,0,1:T(8,128)(2,1)}, bf16[2,2,2,32,1536]{4,3,2,0,1:T(8,128)(2,1)}, u32[]{:S(2)}, u32[]{:S(2)}) collective-permute-start(bf16[2,2,2,32,1536]{4,3,2,0,1:T(8,128)(2,1)} %bitcast.142), channel_id=1, source_target_pairs={{0,1},{1,0},{2,3},{3,2},{4,5},{5,4},{6,7},{7,6},{8,9},{9,8},{10,11... | collective-permute-start | bytes 2359304 | tf_op jit(solution)/shard_map/ppermute | solution.py:241
  129.2 1.0 fusion.13
  130.9 1.5 collective-permute-start.12
  132.4 1.1 fusion.27
  133.5 1.0 fusion.11
  135.2 1.3 collective-permute-start.14
  137.2 4.5 %all-to-all-start.2 = ((f32[16,1,64]{2,1,0:T(1,128)}), f32[16,1,64]{2,1,0:T(1,128)S(1)}, u32[]{:S(2)}, u32[]{:S(2)}) async-start(f32[16,1,64]{2,1,0:T(1,128)} %bitcast.55), calls=%async_computation.2 | async-start | bytes 16384 | tf_op jit(solution)/shard_map/all_to_all | solution.py:227
  141.8 1.8 %fusion.26 = bf16[128,512]{1,0:T(8,128)(2,1)} fusion(bf16[128,512]{1,0:T(8,128)(2,1)S(1)} %copy-done.4, bf16[128,512]{1,0:T(8,128)(2,1)S(1)} %copy-done.11, f32[128,512]{1,0:T(8,128)} %get-tuple-element.59, f32[128]{0:T(128)S(1)} %broadcast_multiply_fusion.1, f32[512]{0:T(512)S(1)} %copy-done.27, f32[128]{0:T(128)S(1)} %add_rsqrt_fusion.2), kind=kLoop, calls=%fused_computation.63 | loop fusion | flops 589824 | bytes 658432 | tf_op jit(solution)/shard_map/convert_element_type | solution.py:532
  143.5 4.6 %all-to-all-done.2 = f32[16,1,64]{2,1,0:T(1,128)S(1)} async-done(((f32[16,1,64]{2,1,0:T(1,128)}), f32[16,1,64]{2,1,0:T(1,128)S(1)}, u32[]{:S(2)}, u32[]{:S(2)}) %all-to-all-start.2) | async-done | bytes 4128 | tf_op jit(solution)/shard_map/all_to_all | solution.py:227
  148.6 1.0 convert_add_fusion.10
  150.9 1.3 fusion.1
  152.9 1.6 convert_add_fusion.9
  155.2 3.8 %collective-permute-done.5 = bf16[2,2,32,768]{3,2,0,1:T(8,128)(2,1)S(1)} collective-permute-done((bf16[2,2,32,768]{3,2,0,1:T(8,128)(2,1)S(1)}, bf16[2,2,32,768]{3,2,0,1:T(8,128)(2,1)S(1)}, u32[]{:S(2)}, u32[]{:S(2)}) %collective-permute-start.5) | collective-permute-done | bytes 196640 | tf_op jit(solution)/shard_map/ppermute | solution.py:241
  159.7 1.6 collective-permute-done.8
  162.0 2.2 %collective-permute-done.6 = bf16[2,32,768]{2,1,0:T(8,128)(2,1)S(1)} collective-permute-done((bf16[2,32,768]{2,1,0:T(8,128)(2,1)S(1)}, bf16[2,32,768]{2,1,0:T(8,128)(2,1)S(1)}, u32[]{:S(2)}, u32[]{:S(2)}) %collective-permute-start.6) | collective-permute-done | bytes 98336 | tf_op jit(solution)/shard_map/ppermute | solution.py:241
  164.2 0.8 collective-permute-start.7
  165.0 3.7 %collective-permute-done.9 = bf16[2,32,768]{2,1,0:T(8,128)(2,1)S(1)} collective-permute-done((bf16[2,32,768]{2,1,0:T(8,128)(2,1)S(1)}, bf16[2,32,768]{2,1,0:T(8,128)(2,1)S(1)}, u32[]{:S(2)}, u32[]{:S(2)}) %collective-permute-start.9) | collective-permute-done | bytes 98336 | tf_op jit(solution)/shard_map/ppermute | solution.py:241
  168.7 2.3 %collective-permute-start.10 = (bf16[32,768]{1,0:T(8,128)(2,1)S(1)}, bf16[32,768]{1,0:T(8,128)(2,1)S(1)}, u32[]{:S(2)}, u32[]{:S(2)}) collective-permute-start(bf16[32,768]{1,0:T(8,128)(2,1)S(1)} %dynamic-slice_bitcast_fusion.11), channel_id=1, source_target_pairs={{0,2},{1,3},{2,0},{3,1},{4,6},{5,7},{6,4},{7,5},{8,10},{9,11},{10,... | collective-permute-start | bytes 147464 | tf_op jit(solution)/shard_map/ppermute | solution.py:241
  171.0 2.0 %collective-permute-done.10 = bf16[32,768]{1,0:T(8,128)(2,1)S(1)} collective-permute-done((bf16[32,768]{1,0:T(8,128)(2,1)S(1)}, bf16[32,768]{1,0:T(8,128)(2,1)S(1)}, u32[]{:S(2)}, u32[]{:S(2)}) %collective-permute-start.10) | collective-permute-done | bytes 49184 | tf_op jit(solution)/shard_map/ppermute | solution.py:241
  173.4 0.7 pad_maximum_fusion.6
  (141 shorter events, 13.5 us)
Async XLA Ops:
  0.6 43.1 %copy-start = (bf16[512,2048]{1,0:T(8,128)(2,1)S(1)}, bf16[512,2048]{1,0:T(8,128)(2,1)}, u32[]{:S(2)}) copy-start(bf16[512,2048]{1,0:T(8,128)(2,1)} %param.16) | copy-start | bytes 6291460
  8.3 1.1 copy-start.28
  30.3 13.1 %copy-start.20 = (f32[32,512]{1,0:T(8,128)}, f32[32,512]{1,0:T(8,128)S(1)}, u32[]{:S(2)}) copy-start(f32[32,512]{1,0:T(8,128)S(1)} %reshape.176) | copy-start | bytes 196612
  31.4 11.9 %copy-start.4 = (bf16[128,512]{1,0:T(8,128)(2,1)S(1)}, bf16[128,512]{1,0:T(8,128)(2,1)}, u32[]{:S(2)}) copy-start(bf16[128,512]{1,0:T(8,128)(2,1)} %param.11) | copy-start | bytes 393220
  31.5 11.9 %copy-start.5 = (bf16[512,512]{1,0:T(8,128)(2,1)S(1)}, bf16[512,512]{1,0:T(8,128)(2,1)}, u32[]{:S(2)}) copy-start(bf16[512,512]{1,0:T(8,128)(2,1)} %param.15) | copy-start | bytes 1572868
  31.5 12.3 %copy-start.26 = (f32[512]{0:T(512)S(1)}, f32[512]{0:T(512)}, u32[]{:S(2)}) copy-start(f32[512]{0:T(512)} %param.13) | copy-start | bytes 6148
  43.8 1.2 copy-start.14
  43.8 1.2 copy-start.17
  45.6 1.6 copy-start.22
  45.6 1.6 copy-start.24
  45.6 1.6 copy-start.15
  47.2 1.6 copy-start.19
  48.9 2.6 %copy-start.9 = (bf16[128,512]{1,0:T(8,128)(2,1)}, bf16[128,512]{1,0:T(8,128)(2,1)S(1)}, u32[]{:S(2)}) copy-start(bf16[128,512]{1,0:T(8,128)(2,1)S(1)} %add_convert_fusion) | copy-start | bytes 393220
  51.5 1.1 copy-start.2
  52.6 1.5 copy-start.23
  52.6 1.5 copy-start.25
  53.6 14.9 %collective-permute-start.1 = (bf16[2,2,2,32,1536]{4,3,2,1,0:T(8,128)(2,1)}, bf16[2,2,2,32,1536]{4,3,2,1,0:T(8,128)(2,1)}, u32[]{:S(2)}, u32[]{:S(2)}) collective-permute-start(bf16[2,2,2,32,1536]{4,3,2,1,0:T(8,128)(2,1)} %dynamic-slice_bitcast_fusion), channel_id=1, source_target_pairs={{0,1},{1,0},{2,3},{3,2},{4,5},{5,4},{6,7},{7,6},{8,9},{9,8},{10,11... | collective-permute-start | bytes 2359304 | tf_op jit(solution)/shard_map/ppermute | solution.py:241
  59.0 1.3 copy-start.6
  59.0 1.3 copy-start.10
  60.1 11.0 %collective-permute-start = (bf16[2,2,2,32,2048]{4,3,0,1,2:T(8,128)(2,1)}, bf16[2,2,2,32,2048]{4,3,0,1,2:T(8,128)(2,1)}, u32[]{:S(2)}, u32[]{:S(2)}) collective-permute-start(bf16[2,2,2,32,2048]{4,3,0,1,2:T(8,128)(2,1)} %bitcast.141), channel_id=1, source_target_pairs={{0,1},{1,0},{2,3},{3,2},{4,5},{5,4},{6,7},{7,6},{8,9},{9,8},{10,11... | collective-permute-start | bytes 3145736 | tf_op jit(solution)/shard_map/ppermute | solution.py:241
  62.9 13.4 %all-to-all-start = ((bf16[16,32,128]{2,1,0:T(8,128)(2,1)}), bf16[16,32,128]{2,1,0:T(8,128)(2,1)S(1)}, u32[]{:S(2)}, u32[]{:S(2)}) async-start(bf16[16,32,128]{2,1,0:T(8,128)(2,1)} %bitcast.15), calls=%async_computation | async-start | bytes 262144 | tf_op jit(solution)/shard_map/all_to_all | solution.py:227
  68.5 2.6 %copy-start.3 = (bf16[2,2,2,1,32,2048]{5,4,3,2,1,0:T(8,128)(2,1)S(1)}, bf16[2,2,2,1,32,2048]{5,4,3,2,1,0:T(8,128)(2,1)}, u32[]{:S(2)}) copy-start(bf16[2,2,2,1,32,2048]{5,4,3,2,1,0:T(8,128)(2,1)} %get-tuple-element.37) | copy-start | bytes 3145732
  78.2 14.5 %collective-permute-start.3 = (bf16[2,2,32,1536]{3,2,1,0:T(8,128)(2,1)}, bf16[2,2,32,1536]{3,2,1,0:T(8,128)(2,1)}, u32[]{:S(2)}, u32[]{:S(2)}) collective-permute-start(bf16[2,2,32,1536]{3,2,1,0:T(8,128)(2,1)} %dynamic-slice_bitcast_fusion.2), channel_id=1, source_target_pairs={{0,4},{1,5},{2,6},{3,7},{4,0},{5,1},{6,2},{7,3},{8,12},{9,13},{10,... | collective-permute-start | bytes 1179656 | tf_op jit(solution)/shard_map/ppermute | solution.py:241
  80.0 14.6 %collective-permute-start.2 = (bf16[2,2,32,2048]{3,2,0,1:T(8,128)(2,1)}, bf16[2,2,32,2048]{3,2,0,1:T(8,128)(2,1)}, u32[]{:S(2)}, u32[]{:S(2)}) collective-permute-start(bf16[2,2,32,2048]{3,2,0,1:T(8,128)(2,1)} %dynamic-slice_bitcast_fusion.1), channel_id=1, source_target_pairs={{0,2},{1,3},{2,0},{3,1},{4,6},{5,7},{6,4},{7,5},{8,10},{9,11},{10,... | collective-permute-start | bytes 1572872 | tf_op jit(solution)/shard_map/ppermute | solution.py:241
  96.0 11.1 %copy-start.7 = (bf16[2,2,32,2048]{3,2,0,1:T(8,128)(2,1)}, bf16[2,2,32,2048]{3,2,0,1:T(8,128)(2,1)S(1)}, u32[]{:S(2)}) copy-start(bf16[2,2,32,2048]{3,2,0,1:T(8,128)(2,1)S(1)} %fusion.7) | copy-start | bytes 1572868
  96.9 7.0 %copy-start.12 = (bf16[2,2,32,1536]{3,2,1,0:T(8,128)(2,1)S(1)}, bf16[2,2,32,1536]{3,2,1,0:T(8,128)(2,1)}, u32[]{:S(2)}) copy-start(bf16[2,2,32,1536]{3,2,1,0:T(8,128)(2,1)} %fusion.10) | copy-start | bytes 1179652
  96.9 18.1 %all-to-all-start.1 = ((bf16[16,112,128]{2,1,0:T(8,128)(2,1)}), bf16[16,112,128]{2,1,0:T(8,128)(2,1)}, u32[]{:S(2)}, u32[]{:S(2)}) async-start(bf16[16,112,128]{2,1,0:T(8,128)(2,1)} %pad_maximum_fusion.2), calls=%async_computation.1 | async-start | bytes 917504 | tf_op jit(solution)/shard_map/all_to_all | solution.py:227
  104.5 24.7 %collective-permute-start.11 = (bf16[2,32,1536]{2,1,0:T(8,128)(2,1)}, bf16[2,32,1536]{2,1,0:T(8,128)(2,1)}, u32[]{:S(2)}, u32[]{:S(2)}) collective-permute-start(bf16[2,32,1536]{2,1,0:T(8,128)(2,1)} %dynamic-slice_bitcast_fusion.4), channel_id=1, source_target_pairs={{0,8},{1,9},{2,10},{3,11},{4,12},{5,13},{6,14},{7,15},{8,0},{9,1},... | collective-permute-start | bytes 589832 | tf_op jit(solution)/shard_map/ppermute | solution.py:241
  107.8 25.7 %collective-permute-start.13 = (bf16[2,32,2048]{2,1,0:T(8,128)(2,1)}, bf16[2,32,2048]{2,1,0:T(8,128)(2,1)}, u32[]{:S(2)}, u32[]{:S(2)}) collective-permute-start(bf16[2,32,2048]{2,1,0:T(8,128)(2,1)} %dynamic-slice_bitcast_fusion.3), channel_id=1, source_target_pairs={{0,4},{1,5},{2,6},{3,7},{4,0},{5,1},{6,2},{7,3},{8,12},{9,13},{10,... | collective-permute-start | bytes 786440 | tf_op jit(solution)/shard_map/ppermute | solution.py:241
  115.0 1.6 copy-start.1
  116.2 1.8 %copy-start.27 = (f32[512]{0:T(512)S(1)}, f32[512]{0:T(512)}, u32[]{:S(2)}) copy-start(f32[512]{0:T(512)} %param.12) | copy-start | bytes 6148
  118.0 3.6 %copy-start.21 = (f32[32,512]{1,0:T(8,128)S(1)}, f32[32,512]{1,0:T(8,128)}, u32[]{:S(2)}) copy-start(f32[32,512]{1,0:T(8,128)} %copy-done.20) | copy-start | bytes 196612
  124.9 4.4 %copy-start.13 = (bf16[2,2,32,1536]{3,2,1,0:T(8,128)(2,1)S(1)}, bf16[2,2,32,1536]{3,2,1,0:T(8,128)(2,1)}, u32[]{:S(2)}) copy-start(bf16[2,2,32,1536]{3,2,1,0:T(8,128)(2,1)} %fusion.10) | copy-start | bytes 1179652
  124.9 7.6 %copy-start.18 = (f32[128,512]{1,0:T(8,128)S(1)}, f32[128,512]{1,0:T(8,128)}, u32[]{:S(2)}) copy-start(f32[128,512]{1,0:T(8,128)} %fusion.63) | copy-start | bytes 786436
  124.9 7.6 %copy-start.29 = (s32[128]{0:T(128)S(1)}, s32[128]{0:T(128)}, u32[]{:S(2)}) copy-start(s32[128]{0:T(128)} %param.20) | copy-start | bytes 1540
  124.9 8.6 %copy-start.8 = (bf16[2,2,32,2048]{3,2,0,1:T(8,128)(2,1)S(1)}, bf16[2,2,32,2048]{3,2,0,1:T(8,128)(2,1)}, u32[]{:S(2)}) copy-start(bf16[2,2,32,2048]{3,2,0,1:T(8,128)(2,1)} %copy-done.7) | copy-start | bytes 1572868
  125.8 15.9 %copy-start.11 = (bf16[128,512]{1,0:T(8,128)(2,1)S(1)}, bf16[128,512]{1,0:T(8,128)(2,1)}, u32[]{:S(2)}) copy-start(bf16[128,512]{1,0:T(8,128)(2,1)} %copy-done.9) | copy-start | bytes 393220
  125.8 25.1 %collective-permute-start.4 = (bf16[2,2,2,32,1536]{4,3,2,0,1:T(8,128)(2,1)}, bf16[2,2,2,32,1536]{4,3,2,0,1:T(8,128)(2,1)}, u32[]{:S(2)}, u32[]{:S(2)}) collective-permute-start(bf16[2,2,2,32,1536]{4,3,2,0,1:T(8,128)(2,1)} %bitcast.142), channel_id=1, source_target_pairs={{0,1},{1,0},{2,3},{3,2},{4,5},{5,4},{6,7},{7,6},{8,9},{9,8},{10,11... | collective-permute-start | bytes 2359304 | tf_op jit(solution)/shard_map/ppermute | solution.py:241
  130.2 3.3 %copy-start.16 = (bf16[2,32,1536]{2,1,0:T(8,128)(2,1)}, bf16[2,32,1536]{2,1,0:T(8,128)(2,1)S(1)}, u32[]{:S(2)}) copy-start(bf16[2,32,1536]{2,1,0:T(8,128)(2,1)S(1)} %fusion.13) | copy-start | bytes 589828
  130.9 17.7 %collective-permute-start.12 = (bf16[32,1536]{1,0:T(8,128)(2,1)}, bf16[32,1536]{1,0:T(8,128)(2,1)}, u32[]{:S(2)}, u32[]{:S(2)}) collective-permute-start(bf16[32,1536]{1,0:T(8,128)(2,1)} %dynamic-slice_bitcast_fusion.8), channel_id=1, source_target_pairs={{0,2},{1,3},{2,0},{3,1},{4,6},{5,7},{6,4},{7,5},{8,10},{9,11},{10,... | collective-permute-start | bytes 294920 | tf_op jit(solution)/shard_map/ppermute | solution.py:241
  135.2 17.7 %collective-permute-start.14 = (bf16[32,2048]{1,0:T(8,128)(2,1)}, bf16[32,2048]{1,0:T(8,128)(2,1)}, u32[]{:S(2)}, u32[]{:S(2)}) collective-permute-start(bf16[32,2048]{1,0:T(8,128)(2,1)} %dynamic-slice_bitcast_fusion.7), channel_id=1, source_target_pairs={{0,8},{1,9},{2,10},{3,11},{4,12},{5,13},{6,14},{7,15},{8,0},{9,1},... | collective-permute-start | bytes 393224 | tf_op jit(solution)/shard_map/ppermute | solution.py:241
  137.2 10.9 %all-to-all-start.2 = ((f32[16,1,64]{2,1,0:T(1,128)}), f32[16,1,64]{2,1,0:T(1,128)S(1)}, u32[]{:S(2)}, u32[]{:S(2)}) async-start(f32[16,1,64]{2,1,0:T(1,128)} %bitcast.55), calls=%async_computation.2 | async-start | bytes 16384 | tf_op jit(solution)/shard_map/all_to_all | solution.py:227
  152.4 6.7 %collective-permute-start.5 = (bf16[2,2,32,768]{3,2,0,1:T(8,128)(2,1)S(1)}, bf16[2,2,32,768]{3,2,0,1:T(8,128)(2,1)S(1)}, u32[]{:S(2)}, u32[]{:S(2)}) collective-permute-start(bf16[2,2,32,768]{3,2,0,1:T(8,128)(2,1)S(1)} %dynamic-slice_bitcast_fusion.6), channel_id=1, source_target_pairs={{0,2},{1,3},{2,0},{3,1},{4,6},{5,7},{6,4},{7,5},{8,10},{9,11},{10,... | collective-permute-start | bytes 589832 | tf_op jit(solution)/shard_map/ppermute | solution.py:241
  154.6 6.7 %collective-permute-start.8 = (bf16[2,2,32,768]{3,2,1,0:T(8,128)(2,1)S(1)}, bf16[2,2,32,768]{3,2,1,0:T(8,128)(2,1)S(1)}, u32[]{:S(2)}, u32[]{:S(2)}) collective-permute-start(bf16[2,2,32,768]{3,2,1,0:T(8,128)(2,1)S(1)} %dynamic-slice_bitcast_fusion.5), channel_id=1, source_target_pairs={{0,4},{1,5},{2,6},{3,7},{4,0},{5,1},{6,2},{7,3},{8,12},{9,13},{10,... | collective-permute-start | bytes 589832 | tf_op jit(solution)/shard_map/ppermute | solution.py:241
  159.1 5.1 %collective-permute-start.6 = (bf16[2,32,768]{2,1,0:T(8,128)(2,1)S(1)}, bf16[2,32,768]{2,1,0:T(8,128)(2,1)S(1)}, u32[]{:S(2)}, u32[]{:S(2)}) collective-permute-start(bf16[2,32,768]{2,1,0:T(8,128)(2,1)S(1)} %dynamic-slice_bitcast_fusion.10), channel_id=1, source_target_pairs={{0,4},{1,5},{2,6},{3,7},{4,0},{5,1},{6,2},{7,3},{8,12},{9,13},{10,... | collective-permute-start | bytes 294920 | tf_op jit(solution)/shard_map/ppermute | solution.py:241
  161.4 7.3 %collective-permute-start.9 = (bf16[2,32,768]{2,1,0:T(8,128)(2,1)S(1)}, bf16[2,32,768]{2,1,0:T(8,128)(2,1)S(1)}, u32[]{:S(2)}, u32[]{:S(2)}) collective-permute-start(bf16[2,32,768]{2,1,0:T(8,128)(2,1)S(1)} %dynamic-slice_bitcast_fusion.9), channel_id=1, source_target_pairs={{0,8},{1,9},{2,10},{3,11},{4,12},{5,13},{6,14},{7,15},{8,0},{9,1},... | collective-permute-start | bytes 294920 | tf_op jit(solution)/shard_map/ppermute | solution.py:241
  164.2 6.8 %collective-permute-start.7 = (bf16[32,768]{1,0:T(8,128)(2,1)S(1)}, bf16[32,768]{1,0:T(8,128)(2,1)S(1)}, u32[]{:S(2)}, u32[]{:S(2)}) collective-permute-start(bf16[32,768]{1,0:T(8,128)(2,1)S(1)} %dynamic-slice_bitcast_fusion.12), channel_id=1, source_target_pairs={{0,8},{1,9},{2,10},{3,11},{4,12},{5,13},{6,14},{7,15},{8,0},{9,1},... | collective-permute-start | bytes 147464 | tf_op jit(solution)/shard_map/ppermute | solution.py:241
  168.7 4.4 %collective-permute-start.10 = (bf16[32,768]{1,0:T(8,128)(2,1)S(1)}, bf16[32,768]{1,0:T(8,128)(2,1)S(1)}, u32[]{:S(2)}, u32[]{:S(2)}) collective-permute-start(bf16[32,768]{1,0:T(8,128)(2,1)S(1)} %dynamic-slice_bitcast_fusion.11), channel_id=1, source_target_pairs={{0,2},{1,3},{2,0},{3,1},{4,6},{5,7},{6,4},{7,5},{8,10},{9,11},{10,... | collective-permute-start | bytes 147464 | tf_op jit(solution)/shard_map/ppermute | solution.py:241

commit v5 on v4

--- a/solution.py
+++ b/solution.py
@@ -172,7 +172,7 @@
         dvirt_ref[head_dim : 2 * head_dim, :] += dot_nt(grad, pb[KT])
         return carry
 
-    lax.fori_loop(0, grad_ref.shape[0], body, 0)
+    lax.fori_loop(0, grad_ref.shape[0], body, 0, unroll=2)
     dkv_ref[...] = acc_ref[...].astype(jnp.bfloat16)
 
 
@@ -329,6 +329,98 @@
             flops=sums.size, bytes_accessed=4 * size * qkv_heads[0].size, transcendentals=0
         ),
     )(sums, list_rows, qkv_heads)
+
+
+def fold_kernel(orders, *refs):
+    me = lax.axis_index("seq")
+    steps = len(orders[0])
+    inputs, outputs, scratch = refs[:2], refs[2:4], refs[4:-2]
+    send, recv = refs[-2:]
+    landing = (scratch[:steps], scratch[steps : 2 * steps])
+    rest = scratch[2 * steps :]
+    held = (rest[: steps - 1], rest[steps - 1 :])
+
+    def partner(bit):
+        return me + (1 << bit) * (1 - 2 * ((me // (1 << bit)) % 2))
+
+    def half(stream, step, theirs):
+        bit = orders[stream][step]
+        left = sorted(set(range(steps)) - set(orders[stream][:step]), reverse=True)
+        mine = (me // (1 << bit)) % 2
+        index = (slice(None),) * left.index(bit) + (1 - mine if theirs else mine,)
+        return (inputs[stream] if step == 0 else held[stream][step - 1]), index
+
+    def copy(stream, step):
+        source, index = half(stream, step, True)
+        return pltpu.make_async_remote_copy(
+            src_ref=source.at[index],
+            dst_ref=landing[stream][step],
+            send_sem=send.at[stream, step],
+            recv_sem=recv.at[stream, step],
+            device_id={"seq": partner(orders[stream][step])},
+            device_id_type=pl.DeviceIdType.MESH,
+        )
+
+    barrier = pltpu.get_barrier_semaphore()
+    for bit in range(steps):
+        pl.semaphore_signal(
+            barrier,
+            inc=1,
+            device_id={"seq": partner(bit)},
+            device_id_type=pl.DeviceIdType.MESH,
+        )
+    pl.semaphore_wait(barrier, steps)
+    for stream in range(2):
+        copy(stream, 0).start()
+    for step in range(steps):
+        for stream in range(2):
+            copy(stream, step).wait_recv()
+            source, index = half(stream, step, False)
+            total = source[index].astype(jnp.float32) + landing[stream][step][...].astype(
+                jnp.float32
+            )
+            if step == steps - 1:
+                outputs[stream][...] = total
+            else:
+                held[stream][step][...] = total.astype(jnp.bfloat16)
+                copy(stream, step + 1).start()
+    for step in range(steps):
+        for stream in range(2):
+            copy(stream, step).wait_send()
+
+
+def fold(one, two):
+    size = one.shape[0]
+    steps = size.bit_length() - 1
+    orders = ([0, 1] + list(range(2, steps)), [0] + list(range(2, steps)) + [1])
+    vmem = pl.BlockSpec(memory_space=pltpu.VMEM)
+    blocks = [as_bits(one)[0], as_bits(two)[0]]
+    tails = [one.shape[1:], two.shape[1:]]
+    landing = [
+        pltpu.VMEM((2,) * (steps - 1 - step) + tail, jnp.bfloat16)
+        for tail in tails
+        for step in range(steps)
+    ]
+    held = [
+        pltpu.VMEM((2,) * (steps - 1 - step) + tail, jnp.bfloat16)
+        for tail in tails
+        for step in range(steps - 1)
+    ]
+    return pl.pallas_call(
+        functools.partial(fold_kernel, orders),
+        out_shape=tuple(jax.ShapeDtypeStruct(tail, jnp.float32) for tail in tails),
+        in_specs=[vmem, vmem],
+        out_specs=(vmem, vmem),
+        scratch_shapes=landing
+        + held
+        + [pltpu.SemaphoreType.DMA((2, steps)), pltpu.SemaphoreType.DMA((2, steps))],
+        compiler_params=pltpu.CompilerParams(
+            vmem_limit_bytes=VMEM_BYTES, collective_id=2, has_side_effects=True
+        ),
+        cost_estimate=pl.CostEstimate(
+            flops=one.size, bytes_accessed=8 * (one.size + two.size), transcendentals=0
+        ),
+    )(*blocks)
 
 
 def on_device(
@@ -511,15 +603,6 @@
         one, one_left = halve(one, one_left, bit, late if step == 0 else None)
     for step, bit in enumerate(two_order):
         two, two_left = halve(two, two_left, bit, late if step == 0 else None)
-    late, late_left = as_bits(late)
-    late, late_left = halve(late, late_left, 0)
-    middle = late.shape[-1] // 2
-    late_one, late_two = late[..., :middle], late[..., middle:]
-    one_left, two_left = late_left, late_left
-    for one_bit, two_bit in zip([1] + outer, outer + [1]):
-        late_one, one_left = halve(late_one, one_left, one_bit)
-        late_two, two_left = halve(late_two, two_left, two_bit)
-    late_sum = jnp.concatenate([late_one, late_two], axis=1)
     d_normed = jnp.einsum(
         "cr,dc->rd", d_qkv_t, query_key_value_weight, preferred_element_type=jnp.float32
     )
@@ -534,7 +617,23 @@
         [jnp.sum(d_normed * unit_attn, axis=0), jnp.sum(d_normed_ffn * unit_ffn, axis=0)]
     )
     gain_share = 2 * width // seq_size
-    grad_gains = jnp.sum(all_to_all(gain_local.reshape(seq_size, gain_share)), axis=0)
+    gain_block = jnp.pad(
+        gain_local.astype(jnp.bfloat16).reshape(seq_size, 1, gain_share),
+        ((0, 0), (0, share - 1), (0, 128 - gain_share)),
+    )
+    middle = late.shape[2] // 2
+    late_one = late[:, :, :middle]
+    late_two = jnp.concatenate([late[:, :, middle:], gain_block], axis=2)
+    if share % 16 == 0:
+        late_one, late_two = fold(late_one, late_two)
+    else:
+        late_one, first_left = as_bits(late_one)
+        late_two, second_left = as_bits(late_two)
+        for bit in [0, 1] + outer:
+            late_one, first_left = halve(late_one, first_left, bit)
+            late_two, second_left = halve(late_two, second_left, bit)
+    late_sum = jnp.concatenate([late_one, late_two], axis=1)
+    grad_gains = late_sum[0, 3 * width : 3 * width + gain_share]
     grad_w_in = one
     grad_w_out = two[:, :width]
     grad_w_down = jnp.concatenate(

time: 175 us -> 168 us (0.960)
  Pallas kernels: 43.5 us -> 67.6 us
  starting transfers between devices: 31.7 us -> 17.5 us
  waiting for transfers between devices: 26.3 us -> 13.6 us
  other arithmetic: 24 us -> 18.5 us
    pallas_call x0 -> x1, Pallas kernels: none -> 25.6 us  [fold(): pl.pallas_call(functools.partial(fold_kernel, orders), out_shape=tuple((j...]
    ppermute x15 -> x8, starting transfers between devices: 17.1 us -> 7.61 us  [halve(): got = lax.ppermute(send, 'seq', [(i, i ^ 1 << bit) for i in range(size)])]
    ppermute x15 -> x8, waiting for transfers between devices: 13.3 us -> 6.09 us  [halve(): got = lax.ppermute(send, 'seq', [(i, i ^ 1 << bit) for i in range(size)])]
    all_to_all x3 -> x2, waiting for transfers between devices: 13 us -> 7.53 us  [all_to_all(): lax.all_to_all(blocks, 'seq', split_axis=0, concat_axis=0, tiled=True)]
    all_to_all x3 -> x2, starting transfers between devices: 14.6 us -> 9.91 us  [all_to_all(): lax.all_to_all(blocks, 'seq', split_axis=0, concat_axis=0, tiled=True)]
    add x4 -> x2, other arithmetic: 2.62 us -> 0.75 us  [halve(): total = keep.astype(jnp.float32) + got.astype(jnp.float32)]
    convert_element_type x11 -> x6, other arithmetic: 12 us -> 10.5 us  [halve(): return (total if not rest else total.astype(jnp.bfloat16), rest)]
    dynamic_slice x2 -> x1, local copies, waits for them, and re-layouts: 4.2 us -> 2.71 us  [halve(): keep = lax.dynamic_index_in_dim(held, mine, axis, keepdims=False)]
  transfers between devices with their start and end apart: 18 -> 10, of which waited for: 8 -> 4; matrix products, arithmetic and copies ran while one was open for 26% -> 24% of each run, Pallas kernels for 7% -> 22%
where the time goes in v5:
time: 168 us; the launch traced here: 167 us
  Pallas kernels  67.6 us (40%)
  local copies, waits for them, and re-layouts  26.2 us (16%)
  matrix products  21.1 us (13%)
  other arithmetic  18.5 us (11%)
  starting transfers between devices  17.5 us (10%)
  waiting for transfers between devices  13.6 us (8%)
  between operations  1.97 us (1%)
    pallas_call x1, Pallas kernels, fold(): pl.pallas_call(functools.partial(fold_kernel, orders), out_shape=tuple((j...  25.6 us
    pallas_call x1, Pallas kernels, exchange(): pl.pallas_call(functools.partial(exchange_kernel, slices), out_shape=(jax...  19.8 us
    pallas_call x1, Pallas kernels, attention_forward(): pl.pallas_call(functools.partial(forward_kernel, head_dim, slices, size),...  11.9 us
    convert_element_type x6, other arithmetic, halve(): return (total if not rest else total.astype(jnp.bfloat16), rest)  10.5 us
    pallas_call x1, Pallas kernels, attention_backward(): pl.pallas_call(functools.partial(backward_kernel, head_dim), out_shape=(j...  10.3 us
    all_to_all x2, starting transfers between devices, all_to_all(): lax.all_to_all(blocks, 'seq', split_axis=0, concat_axis=0, tiled=True)  9.91 us
    ppermute x8, starting transfers between devices, halve(): got = lax.ppermute(send, 'seq', [(i, i ^ 1 << bit) for i in range(size)])  7.61 us
    all_to_all x2, waiting for transfers between devices, all_to_all(): lax.all_to_all(blocks, 'seq', split_axis=0, concat_axis=0, tiled=True)  7.53 us
  transfers between devices with their start and end apart: 10, of which 4 were waited for; matrix products, arithmetic and copies ran while one was open for 24% of the time, Pallas kernels for 22%

profile of v5, /device:TPU:0, one launch (start us, length us, event | category | flops | bytes accessed | tf_op | source)
XLA Modules:
  0.0 166.5 jit_solution(2051766258506822035)
XLA Ops:
  0.6 0.9 fusion.39
  1.6 1.0 fusion.27
  2.6 1.1 convolution_convert_fusion.6
  3.7 1.9 %convolution_convert_fusion.2 = bf16[128,1536]{1,0:T(8,128)(2,1)S(1)} fusion(bf16[512,1536]{1,0:T(8,128)(2,1)} %param.14, bf16[128,512]{1,0:T(8,128)(2,1)} %param.11, f32[512]{0:T(512)} %param.12, f32[128]{0:T(128)S(1)} %add_rsqrt_fusion.2), kind=kOutput, calls=%fused_computation.2 | convolution fusion | flops 201785344 | bytes 2099712 | tf_op jit(solution)/shard_map/dot_general | solution.py:477
  5.7 2.6 %copy.62 = bf16[512,1536]{0,1:T(8,128)(2,1)} copy(bf16[512,1536]{1,0:T(8,128)(2,1)} %param.14) | data formatting | bytes 3145728 | tf_op args[3]
  9.7 19.8 %shard_map.162 = (bf16[16,96,128]{2,1,0:T(8,128)(2,1)S(1)}, bf16[16,16,128]{2,1,0:T(8,128)(2,1)S(1)}) custom-call(bf16[16,16,128]{2,1,0:T(8,128)(2,1)S(1)} %maximum_maximum_fusion.sums_ref, f32[16,128]{1,0:T(8,128)S(1)} %pad.8.list_ref, bf16[16,96,128]{2,1,0:T(8,128)(2,1)S(1)} %bitcast.110), custom_call_target="tpu_custom_call" | custom-call | flops 32768 | bytes 786432 | tf_op jit(solution)/shard_map/pallas_call | solution.py:311
  30.5 1.0 convolution_convert_fusion.7.virt_ref
  31.5 11.9 %shard_map.163 = bf16[16,32,128]{2,1,0:T(8,128)(2,1)S(1)} custom-call(s32[16,5]{1,0:T(8,128)S(1)} %bitcast.113, bf16[16,96,128]{2,1,0:T(8,128)(2,1)S(1)} %get-tuple-element.23.qkv_ref, bf16[2,32,32]{2,1,0:T(8,128)(2,1)S(1)} %convolution_convert_fusion.7.virt_ref), custom_call_target="tpu_custom_call" | custom-call | flops 142606336 | bytes 393216 | tf_op jit(solution)/shard_map/pallas_call | solution.py:184
  43.8 0.5 fusion.47
  44.3 0.7 copy-done.11
  45.0 0.5 multiply_convert_fusion.1
  45.6 0.7 copy-done.18
  46.3 1.5 multiply_reduce_fusion
  47.8 0.5 convolution_convert_fusion.3
  48.3 1.1 fusion.53
  49.5 1.1 convolution_convert_fusion.4
  50.6 1.5 pad_maximum_fusion
  52.2 1.1 copy-done.2
  53.3 1.0 dynamic-slice_bitcast_fusion
  54.3 0.5 collective-permute-start.1
  54.8 2.1 %convolution_convert_fusion = bf16[512,2048]{1,0:T(8,128)(2,1)} fusion(bf16[128,1024]{1,0:T(8,128)(2,1)S(1)} %copy-done.21, bf16[128,1024]{1,0:T(8,128)(2,1)S(1)} %copy-done.19, f32[128,512]{1,0:T(8,128)S(1)} %get-tuple-element.57, f32[512]{0:T(512)S(1)} %copy-done.22, f32[128]{0:T(128)S(1)} %add_rsqrt_fusion), kind=kOutput, calls=%fused_computation | convolution fusion | flops 270729216 | bytes 2886144 | tf_op jit(solution)/shard_map/rd,rf->df/dot_general | solution.py:545
  57.0 2.7 %constant_dynamic-slice_fusion.1 = (bf16[2,2,2,1,32,2048]{5,4,3,2,1,0:T(8,128)(2,1)}, bf16[2,2,2,1,32,2048]{5,4,3,2,1,0:T(8,128)(2,1)S(1)}) fusion(bf16[2,2,2,2,32,2048]{5,4,3,2,1,0:T(8,128)(2,1)} %bitcast.115, s32[]{:T(128)S(6)} %select_n.99, s32[]{:T(128)S(6)} %select_n.100), kind=kLoop, calls=%fused_computation.99 | loop fusion | bytes 4194312 | tf_op jit(solution)/shard_map/jit(dynamic_index_in_dim)/dynamic_slice | solution.py:239
  59.7 1.1 copy.84
  61.0 1.0 fusion.6
  62.0 1.7 copy.66
  63.6 5.5 %all-to-all-start = ((bf16[16,32,128]{2,1,0:T(8,128)(2,1)}), bf16[16,32,128]{2,1,0:T(8,128)(2,1)S(1)}, u32[]{:S(2)}, u32[]{:S(2)}) async-start(bf16[16,32,128]{2,1,0:T(8,128)(2,1)} %bitcast.15), calls=%async_computation | async-start | bytes 262144 | tf_op jit(solution)/shard_map/all_to_all | solution.py:227
  69.2 2.6 %fusion.2 = bf16[2,2,2,32,1536]{4,3,2,1,0:T(8,128)(2,1)} fusion(bf16[2,2,2,32,1536]{4,3,2,1,0:T(8,128)(2,1)} %collective-permute-done.1, bf16[2,2,2,2,32,1536]{5,4,3,2,1,0:T(8,128)(2,1)} %copy-done.2, s32[]{:T(128)S(6)} %select_n.99), kind=kLoop, calls=%fused_computation.9 | loop fusion | flops 1572864 | bytes 2359300 | tf_op jit(solution)/shard_map/convert_element_type | solution.py:246
  71.8 2.6 %fusion = bf16[2,2,2,32,2048]{4,3,0,1,2:T(8,128)(2,1)} fusion(bf16[2,2,2,32,2048]{4,3,0,1,2:T(8,128)(2,1)} %collective-permute-done, bf16[2,2,2,1,32,2048]{5,4,3,2,1,0:T(8,128)(2,1)S(1)} %copy-done.3), kind=kLoop, calls=%fused_computation.4 | loop fusion | flops 2097152 | bytes 3145728 | tf_op jit(solution)/shard_map/convert_element_type | solution.py:246
  74.4 2.7 %all-to-all-done.grad_ref = bf16[16,32,128]{2,1,0:T(8,128)(2,1)S(1)} async-done(((bf16[16,32,128]{2,1,0:T(8,128)(2,1)}), bf16[16,32,128]{2,1,0:T(8,128)(2,1)S(1)}, u32[]{:S(2)}, u32[]{:S(2)}) %all-to-all-start) | async-done | bytes 131104 | tf_op jit(solution)/shard_map/all_to_all | solution.py:227
  77.1 1.8 %dynamic-slice_bitcast_fusion.2 = bf16[2,2,32,1536]{3,2,1,0:T(8,128)(2,1)} fusion(bf16[2,2,2,32,1536]{4,3,2,1,0:T(8,128)(2,1)} %fusion.2, s32[]{:T(128)S(6)} %select_n.108), kind=kLoop, calls=%fused_computation.46 | loop fusion | bytes 786436 | tf_op jit(solution)/shard_map/jit(dynamic_index_in_dim)/squeeze | solution.py:240
  78.8 1.9 %dynamic-slice_bitcast_fusion.1 = bf16[2,2,32,2048]{3,2,0,1:T(8,128)(2,1)} fusion(bf16[2,2,2,32,2048]{4,3,0,1,2:T(8,128)(2,1)} %fusion, s32[]{:T(128)S(6)} %select_n.104), kind=kLoop, calls=%fused_computation.36 | loop fusion | bytes 1048580 | tf_op jit(solution)/shard_map/jit(dynamic_index_in_dim)/squeeze | solution.py:240
  80.7 0.7 collective-permute-start.2
  81.4 10.3 %shard_map.164 = (bf16[16,32,128]{2,1,0:T(8,128)(2,1)S(1)}, bf16[16,64,128]{2,1,0:T(8,128)(2,1)S(1)}, f32[64,32]{1,0:T(8,128)S(1)}) custom-call(s32[16,5]{1,0:T(8,128)S(1)} %bitcast.114, bf16[16,96,128]{2,1,0:T(8,128)(2,1)S(1)} %get-tuple-element.23.qkv_ref, bf16[2,32,32]{2,1,0:T(8,128)(2,1)S(1)} %convolution_convert_fusion.7.virt_ref, ...), custom_call_target="tpu_custom_call" | custom-call | flops 356515840 | bytes 1179648 | tf_op jit(solution)/shard_map/pallas_call | solution.py:209
  91.8 2.0 %fusion.11 = bf16[2,2,32,1536]{3,2,1,0:T(8,128)(2,1)} fusion(bf16[2,2,32,1536]{3,2,1,0:T(8,128)(2,1)} %collective-permute-done.3, bf16[2,2,2,32,1536]{4,3,2,1,0:T(8,128)(2,1)} %fusion.2, s32[]{:T(128)S(6)} %select_n.107), kind=kLoop, calls=%fused_computation.31 | loop fusion | flops 786432 | bytes 1179652 | tf_op jit(solution)/shard_map/convert_element_type | solution.py:246
  93.8 0.9 collective-permute-done.2
  94.6 1.3 fusion.7
  96.0 0.8 pad_maximum_fusion.2
  96.8 4.4 %all-to-all-start.1 = ((bf16[16,112,128]{2,1,0:T(8,128)(2,1)}), bf16[16,112,128]{2,1,0:T(8,128)(2,1)}, u32[]{:S(2)}, u32[]{:S(2)}) async-start(bf16[16,112,128]{2,1,0:T(8,128)(2,1)} %pad_maximum_fusion.2), calls=%async_computation.1 | async-start | bytes 917504 | tf_op jit(solution)/shard_map/all_to_all | solution.py:227
  101.3 2.3 %fusion.5 = bf16[128,512]{1,0:T(8,128)(2,1)} fusion(f32[128,512]{1,0:T(8,128)S(1)} %get-tuple-element.57, bf16[128,1024]{1,0:T(8,128)(2,1)} %copy-done.12, bf16[1024,512]{1,0:T(8,128)(2,1)} %param.17), kind=kOutput, calls=%fused_computation.18 | convolution fusion | flops 134348800 | bytes 1703936 | tf_op jit(solution)/shard_map/dot_general | solution.py:521
  103.6 1.6 dynamic-slice_bitcast_fusion.4
  105.2 2.5 %collective-permute-start.4 = (bf16[2,32,1536]{2,1,0:T(8,128)(2,1)}, bf16[2,32,1536]{2,1,0:T(8,128)(2,1)}, u32[]{:S(2)}, u32[]{:S(2)}) collective-permute-start(bf16[2,32,1536]{2,1,0:T(8,128)(2,1)} %dynamic-slice_bitcast_fusion.4), channel_id=1, source_target_pairs={{0,8},{1,9},{2,10},{3,11},{4,12},{5,13},{6,14},{7,15},{8,0},{9,1},... | collective-permute-start | bytes 589832 | tf_op jit(solution)/shard_map/ppermute | solution.py:241
  107.7 0.7 dynamic-slice_bitcast_fusion.3
  108.4 1.5 collective-permute-start.6
  109.9 4.8 %all-to-all-done.1 = bf16[16,112,128]{2,1,0:T(8,128)(2,1)} async-done(((bf16[16,112,128]{2,1,0:T(8,128)(2,1)}), bf16[16,112,128]{2,1,0:T(8,128)(2,1)}, u32[]{:S(2)}, u32[]{:S(2)}) %all-to-all-start.1) | async-done | bytes 458784 | tf_op jit(solution)/shard_map/all_to_all | solution.py:227
  114.8 1.2 fusion.54
  116.0 0.4 copy-done.1
  116.4 1.4 fusion.56
  117.7 1.8 %convolution_convert_fusion.1 = bf16[512,1536]{1,0:T(8,128)(2,1)} fusion(bf16[1536,128]{1,0:T(8,128)(2,1)S(1)} %bitcast.119, bf16[128,512]{1,0:T(8,128)(2,1)S(1)} %copy-done.4, f32[512]{0:T(512)S(1)} %copy-done.23, f32[128]{0:T(128)S(1)} %add_rsqrt_fusion.2), kind=kOutput, calls=%fused_computation.1 | convolution fusion | flops 202375168 | bytes 2099712 | tf_op jit(solution)/shard_map/rd,cr->dc/dot_general | solution.py:600
  119.6 0.9 slice.98
  120.6 0.4 copy.72
  121.3 1.8 %multiply_reduce_fusion.3 = (f32[32]{0:T(128)S(1)}, f32[32,512]{1,0:T(8,128)S(1)}) fusion(f32[32]{0:T(128)S(1)} %add_rsqrt_fusion.1, f32[32,512]{1,0:T(8,128)S(1)} %copy-done.17, f32[32]{0:T(128)S(1)} %div.78, bf16[1024,32]{0,1:T(8,128)(2,1)S(1)} %reshape.201, bf16[512,1536]{1,0:T(8,128)(2,1)} %param.14), kind=kOutput, calls=%fused_computation.83 | convolution fusion | flops 33619936 | bytes 1245568 | tf_op jit(solution)/shard_map/sp,ds->pd/dot_general | solution.py:595
  123.1 2.0 %fusion.26 = (bf16[512]{0:T(512)(128)(2,1)S(1)}, f32[128]{0:T(128)S(1)}, f32[128,512]{1,0:T(8,128)}) fusion(bf16[128,512]{1,0:T(8,128)(2,1)S(1)} %copy-done.4, f32[128]{0:T(128)S(1)} %add_rsqrt_fusion.2, f32[512]{0:T(512)S(1)} %copy-done.23, f32[128,512]{1,0:T(8,128)} %fusion.56, f32[32,512]{1,0:T(8,128)S(1)} %get-tuple-element.60, ...), kind=kOutput, calls=%fused_computation.60 | convolution fusion | flops 25791872 | bytes 791424 | tf_op jit(solution)/shard_map/dot_general | solution.py:609
  125.2 1.5 fusion.52
  126.8 1.0 fusion.14
  127.9 25.6 %shard_map.165 = (f32[32,768]{1,0:T(8,128)S(1)}, f32[32,896]{1,0:T(8,128)S(1)}) custom-call(bf16[2,2,2,2,32,768]{5,4,3,2,1,0:T(8,128)(2,1)S(1)} %bitcast.109, bf16[2,2,2,2,32,896]{5,4,3,2,1,0:T(8,128)(2,1)S(1)} %bitcast.108), custom_call_target="tpu_custom_call" | custom-call | flops 393216 | bytes 6815744 | tf_op jit(solution)/shard_map/pallas_call | solution.py:409
  153.5 2.4 %collective-permute-start.5 = (bf16[32,1536]{1,0:T(8,128)(2,1)S(1)}, bf16[32,1536]{1,0:T(8,128)(2,1)S(1)}, u32[]{:S(2)}, u32[]{:S(2)}) collective-permute-start(bf16[32,1536]{1,0:T(8,128)(2,1)S(1)} %dynamic-slice_bitcast_fusion.6), channel_id=1, source_target_pairs={{0,2},{1,3},{2,0},{3,1},{4,6},{5,7},{6,4},{7,5},{8,10},{9,11},{10,... | collective-permute-start | bytes 294920 | tf_op jit(solution)/shard_map/ppermute | solution.py:241
  155.9 1.0 fusion.12
  157.0 0.8 fusion.25
  158.1 0.7 pad_maximum_fusion.6
  158.8 0.5 slice_bitcast_fusion
  159.3 0.6 fusion.55
  160.0 0.7 pad_maximum_fusion.8
  160.6 5.2 %collective-permute-done.7 = bf16[32,2048]{1,0:T(8,128)(2,1)S(1)} collective-permute-done((bf16[32,2048]{1,0:T(8,128)(2,1)S(1)}, bf16[32,2048]{1,0:T(8,128)(2,1)S(1)}, u32[]{:S(2)}, u32[]{:S(2)}) %collective-permute-start.7) | collective-permute-done | bytes 131104 | tf_op jit(solution)/shard_map/ppermute | solution.py:241
  165.8 0.7 convert_add_fusion.6
  (105 shorter events, 3.6 us)
Async XLA Ops:
  0.6 43.2 %copy-start = (bf16[512,2048]{1,0:T(8,128)(2,1)S(1)}, bf16[512,2048]{1,0:T(8,128)(2,1)}, u32[]{:S(2)}) copy-start(bf16[512,2048]{1,0:T(8,128)(2,1)} %param.16) | copy-start | bytes 6291460
  5.7 3.8 %copy-start.24 = (s32[1,4]{1,0:T(1,128)S(1)}, s32[1,4]{1,0:T(1,128)}, u32[]{:S(2)}) copy-start(s32[1,4]{1,0:T(1,128)} %param.18) | copy-start | bytes 52
  30.3 13.1 %copy-start.16 = (f32[32,512]{1,0:T(8,128)}, f32[32,512]{1,0:T(8,128)S(1)}, u32[]{:S(2)}) copy-start(f32[32,512]{1,0:T(8,128)S(1)} %reshape.195) | copy-start | bytes 196612
  31.4 12.0 %copy-start.4 = (bf16[128,512]{1,0:T(8,128)(2,1)S(1)}, bf16[128,512]{1,0:T(8,128)(2,1)}, u32[]{:S(2)}) copy-start(bf16[128,512]{1,0:T(8,128)(2,1)} %param.11) | copy-start | bytes 393220
  31.5 11.9 %copy-start.5 = (bf16[512,512]{1,0:T(8,128)(2,1)S(1)}, bf16[512,512]{1,0:T(8,128)(2,1)}, u32[]{:S(2)}) copy-start(bf16[512,512]{1,0:T(8,128)(2,1)} %param.15) | copy-start | bytes 1572868
  31.5 12.3 %copy-start.22 = (f32[512]{0:T(512)S(1)}, f32[512]{0:T(512)}, u32[]{:S(2)}) copy-start(f32[512]{0:T(512)} %param.13) | copy-start | bytes 6148
  43.8 1.2 copy-start.11
  43.8 1.2 copy-start.13
  45.5 0.7 copy-start.18
  45.5 2.3 %copy-start.20 = (bf16[128,1024]{1,0:T(8,128)(2,1)}, bf16[128,1024]{1,0:T(8,128)(2,1)S(1)}, u32[]{:S(2)}) copy-start(bf16[128,1024]{1,0:T(8,128)(2,1)S(1)} %get-tuple-element.46) | copy-start | bytes 786436
  45.6 2.7 %copy-start.12 = (bf16[128,1024]{1,0:T(8,128)(2,1)}, bf16[128,1024]{1,0:T(8,128)(2,1)S(1)}, u32[]{:S(2)}) copy-start(bf16[128,1024]{1,0:T(8,128)(2,1)S(1)} %get-tuple-element.49) | copy-start | bytes 786436
  47.8 1.5 copy-start.15
  49.5 2.7 %copy-start.7 = (bf16[128,512]{1,0:T(8,128)(2,1)}, bf16[128,512]{1,0:T(8,128)(2,1)S(1)}, u32[]{:S(2)}) copy-start(bf16[128,512]{1,0:T(8,128)(2,1)S(1)} %add_convert_fusion) | copy-start | bytes 393220
  50.6 4.2 %copy-start.19 = (bf16[128,1024]{1,0:T(8,128)(2,1)S(1)}, bf16[128,1024]{1,0:T(8,128)(2,1)}, u32[]{:S(2)}) copy-start(bf16[128,1024]{1,0:T(8,128)(2,1)} %copy-done.18) | copy-start | bytes 786436
  50.6 4.2 %copy-start.21 = (bf16[128,1024]{1,0:T(8,128)(2,1)S(1)}, bf16[128,1024]{1,0:T(8,128)(2,1)}, u32[]{:S(2)}) copy-start(bf16[128,1024]{1,0:T(8,128)(2,1)} %copy-done.20) | copy-start | bytes 786436
  52.2 1.1 copy-start.2
  54.3 14.9 %collective-permute-start.1 = (bf16[2,2,2,32,1536]{4,3,2,1,0:T(8,128)(2,1)}, bf16[2,2,2,32,1536]{4,3,2,1,0:T(8,128)(2,1)}, u32[]{:S(2)}, u32[]{:S(2)}) collective-permute-start(bf16[2,2,2,32,1536]{4,3,2,1,0:T(8,128)(2,1)} %dynamic-slice_bitcast_fusion), channel_id=1, source_target_pairs={{0,1},{1,0},{2,3},{3,2},{4,5},{5,4},{6,7},{7,6},{8,9},{9,8},{10,11... | collective-permute-start | bytes 2359304 | tf_op jit(solution)/shard_map/ppermute | solution.py:241
  59.7 1.2 copy-start.6
  59.7 1.3 copy-start.8
  60.7 11.0 %collective-permute-start = (bf16[2,2,2,32,2048]{4,3,0,1,2:T(8,128)(2,1)}, bf16[2,2,2,32,2048]{4,3,0,1,2:T(8,128)(2,1)}, u32[]{:S(2)}, u32[]{:S(2)}) collective-permute-start(bf16[2,2,2,32,2048]{4,3,0,1,2:T(8,128)(2,1)} %bitcast.106), channel_id=1, source_target_pairs={{0,1},{1,0},{2,3},{3,2},{4,5},{5,4},{6,7},{7,6},{8,9},{9,8},{10,11... | collective-permute-start | bytes 3145736 | tf_op jit(solution)/shard_map/ppermute | solution.py:241
  63.6 13.4 %all-to-all-start = ((bf16[16,32,128]{2,1,0:T(8,128)(2,1)}), bf16[16,32,128]{2,1,0:T(8,128)(2,1)S(1)}, u32[]{:S(2)}, u32[]{:S(2)}) async-start(bf16[16,32,128]{2,1,0:T(8,128)(2,1)} %bitcast.15), calls=%async_computation | async-start | bytes 262144 | tf_op jit(solution)/shard_map/all_to_all | solution.py:227
  69.2 2.6 %copy-start.3 = (bf16[2,2,2,1,32,2048]{5,4,3,2,1,0:T(8,128)(2,1)S(1)}, bf16[2,2,2,1,32,2048]{5,4,3,2,1,0:T(8,128)(2,1)}, u32[]{:S(2)}) copy-start(bf16[2,2,2,1,32,2048]{5,4,3,2,1,0:T(8,128)(2,1)} %get-tuple-element.41) | copy-start | bytes 3145732
  78.8 13.0 %collective-permute-start.3 = (bf16[2,2,32,1536]{3,2,1,0:T(8,128)(2,1)}, bf16[2,2,32,1536]{3,2,1,0:T(8,128)(2,1)}, u32[]{:S(2)}, u32[]{:S(2)}) collective-permute-start(bf16[2,2,32,1536]{3,2,1,0:T(8,128)(2,1)} %dynamic-slice_bitcast_fusion.2), channel_id=1, source_target_pairs={{0,4},{1,5},{2,6},{3,7},{4,0},{5,1},{6,2},{7,3},{8,12},{9,13},{10,... | collective-permute-start | bytes 1179656 | tf_op jit(solution)/shard_map/ppermute | solution.py:241
  80.7 13.9 %collective-permute-start.2 = (bf16[2,2,32,2048]{3,2,0,1:T(8,128)(2,1)}, bf16[2,2,32,2048]{3,2,0,1:T(8,128)(2,1)}, u32[]{:S(2)}, u32[]{:S(2)}) collective-permute-start(bf16[2,2,32,2048]{3,2,0,1:T(8,128)(2,1)} %dynamic-slice_bitcast_fusion.1), channel_id=1, source_target_pairs={{0,2},{1,3},{2,0},{3,1},{4,6},{5,7},{6,4},{7,5},{8,10},{9,11},{10,... | collective-permute-start | bytes 1572872 | tf_op jit(solution)/shard_map/ppermute | solution.py:241
  96.8 18.0 %all-to-all-start.1 = ((bf16[16,112,128]{2,1,0:T(8,128)(2,1)}), bf16[16,112,128]{2,1,0:T(8,128)(2,1)}, u32[]{:S(2)}, u32[]{:S(2)}) async-start(bf16[16,112,128]{2,1,0:T(8,128)(2,1)} %pad_maximum_fusion.2), calls=%async_computation.1 | async-start | bytes 917504 | tf_op jit(solution)/shard_map/all_to_all | solution.py:227
  105.2 21.5 %collective-permute-start.4 = (bf16[2,32,1536]{2,1,0:T(8,128)(2,1)}, bf16[2,32,1536]{2,1,0:T(8,128)(2,1)}, u32[]{:S(2)}, u32[]{:S(2)}) collective-permute-start(bf16[2,32,1536]{2,1,0:T(8,128)(2,1)} %dynamic-slice_bitcast_fusion.4), channel_id=1, source_target_pairs={{0,8},{1,9},{2,10},{3,11},{4,12},{5,13},{6,14},{7,15},{8,0},{9,1},... | collective-permute-start | bytes 589832 | tf_op jit(solution)/shard_map/ppermute | solution.py:241
  108.4 9.3 %copy-start.23 = (f32[512]{0:T(512)S(1)}, f32[512]{0:T(512)}, u32[]{:S(2)}) copy-start(f32[512]{0:T(512)} %param.12) | copy-start | bytes 6148
  108.4 47.5 %collective-permute-start.6 = (bf16[2,32,2048]{2,1,0:T(8,128)(2,1)}, bf16[2,32,2048]{2,1,0:T(8,128)(2,1)}, u32[]{:S(2)}, u32[]{:S(2)}) collective-permute-start(bf16[2,32,2048]{2,1,0:T(8,128)(2,1)} %dynamic-slice_bitcast_fusion.3), channel_id=1, source_target_pairs={{0,4},{1,5},{2,6},{3,7},{4,0},{5,1},{6,2},{7,3},{8,12},{9,13},{10,... | collective-permute-start | bytes 786440 | tf_op jit(solution)/shard_map/ppermute | solution.py:241
  114.8 1.6 copy-start.1
  117.7 3.6 %copy-start.17 = (f32[32,512]{1,0:T(8,128)S(1)}, f32[32,512]{1,0:T(8,128)}, u32[]{:S(2)}) copy-start(f32[32,512]{1,0:T(8,128)} %copy-done.16) | copy-start | bytes 196612
  119.6 3.5 %copy-start.25 = (s32[128]{0:T(128)S(1)}, s32[128]{0:T(128)}, u32[]{:S(2)}) copy-start(s32[128]{0:T(128)} %param.20) | copy-start | bytes 1540
  125.1 1.6 copy-start.10
  127.9 29.1 %copy-start.9 = (bf16[128,512]{1,0:T(8,128)(2,1)S(1)}, bf16[128,512]{1,0:T(8,128)(2,1)}, u32[]{:S(2)}) copy-start(bf16[128,512]{1,0:T(8,128)(2,1)} %copy-done.7) | copy-start | bytes 393220
  127.9 29.1 %copy-start.14 = (f32[128,512]{1,0:T(8,128)S(1)}, f32[128,512]{1,0:T(8,128)}, u32[]{:S(2)}) copy-start(f32[128,512]{1,0:T(8,128)} %get-tuple-element.61) | copy-start | bytes 786436
  153.5 5.8 %collective-permute-start.5 = (bf16[32,1536]{1,0:T(8,128)(2,1)S(1)}, bf16[32,1536]{1,0:T(8,128)(2,1)S(1)}, u32[]{:S(2)}, u32[]{:S(2)}) collective-permute-start(bf16[32,1536]{1,0:T(8,128)(2,1)S(1)} %dynamic-slice_bitcast_fusion.6), channel_id=1, source_target_pairs={{0,2},{1,3},{2,0},{3,1},{4,6},{5,7},{6,4},{7,5},{8,10},{9,11},{10,... | collective-permute-start | bytes 294920 | tf_op jit(solution)/shard_map/ppermute | solution.py:241
  159.3 6.5 %collective-permute-start.7 = (bf16[32,2048]{1,0:T(8,128)(2,1)S(1)}, bf16[32,2048]{1,0:T(8,128)(2,1)S(1)}, u32[]{:S(2)}, u32[]{:S(2)}) collective-permute-start(bf16[32,2048]{1,0:T(8,128)(2,1)S(1)} %dynamic-slice_bitcast_fusion.5), channel_id=1, source_target_pairs={{0,8},{1,9},{2,10},{3,11},{4,12},{5,13},{6,14},{7,15},{8,0},{9,1},... | collective-permute-start | bytes 393224 | tf_op jit(solution)/shard_map/ppermute | solution.py:241

commit v6 on v5

--- a/solution.py
+++ b/solution.py
@@ -331,21 +331,22 @@
     )(sums, list_rows, qkv_heads)
 
 
-def fold_kernel(orders, *refs):
+def fold_kernel(orders, bits, *refs):
     me = lax.axis_index("seq")
-    steps = len(orders[0])
-    inputs, outputs, scratch = refs[:2], refs[2:4], refs[4:-2]
+    streams = range(len(orders))
+    count = len(orders)
+    inputs, outputs = refs[:count], refs[count : 2 * count]
+    scratch = list(refs[2 * count : -2])
     send, recv = refs[-2:]
-    landing = (scratch[:steps], scratch[steps : 2 * steps])
-    rest = scratch[2 * steps :]
-    held = (rest[: steps - 1], rest[steps - 1 :])
+    landing = [[scratch.pop(0) for _ in order] for order in orders]
+    held = [[scratch.pop(0) for _ in order[1:]] for order in orders]
 
     def partner(bit):
         return me + (1 << bit) * (1 - 2 * ((me // (1 << bit)) % 2))
 
     def half(stream, step, theirs):
         bit = orders[stream][step]
-        left = sorted(set(range(steps)) - set(orders[stream][:step]), reverse=True)
+        left = sorted(orders[stream][step:], reverse=True)
         mine = (me // (1 << bit)) % 2
         index = (slice(None),) * left.index(bit) + (1 - mine if theirs else mine,)
         return (inputs[stream] if step == 0 else held[stream][step - 1]), index
@@ -362,65 +363,62 @@
         )
 
     barrier = pltpu.get_barrier_semaphore()
-    for bit in range(steps):
+    for bit in range(bits):
         pl.semaphore_signal(
             barrier,
             inc=1,
             device_id={"seq": partner(bit)},
             device_id_type=pl.DeviceIdType.MESH,
         )
-    pl.semaphore_wait(barrier, steps)
-    for stream in range(2):
+    pl.semaphore_wait(barrier, bits)
+    for stream in streams:
         copy(stream, 0).start()
-    for step in range(steps):
-        for stream in range(2):
+    for step in range(bits):
+        for stream in streams:
+            last = len(orders[stream]) - 1
+            if step > last:
+                continue
             copy(stream, step).wait_recv()
             source, index = half(stream, step, False)
             total = source[index].astype(jnp.float32) + landing[stream][step][...].astype(
                 jnp.float32
             )
-            if step == steps - 1:
+            if step == last:
                 outputs[stream][...] = total
             else:
                 held[stream][step][...] = total.astype(jnp.bfloat16)
                 copy(stream, step + 1).start()
-    for step in range(steps):
-        for stream in range(2):
+    for stream in streams:
+        for step in range(len(orders[stream])):
             copy(stream, step).wait_send()
 
 
-def fold(one, two):
-    size = one.shape[0]
-    steps = size.bit_length() - 1
-    orders = ([0, 1] + list(range(2, steps)), [0] + list(range(2, steps)) + [1])
+def fold(arrays, orders, bits):
+    count = len(arrays)
     vmem = pl.BlockSpec(memory_space=pltpu.VMEM)
-    blocks = [as_bits(one)[0], as_bits(two)[0]]
-    tails = [one.shape[1:], two.shape[1:]]
-    landing = [
-        pltpu.VMEM((2,) * (steps - 1 - step) + tail, jnp.bfloat16)
-        for tail in tails
-        for step in range(steps)
-    ]
-    held = [
-        pltpu.VMEM((2,) * (steps - 1 - step) + tail, jnp.bfloat16)
-        for tail in tails
-        for step in range(steps - 1)
-    ]
+    tails = [array.shape[len(order) :] for array, order in zip(arrays, orders)]
+    landing, held = [], []
+    for tail, order in zip(tails, orders):
+        shapes = [(2,) * (len(order) - 1 - step) + tail for step in range(len(order))]
+        landing += [pltpu.VMEM(shape, jnp.bfloat16) for shape in shapes]
+        held += [pltpu.VMEM(shape, jnp.bfloat16) for shape in shapes[:-1]]
     return pl.pallas_call(
-        functools.partial(fold_kernel, orders),
+        functools.partial(fold_kernel, orders, bits),
         out_shape=tuple(jax.ShapeDtypeStruct(tail, jnp.float32) for tail in tails),
-        in_specs=[vmem, vmem],
-        out_specs=(vmem, vmem),
+        in_specs=[vmem] * count,
+        out_specs=(vmem,) * count,
         scratch_shapes=landing
         + held
-        + [pltpu.SemaphoreType.DMA((2, steps)), pltpu.SemaphoreType.DMA((2, steps))],
+        + [pltpu.SemaphoreType.DMA((count, bits)), pltpu.SemaphoreType.DMA((count, bits))],
         compiler_params=pltpu.CompilerParams(
             vmem_limit_bytes=VMEM_BYTES, collective_id=2, has_side_effects=True
         ),
         cost_estimate=pl.CostEstimate(
-            flops=one.size, bytes_accessed=8 * (one.size + two.size), transcendentals=0
-        ),
-    )(*blocks)
+            flops=arrays[0].size,
+            bytes_accessed=8 * sum(array.size for array in arrays),
+            transcendentals=0,
+        ),
+    )(*arrays)
 
 
 def on_device(
@@ -599,10 +597,10 @@
     per_part = inv_vn * (d_virtual - unit_vn * inner_vn) / counts
     grad_qkv_local = jnp.einsum("rd,cr->dc", normed, d_qkv_t, preferred_element_type=jnp.float32)
     late = grad_qkv_local.astype(jnp.bfloat16).reshape(seq_size, share, -1)
-    for step, bit in enumerate(one_order):
-        one, one_left = halve(one, one_left, bit, late if step == 0 else None)
-    for step, bit in enumerate(two_order):
-        two, two_left = halve(two, two_left, bit, late if step == 0 else None)
+    for bit in one_order[:-1]:
+        one, one_left = halve(one, one_left, bit, late)
+    for bit in two_order[:-1]:
+        two, two_left = halve(two, two_left, bit, late)
     d_normed = jnp.einsum(
         "cr,dc->rd", d_qkv_t, query_key_value_weight, preferred_element_type=jnp.float32
     )
@@ -624,11 +622,17 @@
     middle = late.shape[2] // 2
     late_one = late[:, :, :middle]
     late_two = jnp.concatenate([late[:, :, middle:], gain_block], axis=2)
+    late_one, first_left = as_bits(late_one)
+    late_two, second_left = as_bits(late_two)
     if share % 16 == 0:
-        late_one, late_two = fold(late_one, late_two)
+        one, two, late_one, late_two = fold(
+            [one, two, late_one, late_two],
+            [one_left, two_left, [0, 1] + outer, [0] + outer + [1]],
+            bits,
+        )
     else:
-        late_one, first_left = as_bits(late_one)
-        late_two, second_left = as_bits(late_two)
+        one, one_left = halve(one, one_left, one_left[0])
+        two, two_left = halve(two, two_left, two_left[0])
         for bit in [0, 1] + outer:
             late_one, first_left = halve(late_one, first_left, bit)
             late_two, second_left = halve(late_two, second_left, bit)

time: 168 us -> 157 us (0.935)
  waiting for transfers between devices: 13.6 us -> 9.87 us
  matrix products: 21.1 us -> 17.6 us
  local copies, waits for them, and re-layouts: 26.2 us -> 22.8 us
  starting transfers between devices: 17.5 us -> 14.9 us
  Pallas kernels: 67.6 us -> 69.5 us
    ppermute x8 -> x6, waiting for transfers between devices: 6.09 us -> 2.46 us  [halve(): got = lax.ppermute(send, 'seq', [(i, i ^ 1 << bit) for i in range(size)])]
    ppermute x8 -> x6, starting transfers between devices: 7.61 us -> 5.43 us  [halve(): got = lax.ppermute(send, 'seq', [(i, i ^ 1 << bit) for i in range(size)])]
    pallas_call x1, Pallas kernels: 25.6 us -> 27.5 us  [fold(): pl.pallas_call(functools.partial(fold_kernel, orders, bits), out_shape=tu...]
    squeeze x7 -> x4, local copies, waits for them, and re-layouts: 7.02 us -> 6.03 us  [halve(): send = lax.dynamic_index_in_dim(held, 1 - mine, axis, keepdims=False)]
    unnamed x54 -> x72, local copies, waits for them, and re-layouts: 5.88 us -> 6.56 us
  transfers between devices with their start and end apart: 10 -> 8, of which waited for: 4 -> 4; matrix products, arithmetic and copies ran while one was open for 24% -> 16% of each run, Pallas kernels for 22% -> 7%
where the time goes in v6:
time: 157 us; the launch traced here: 156 us
  Pallas kernels  69.5 us (44%)
  local copies, waits for them, and re-layouts  22.8 us (15%)
  other arithmetic  19.4 us (12%)
  matrix products  17.6 us (11%)
  starting transfers between devices  14.9 us (9%)
  waiting for transfers between devices  9.87 us (6%)
  between operations  2.1 us (1%)
    pallas_call x1, Pallas kernels, fold(): pl.pallas_call(functools.partial(fold_kernel, orders, bits), out_shape=tu...  27.5 us
    pallas_call x1, Pallas kernels, exchange(): pl.pallas_call(functools.partial(exchange_kernel, slices), out_shape=(jax...  19.8 us
    pallas_call x1, Pallas kernels, attention_forward(): pl.pallas_call(functools.partial(forward_kernel, head_dim, slices, size),...  11.9 us
    convert_element_type x6, other arithmetic, halve(): return (total if not rest else total.astype(jnp.bfloat16), rest)  10.5 us
    pallas_call x1, Pallas kernels, attention_backward(): pl.pallas_call(functools.partial(backward_kernel, head_dim), out_shape=(j...  10.3 us
    all_to_all x2, starting transfers between devices, all_to_all(): lax.all_to_all(blocks, 'seq', split_axis=0, concat_axis=0, tiled=True)  9.47 us
    all_to_all x2, waiting for transfers between devices, all_to_all(): lax.all_to_all(blocks, 'seq', split_axis=0, concat_axis=0, tiled=True)  7.41 us
    unnamed x72, local copies, waits for them, and re-layouts  6.56 us
  transfers between devices with their start and end apart: 8, of which 4 were waited for; matrix products, arithmetic and copies ran while one was open for 16% of the time, Pallas kernels for 7%

profile of v6, /device:TPU:0, one launch (start us, length us, event | category | flops | bytes accessed | tf_op | source)
XLA Modules:
  0.0 156.1 jit_solution(13800144953651857091)
XLA Ops:
  0.6 0.9 fusion.39
  1.6 1.0 fusion.27
  2.6 1.1 convolution_convert_fusion.6
  3.7 1.9 %convolution_convert_fusion.2 = bf16[128,1536]{1,0:T(8,128)(2,1)S(1)} fusion(bf16[512,1536]{1,0:T(8,128)(2,1)} %param.14, bf16[128,512]{1,0:T(8,128)(2,1)} %param.11, f32[512]{0:T(512)} %param.12, f32[128]{0:T(128)S(1)} %add_rsqrt_fusion.2), kind=kOutput, calls=%fused_computation.2 | convolution fusion | flops 201785344 | bytes 2099712 | tf_op jit(solution)/shard_map/dot_general | solution.py:475
  5.7 2.6 %copy.65 = bf16[512,1536]{0,1:T(8,128)(2,1)} copy(bf16[512,1536]{1,0:T(8,128)(2,1)} %param.14) | data formatting | bytes 3145728 | tf_op args[3]
  9.7 19.8 %shard_map.162 = (bf16[16,96,128]{2,1,0:T(8,128)(2,1)S(1)}, bf16[16,16,128]{2,1,0:T(8,128)(2,1)S(1)}) custom-call(bf16[16,16,128]{2,1,0:T(8,128)(2,1)S(1)} %maximum_maximum_fusion.sums_ref, f32[16,128]{1,0:T(8,128)S(1)} %pad.8.list_ref, bf16[16,96,128]{2,1,0:T(8,128)(2,1)S(1)} %bitcast.103), custom_call_target="tpu_custom_call" | custom-call | flops 32768 | bytes 786432 | tf_op jit(solution)/shard_map/pallas_call | solution.py:311
  30.5 1.0 convolution_convert_fusion.7.virt_ref
  31.5 11.9 %shard_map.163 = bf16[16,32,128]{2,1,0:T(8,128)(2,1)S(1)} custom-call(s32[16,5]{1,0:T(8,128)S(1)} %bitcast.106, bf16[16,96,128]{2,1,0:T(8,128)(2,1)S(1)} %get-tuple-element.25.qkv_ref, bf16[2,32,32]{2,1,0:T(8,128)(2,1)S(1)} %convolution_convert_fusion.7.virt_ref), custom_call_target="tpu_custom_call" | custom-call | flops 142606336 | bytes 393216 | tf_op jit(solution)/shard_map/pallas_call | solution.py:184
  43.9 0.5 fusion.47
  44.4 0.7 copy-done.13
  45.0 0.5 multiply_convert_fusion.1
  45.6 0.7 copy-done.22
  46.3 1.5 multiply_reduce_fusion
  47.8 0.5 convolution_convert_fusion.3
  48.3 1.1 fusion.53
  49.5 1.1 convolution_convert_fusion.4
  50.6 1.5 pad_maximum_fusion
  52.1 1.0 constant_dynamic-slice_fusion.1
  53.2 0.9 copy.98
  54.1 0.5 collective-permute-start.1
  54.6 0.8 convolution_convert_fusion
  55.4 1.2 constant_dynamic-slice_fusion.3
  56.6 1.1 copy.97
  58.2 0.8 copy.69
  58.9 5.5 %all-to-all-start = ((bf16[16,32,128]{2,1,0:T(8,128)(2,1)}), bf16[16,32,128]{2,1,0:T(8,128)(2,1)S(1)}, u32[]{:S(2)}, u32[]{:S(2)}) async-start(bf16[16,32,128]{2,1,0:T(8,128)(2,1)} %bitcast.15), calls=%async_computation | async-start | bytes 262144 | tf_op jit(solution)/shard_map/all_to_all | solution.py:227
  64.5 2.5 %fusion.2 = bf16[2,2,2,32,1536]{4,3,2,0,1:T(8,128)(2,1)} fusion(bf16[2,2,2,32,1536]{4,3,2,0,1:T(8,128)(2,1)} %collective-permute-done.1, bf16[2,2,2,1,32,1536]{5,4,3,2,1,0:T(8,128)(2,1)} %get-tuple-element.49), kind=kLoop, calls=%fused_computation.9 | loop fusion | flops 1572864 | bytes 2359296 | tf_op jit(solution)/shard_map/convert_element_type | solution.py:246
  67.0 2.6 %fusion = bf16[2,2,2,32,2048]{4,3,0,1,2:T(8,128)(2,1)} fusion(bf16[2,2,2,32,2048]{4,3,0,1,2:T(8,128)(2,1)} %collective-permute-done, bf16[2,2,2,1,32,2048]{5,4,3,2,1,0:T(8,128)(2,1)S(1)} %copy-done.2), kind=kLoop, calls=%fused_computation.4 | loop fusion | flops 2097152 | bytes 3145728 | tf_op jit(solution)/shard_map/convert_element_type | solution.py:246
  69.7 2.7 %all-to-all-done.grad_ref = bf16[16,32,128]{2,1,0:T(8,128)(2,1)S(1)} async-done(((bf16[16,32,128]{2,1,0:T(8,128)(2,1)}), bf16[16,32,128]{2,1,0:T(8,128)(2,1)S(1)}, u32[]{:S(2)}, u32[]{:S(2)}) %all-to-all-start) | async-done | bytes 131104 | tf_op jit(solution)/shard_map/all_to_all | solution.py:227
  72.4 1.8 %dynamic-slice_bitcast_fusion.1 = bf16[2,2,32,1536]{3,2,1,0:T(8,128)(2,1)} fusion(bf16[2,2,2,32,1536]{4,3,2,0,1:T(8,128)(2,1)} %fusion.2, s32[]{:T(128)S(6)} %select_n.96), kind=kLoop, calls=%fused_computation.47 | loop fusion | bytes 786436 | tf_op jit(solution)/shard_map/jit(dynamic_index_in_dim)/squeeze | solution.py:240
  74.2 1.9 %dynamic-slice_bitcast_fusion = bf16[2,2,32,2048]{3,2,0,1:T(8,128)(2,1)} fusion(bf16[2,2,2,32,2048]{4,3,0,1,2:T(8,128)(2,1)} %fusion, s32[]{:T(128)S(6)} %select_n.92), kind=kLoop, calls=%fused_computation.37 | loop fusion | bytes 1048580 | tf_op jit(solution)/shard_map/jit(dynamic_index_in_dim)/squeeze | solution.py:240
  76.0 0.6 collective-permute-start.2
  76.7 10.3 %shard_map.164 = (bf16[16,32,128]{2,1,0:T(8,128)(2,1)S(1)}, bf16[16,64,128]{2,1,0:T(8,128)(2,1)S(1)}, f32[64,32]{1,0:T(8,128)S(1)}) custom-call(s32[16,5]{1,0:T(8,128)S(1)} %bitcast.107, bf16[16,96,128]{2,1,0:T(8,128)(2,1)S(1)} %get-tuple-element.25.qkv_ref, bf16[2,32,32]{2,1,0:T(8,128)(2,1)S(1)} %convolution_convert_fusion.7.virt_ref, ...), custom_call_target="tpu_custom_call" | custom-call | flops 356515840 | bytes 1179648 | tf_op jit(solution)/shard_map/pallas_call | solution.py:209
  87.1 1.2 fusion.11
  88.3 1.6 %collective-permute-done.2 = bf16[2,2,32,2048]{3,2,0,1:T(8,128)(2,1)} collective-permute-done((bf16[2,2,32,2048]{3,2,0,1:T(8,128)(2,1)}, bf16[2,2,32,2048]{3,2,0,1:T(8,128)(2,1)}, u32[]{:S(2)}, u32[]{:S(2)}) %collective-permute-start.2) | collective-permute-done | bytes 524320 | tf_op jit(solution)/shard_map/ppermute | solution.py:241
  89.9 2.1 %fusion.7 = bf16[2,2,32,2048]{3,2,0,1:T(8,128)(2,1)} fusion(bf16[2,2,32,2048]{3,2,0,1:T(8,128)(2,1)} %collective-permute-done.2, bf16[2,2,2,32,2048]{4,3,0,1,2:T(8,128)(2,1)} %fusion, s32[]{:T(128)S(6)} %select_n.91), kind=kLoop, calls=%fused_computation.25 | loop fusion | flops 1048576 | bytes 1572868 | tf_op jit(solution)/shard_map/convert_element_type | solution.py:246
  92.1 0.8 pad_maximum_fusion.2
  92.9 4.0 %all-to-all-start.1 = ((bf16[16,112,128]{2,1,0:T(8,128)(2,1)}), bf16[16,112,128]{2,1,0:T(8,128)(2,1)S(1)}, u32[]{:S(2)}, u32[]{:S(2)}) async-start(bf16[16,112,128]{2,1,0:T(8,128)(2,1)} %pad_maximum_fusion.2), calls=%async_computation.1 | async-start | bytes 917504 | tf_op jit(solution)/shard_map/all_to_all | solution.py:227
  97.0 2.3 %fusion.5 = bf16[128,512]{1,0:T(8,128)(2,1)} fusion(f32[128,512]{1,0:T(8,128)S(1)} %get-tuple-element.63, bf16[128,1024]{1,0:T(8,128)(2,1)} %copy-done.14, bf16[1024,512]{1,0:T(8,128)(2,1)} %param.17), kind=kOutput, calls=%fused_computation.18 | convolution fusion | flops 134348800 | bytes 1703936 | tf_op jit(solution)/shard_map/dot_general | solution.py:519
  99.2 1.7 %dynamic-slice_bitcast_fusion.2 = bf16[2,32,2048]{2,1,0:T(8,128)(2,1)} fusion(bf16[2,2,32,2048]{3,2,0,1:T(8,128)(2,1)} %fusion.7, s32[]{:T(128)S(6)} %select_n.96), kind=kLoop, calls=%fused_computation.64 | loop fusion | bytes 524292 | tf_op jit(solution)/shard_map/jit(dynamic_index_in_dim)/squeeze | solution.py:240
  100.9 1.9 %collective-permute-start.4 = (bf16[2,32,2048]{2,1,0:T(8,128)(2,1)}, bf16[2,32,2048]{2,1,0:T(8,128)(2,1)}, u32[]{:S(2)}, u32[]{:S(2)}) collective-permute-start(bf16[2,32,2048]{2,1,0:T(8,128)(2,1)} %dynamic-slice_bitcast_fusion.2), channel_id=1, source_target_pairs={{0,4},{1,5},{2,6},{3,7},{4,0},{5,1},{6,2},{7,3},{8,12},{9,13},{10,... | collective-permute-start | bytes 786440 | tf_op jit(solution)/shard_map/ppermute | solution.py:241
  102.8 0.7 dynamic-slice_bitcast_fusion.3
  103.5 2.4 %collective-permute-start.5 = (bf16[2,32,1536]{2,1,0:T(8,128)(2,1)}, bf16[2,32,1536]{2,1,0:T(8,128)(2,1)}, u32[]{:S(2)}, u32[]{:S(2)}) collective-permute-start(bf16[2,32,1536]{2,1,0:T(8,128)(2,1)} %dynamic-slice_bitcast_fusion.3), channel_id=1, source_target_pairs={{0,8},{1,9},{2,10},{3,11},{4,12},{5,13},{6,14},{7,15},{8,0},{9,1},... | collective-permute-start | bytes 589832 | tf_op jit(solution)/shard_map/ppermute | solution.py:241
  105.9 4.7 %all-to-all-done.1 = bf16[16,112,128]{2,1,0:T(8,128)(2,1)S(1)} async-done(((bf16[16,112,128]{2,1,0:T(8,128)(2,1)}), bf16[16,112,128]{2,1,0:T(8,128)(2,1)S(1)}, u32[]{:S(2)}, u32[]{:S(2)}) %all-to-all-start.1) | async-done | bytes 458784 | tf_op jit(solution)/shard_map/all_to_all | solution.py:227
  110.7 0.4 copy.78
  111.5 1.8 %multiply_reduce_fusion.3 = (f32[32]{0:T(128)S(1)}, f32[32,512]{1,0:T(8,128)S(1)}) fusion(f32[32]{0:T(128)S(1)} %add_rsqrt_fusion.1, f32[32,512]{1,0:T(8,128)S(1)} %reshape.191, f32[32]{0:T(128)S(1)} %div.76, bf16[1024,32]{0,1:T(8,128)(2,1)S(1)} %reshape.197, bf16[512,1536]{1,0:T(8,128)(2,1)} %param.14), kind=kOutput, calls=%fused_computation.80 | convolution fusion | flops 33619936 | bytes 1245568 | tf_op jit(solution)/shard_map/sp,ds->pd/dot_general | solution.py:593
  113.4 0.7 convolution_convert_fusion.1
  114.1 1.1 fusion.52
  115.2 0.6 copy-done.1
  115.8 0.6 fusion.56
  116.5 0.8 collective-permute-done.4
  117.3 1.0 fusion.12.refs_0_
  118.3 1.6 %fusion.26 = (bf16[512]{0:T(512)(128)(2,1)}, f32[128]{0:T(128)S(1)}, f32[128,512]{1,0:T(8,128)}) fusion(bf16[128,512]{1,0:T(8,128)(2,1)S(1)} %copy-done.4, f32[128]{0:T(128)S(1)} %add_rsqrt_fusion.2, f32[512]{0:T(512)S(1)} %copy-done.28, f32[128,512]{1,0:T(8,128)S(1)} %fusion.56, f32[32,512]{1,0:T(8,128)S(1)} %get-tuple-element.66, ...), kind=kOutput, calls=%fused_computation.61 | convolution fusion | flops 25791872 | bytes 791424 | tf_op jit(solution)/shard_map/dot_general | solution.py:607
  120.0 0.5 broadcast_multiply_fusion.1
  120.5 0.8 concatenate.73
  121.3 1.0 fusion.14.refs_1_
  122.3 1.2 fusion.10
  123.6 27.5 %shard_map.165 = (f32[32,2048]{1,0:T(8,128)S(1)}, f32[32,1536]{1,0:T(8,128)S(1)}, f32[32,768]{1,0:T(8,128)S(1)}, f32[32,896]{1,0:T(8,128)S(1)}) custom-call(bf16[2,32,2048]{2,1,0:T(8,128)(2,1)S(1)} %fusion.12.refs_0_, bf16[2,32,1536]{2,1,0:T(8,128)(2,1)S(1)} %fusion.14.refs_1_, bf16[2,2,2,2,32,768]{5,4,3,2,1,0:T(8,128)(2,1)S(1)} %bitcast.102, ...), custom_call_target="tpu_custom_call" | custom-call | flops 131072 | bytes 8650752 | tf_op jit(solution)/shard_map/pallas_call | solution.py:405
  151.1 0.5 slice_bitcast_fusion
  151.6 1.0 convolution_add_fusion.3
  152.6 0.6 fusion.55
  153.2 0.8 fusion.25
  154.1 0.7 pad_maximum_fusion.6
  154.8 0.7 pad_maximum_fusion.8
  155.4 0.7 copy.101
  (115 shorter events, 3.4 us)
Async XLA Ops:
  0.6 43.2 %copy-start = (bf16[512,2048]{1,0:T(8,128)(2,1)S(1)}, bf16[512,2048]{1,0:T(8,128)(2,1)}, u32[]{:S(2)}) copy-start(bf16[512,2048]{1,0:T(8,128)(2,1)} %param.16) | copy-start | bytes 6291460
  5.7 3.8 %copy-start.32 = (s32[1,4]{1,0:T(1,128)S(1)}, s32[1,4]{1,0:T(1,128)}, u32[]{:S(2)}) copy-start(s32[1,4]{1,0:T(1,128)} %param.18) | copy-start | bytes 52
  30.3 81.2 %copy-start.29 = (f32[32]{0:T(128)}, f32[32]{0:T(128)S(1)}, u32[]{:S(2)}) copy-start(f32[32]{0:T(128)S(1)} %add_rsqrt_fusion.1) | copy-start | bytes 388
  30.3 81.2 %copy-start.20 = (f32[32,512]{1,0:T(8,128)}, f32[32,512]{1,0:T(8,128)S(1)}, u32[]{:S(2)}) copy-start(f32[32,512]{1,0:T(8,128)S(1)} %reshape.191) | copy-start | bytes 196612
  30.5 1.0 copy-start.26
  31.5 11.9 %copy-start.3 = (bf16[128,512]{1,0:T(8,128)(2,1)S(1)}, bf16[128,512]{1,0:T(8,128)(2,1)}, u32[]{:S(2)}) copy-start(bf16[128,512]{1,0:T(8,128)(2,1)} %param.11) | copy-start | bytes 393220
  31.5 11.9 %copy-start.6 = (bf16[512,512]{1,0:T(8,128)(2,1)S(1)}, bf16[512,512]{1,0:T(8,128)(2,1)}, u32[]{:S(2)}) copy-start(bf16[512,512]{1,0:T(8,128)(2,1)} %param.15) | copy-start | bytes 1572868
  31.5 12.3 %copy-start.27 = (f32[512]{0:T(512)S(1)}, f32[512]{0:T(512)}, u32[]{:S(2)}) copy-start(f32[512]{0:T(512)} %param.13) | copy-start | bytes 6148
  43.8 1.2 copy-start.13
  43.8 1.2 copy-start.15
  45.6 0.7 copy-start.22
  45.6 2.2 %copy-start.24 = (bf16[128,1024]{1,0:T(8,128)(2,1)}, bf16[128,1024]{1,0:T(8,128)(2,1)S(1)}, u32[]{:S(2)}) copy-start(bf16[128,1024]{1,0:T(8,128)(2,1)S(1)} %get-tuple-element.52) | copy-start | bytes 786436
  45.6 2.7 %copy-start.14 = (bf16[128,1024]{1,0:T(8,128)(2,1)}, bf16[128,1024]{1,0:T(8,128)(2,1)S(1)}, u32[]{:S(2)}) copy-start(bf16[128,1024]{1,0:T(8,128)(2,1)S(1)} %get-tuple-element.55) | copy-start | bytes 786436
  47.8 1.6 copy-start.19
  49.5 8.2 %copy-start.9 = (bf16[128,512]{1,0:T(8,128)(2,1)}, bf16[128,512]{1,0:T(8,128)(2,1)S(1)}, u32[]{:S(2)}) copy-start(bf16[128,512]{1,0:T(8,128)(2,1)S(1)} %add_convert_fusion) | copy-start | bytes 393220
  52.1 2.5 %copy-start.23 = (bf16[128,1024]{1,0:T(8,128)(2,1)S(1)}, bf16[128,1024]{1,0:T(8,128)(2,1)}, u32[]{:S(2)}) copy-start(bf16[128,1024]{1,0:T(8,128)(2,1)} %copy-done.22) | copy-start | bytes 786436
  52.1 2.5 %copy-start.25 = (bf16[128,1024]{1,0:T(8,128)(2,1)S(1)}, bf16[128,1024]{1,0:T(8,128)(2,1)}, u32[]{:S(2)}) copy-start(bf16[128,1024]{1,0:T(8,128)(2,1)} %copy-done.24) | copy-start | bytes 786436
  54.1 10.4 %collective-permute-start.1 = (bf16[2,2,2,32,1536]{4,3,2,0,1:T(8,128)(2,1)}, bf16[2,2,2,32,1536]{4,3,2,0,1:T(8,128)(2,1)}, u32[]{:S(2)}, u32[]{:S(2)}) collective-permute-start(bf16[2,2,2,32,1536]{4,3,2,0,1:T(8,128)(2,1)} %bitcast.99), channel_id=1, source_target_pairs={{0,1},{1,0},{2,3},{3,2},{4,5},{5,4},{6,7},{7,6},{8,9},{9,8},{10,11... | collective-permute-start | bytes 2359304 | tf_op jit(solution)/shard_map/ppermute | solution.py:241
  56.6 1.2 copy-start.7
  57.7 9.3 %collective-permute-start = (bf16[2,2,2,32,2048]{4,3,0,1,2:T(8,128)(2,1)}, bf16[2,2,2,32,2048]{4,3,0,1,2:T(8,128)(2,1)}, u32[]{:S(2)}, u32[]{:S(2)}) collective-permute-start(bf16[2,2,2,32,2048]{4,3,0,1,2:T(8,128)(2,1)} %bitcast.98), channel_id=1, source_target_pairs={{0,1},{1,0},{2,3},{3,2},{4,5},{5,4},{6,7},{7,6},{8,9},{9,8},{10,11... | collective-permute-start | bytes 3145736 | tf_op jit(solution)/shard_map/ppermute | solution.py:241
  58.9 13.5 %all-to-all-start = ((bf16[16,32,128]{2,1,0:T(8,128)(2,1)}), bf16[16,32,128]{2,1,0:T(8,128)(2,1)S(1)}, u32[]{:S(2)}, u32[]{:S(2)}) async-start(bf16[16,32,128]{2,1,0:T(8,128)(2,1)} %bitcast.15), calls=%async_computation | async-start | bytes 262144 | tf_op jit(solution)/shard_map/all_to_all | solution.py:227
  64.5 2.6 %copy-start.2 = (bf16[2,2,2,1,32,2048]{5,4,3,2,1,0:T(8,128)(2,1)S(1)}, bf16[2,2,2,1,32,2048]{5,4,3,2,1,0:T(8,128)(2,1)}, u32[]{:S(2)}) copy-start(bf16[2,2,2,1,32,2048]{5,4,3,2,1,0:T(8,128)(2,1)} %get-tuple-element.45) | copy-start | bytes 3145732
  74.2 12.9 %collective-permute-start.3 = (bf16[2,2,32,1536]{3,2,1,0:T(8,128)(2,1)}, bf16[2,2,32,1536]{3,2,1,0:T(8,128)(2,1)}, u32[]{:S(2)}, u32[]{:S(2)}) collective-permute-start(bf16[2,2,32,1536]{3,2,1,0:T(8,128)(2,1)} %dynamic-slice_bitcast_fusion.1), channel_id=1, source_target_pairs={{0,4},{1,5},{2,6},{3,7},{4,0},{5,1},{6,2},{7,3},{8,12},{9,13},{10,... | collective-permute-start | bytes 1179656 | tf_op jit(solution)/shard_map/ppermute | solution.py:241
  76.0 13.9 %collective-permute-start.2 = (bf16[2,2,32,2048]{3,2,0,1:T(8,128)(2,1)}, bf16[2,2,32,2048]{3,2,0,1:T(8,128)(2,1)}, u32[]{:S(2)}, u32[]{:S(2)}) collective-permute-start(bf16[2,2,32,2048]{3,2,0,1:T(8,128)(2,1)} %dynamic-slice_bitcast_fusion), channel_id=1, source_target_pairs={{0,2},{1,3},{2,0},{3,1},{4,6},{5,7},{6,4},{7,5},{8,10},{9,11},{10,... | collective-permute-start | bytes 1572872 | tf_op jit(solution)/shard_map/ppermute | solution.py:241
  88.3 14.5 %copy-start.11 = (bf16[2,2,32,1536]{3,2,1,0:T(8,128)(2,1)}, bf16[2,2,32,1536]{3,2,1,0:T(8,128)(2,1)S(1)}, u32[]{:S(2)}) copy-start(bf16[2,2,32,1536]{3,2,1,0:T(8,128)(2,1)S(1)} %fusion.11) | copy-start | bytes 1179652
  92.9 17.7 %all-to-all-start.1 = ((bf16[16,112,128]{2,1,0:T(8,128)(2,1)}), bf16[16,112,128]{2,1,0:T(8,128)(2,1)S(1)}, u32[]{:S(2)}, u32[]{:S(2)}) async-start(bf16[16,112,128]{2,1,0:T(8,128)(2,1)} %pad_maximum_fusion.2), calls=%async_computation.1 | async-start | bytes 917504 | tf_op jit(solution)/shard_map/all_to_all | solution.py:227
  100.9 16.4 %collective-permute-start.4 = (bf16[2,32,2048]{2,1,0:T(8,128)(2,1)}, bf16[2,32,2048]{2,1,0:T(8,128)(2,1)}, u32[]{:S(2)}, u32[]{:S(2)}) collective-permute-start(bf16[2,32,2048]{2,1,0:T(8,128)(2,1)} %dynamic-slice_bitcast_fusion.2), channel_id=1, source_target_pairs={{0,4},{1,5},{2,6},{3,7},{4,0},{5,1},{6,2},{7,3},{8,12},{9,13},{10,... | collective-permute-start | bytes 786440 | tf_op jit(solution)/shard_map/ppermute | solution.py:241
  103.5 17.0 %collective-permute-start.5 = (bf16[2,32,1536]{2,1,0:T(8,128)(2,1)}, bf16[2,32,1536]{2,1,0:T(8,128)(2,1)}, u32[]{:S(2)}, u32[]{:S(2)}) collective-permute-start(bf16[2,32,1536]{2,1,0:T(8,128)(2,1)} %dynamic-slice_bitcast_fusion.3), channel_id=1, source_target_pairs={{0,8},{1,9},{2,10},{3,11},{4,12},{5,13},{6,14},{7,15},{8,0},{9,1},... | collective-permute-start | bytes 589832 | tf_op jit(solution)/shard_map/ppermute | solution.py:241
  110.7 2.7 %copy-start.28 = (f32[512]{0:T(512)S(1)}, f32[512]{0:T(512)}, u32[]{:S(2)}) copy-start(f32[512]{0:T(512)} %param.12) | copy-start | bytes 6148
  111.5 2.6 %copy-start.17 = (bf16[1024,32]{0,1:T(8,128)(2,1)}, bf16[1024,32]{0,1:T(8,128)(2,1)S(1)}, u32[]{:S(2)}) copy-start(bf16[1024,32]{0,1:T(8,128)(2,1)S(1)} %reshape.197) | copy-start | bytes 196612
  114.1 1.7 %copy-start.1 = (bf16[512,1536]{1,0:T(8,128)(2,1)S(1)}, bf16[512,1536]{1,0:T(8,128)(2,1)}, u32[]{:S(2)}) copy-start(bf16[512,1536]{1,0:T(8,128)(2,1)} %param.14) | copy-start | bytes 4718596
  115.8 1.5 copy-start.8
  115.8 2.5 %copy-start.4 = (bf16[128,512]{1,0:T(8,128)(2,1)S(1)}, bf16[128,512]{1,0:T(8,128)(2,1)}, u32[]{:S(2)}) copy-start(bf16[128,512]{1,0:T(8,128)(2,1)} %param.11) | copy-start | bytes 393220
  115.8 2.5 %copy-start.21 = (f32[32,512]{1,0:T(8,128)S(1)}, f32[32,512]{1,0:T(8,128)}, u32[]{:S(2)}) copy-start(f32[32,512]{1,0:T(8,128)} %copy-done.20) | copy-start | bytes 196612
  115.8 2.5 %copy-start.30 = (f32[32]{0:T(128)S(1)}, f32[32]{0:T(128)}, u32[]{:S(2)}) copy-start(f32[32]{0:T(128)} %copy-done.29) | copy-start | bytes 388
  115.8 2.5 %copy-start.33 = (s32[128]{0:T(128)S(1)}, s32[128]{0:T(128)}, u32[]{:S(2)}) copy-start(s32[128]{0:T(128)} %param.20) | copy-start | bytes 1540
  115.8 5.5 %copy-start.12 = (bf16[2,2,32,1536]{3,2,1,0:T(8,128)(2,1)S(1)}, bf16[2,2,32,1536]{3,2,1,0:T(8,128)(2,1)}, u32[]{:S(2)}) copy-start(bf16[2,2,32,1536]{3,2,1,0:T(8,128)(2,1)} %copy-done.11) | copy-start | bytes 1179652
  122.3 29.3 %copy-start.18 = (bf16[1024,32]{0,1:T(8,128)(2,1)S(1)}, bf16[1024,32]{0,1:T(8,128)(2,1)}, u32[]{:S(2)}) copy-start(bf16[1024,32]{0,1:T(8,128)(2,1)} %copy-done.17) | copy-start | bytes 196612
  123.5 29.7 %copy-start.5 = (bf16[128,512]{1,0:T(8,128)(2,1)S(1)}, bf16[128,512]{1,0:T(8,128)(2,1)}, u32[]{:S(2)}) copy-start(bf16[128,512]{1,0:T(8,128)(2,1)} %param.11) | copy-start | bytes 393220
  123.6 29.7 %copy-start.10 = (bf16[128,512]{1,0:T(8,128)(2,1)S(1)}, bf16[128,512]{1,0:T(8,128)(2,1)}, u32[]{:S(2)}) copy-start(bf16[128,512]{1,0:T(8,128)(2,1)} %copy-done.9) | copy-start | bytes 393220
  123.6 29.7 %copy-start.16 = (f32[128,512]{1,0:T(8,128)S(1)}, f32[128,512]{1,0:T(8,128)}, u32[]{:S(2)}) copy-start(f32[128,512]{1,0:T(8,128)} %get-tuple-element.67) | copy-start | bytes 786436
  123.6 29.7 %copy-start.31 = (f32[128]{0:T(128)S(1)}, f32[128]{0:T(128)}, u32[]{:S(2)}) copy-start(f32[128]{0:T(128)} %broadcast_multiply_fusion.1) | copy-start | bytes 1540

commit v7 on v6

--- a/solution.py
+++ b/solution.py
@@ -625,9 +625,9 @@
     late_one, first_left = as_bits(late_one)
     late_two, second_left = as_bits(late_two)
     if share % 16 == 0:
-        one, two, late_one, late_two = fold(
-            [one, two, late_one, late_two],
-            [one_left, two_left, [0, 1] + outer, [0] + outer + [1]],
+        late_one, late_two, one, two = fold(
+            [late_one, late_two, one, two],
+            [[0, 1] + outer, [0] + outer + [1], one_left, two_left],
             bits,
         )
     else:

time: 157 us -> 152 us (0.968)
  Pallas kernels: 69.5 us -> 64.9 us
  other arithmetic: 19.4 us -> 17.8 us
    pallas_call x1, Pallas kernels: 27.5 us -> 22.9 us  [fold(): pl.pallas_call(functools.partial(fold_kernel, orders, bits), out_shape=tu...]
    unnamed x72 -> x60, local copies, waits for them, and re-layouts: 6.56 us -> 7.27 us
  transfers between devices with their start and end apart: 8 -> 8, of which waited for: 4 -> 3; matrix products, arithmetic and copies ran while one was open for 16% -> 18% of each run, Pallas kernels for 7% -> 7%
where the time goes in v7:
time: 152 us; the launch traced here: 151 us
  Pallas kernels  64.9 us (43%)
  local copies, waits for them, and re-layouts  23.2 us (15%)
  matrix products  18.9 us (12%)
  other arithmetic  17.8 us (12%)
  starting transfers between devices  14.9 us (10%)
  waiting for transfers between devices  9.06 us (6%)
  between operations  2.02 us (1%)
    pallas_call x1, Pallas kernels, fold(): pl.pallas_call(functools.partial(fold_kernel, orders, bits), out_shape=tu...  22.9 us
    pallas_call x1, Pallas kernels, exchange(): pl.pallas_call(functools.partial(exchange_kernel, slices), out_shape=(jax...  19.8 us
    pallas_call x1, Pallas kernels, attention_forward(): pl.pallas_call(functools.partial(forward_kernel, head_dim, slices, size),...  11.9 us
    convert_element_type x6, other arithmetic, halve(): return (total if not rest else total.astype(jnp.bfloat16), rest)  10.6 us
    pallas_call x1, Pallas kernels, attention_backward(): pl.pallas_call(functools.partial(backward_kernel, head_dim), out_shape=(j...  10.3 us
    all_to_all x2, starting transfers between devices, all_to_all(): lax.all_to_all(blocks, 'seq', split_axis=0, concat_axis=0, tiled=True)  9.45 us
    all_to_all x2, waiting for transfers between devices, all_to_all(): lax.all_to_all(blocks, 'seq', split_axis=0, concat_axis=0, tiled=True)  7.4 us
    unnamed x60, local copies, waits for them, and re-layouts  7.27 us
  transfers between devices with their start and end apart: 8, of which 3 were waited for; matrix products, arithmetic and copies ran while one was open for 18% of the time, Pallas kernels for 7%

profile of v7, /device:TPU:0, one launch (start us, length us, event | category | flops | bytes accessed | tf_op | source)
XLA Modules:
  0.0 150.8 jit_solution(247057649166419403)
XLA Ops:
  0.6 0.9 fusion.39
  1.6 1.0 fusion.27
  2.6 1.1 convolution_convert_fusion.6
  3.7 1.9 %convolution_convert_fusion.2 = bf16[128,1536]{1,0:T(8,128)(2,1)S(1)} fusion(bf16[512,1536]{1,0:T(8,128)(2,1)} %param.14, bf16[128,512]{1,0:T(8,128)(2,1)} %param.11, f32[512]{0:T(512)} %param.12, f32[128]{0:T(128)S(1)} %add_rsqrt_fusion.2), kind=kOutput, calls=%fused_computation.2 | convolution fusion | flops 201785344 | bytes 2099712 | tf_op jit(solution)/shard_map/dot_general | solution.py:475
  5.7 2.6 %copy.65 = bf16[512,1536]{0,1:T(8,128)(2,1)} copy(bf16[512,1536]{1,0:T(8,128)(2,1)} %param.14) | data formatting | bytes 3145728 | tf_op args[3]
  9.1 0.2 copy.62
  9.7 19.8 %shard_map.162 = (bf16[16,96,128]{2,1,0:T(8,128)(2,1)S(1)}, bf16[16,16,128]{2,1,0:T(8,128)(2,1)S(1)}) custom-call(bf16[16,16,128]{2,1,0:T(8,128)(2,1)S(1)} %maximum_maximum_fusion.sums_ref, f32[16,128]{1,0:T(8,128)S(1)} %pad.8.list_ref, bf16[16,96,128]{2,1,0:T(8,128)(2,1)S(1)} %bitcast.103), custom_call_target="tpu_custom_call" | custom-call | flops 32768 | bytes 786432 | tf_op jit(solution)/shard_map/pallas_call | solution.py:311
  30.5 1.0 convolution_convert_fusion.7.virt_ref
  31.5 11.9 %shard_map.163 = bf16[16,32,128]{2,1,0:T(8,128)(2,1)S(1)} custom-call(s32[16,5]{1,0:T(8,128)S(1)} %bitcast.106, bf16[16,96,128]{2,1,0:T(8,128)(2,1)S(1)} %get-tuple-element.25.qkv_ref, bf16[2,32,32]{2,1,0:T(8,128)(2,1)S(1)} %convolution_convert_fusion.7.virt_ref), custom_call_target="tpu_custom_call" | custom-call | flops 142606336 | bytes 393216 | tf_op jit(solution)/shard_map/pallas_call | solution.py:184
  43.4 0.3 multiply_reduce_fusion.2
  43.8 0.5 fusion.47
  44.3 0.7 copy-done.11
  45.0 0.5 multiply_convert_fusion.1
  45.6 0.7 copy-done.17
  46.3 1.6 %multiply_reduce_fusion = (bf16[512]{0:T(512)(128)(2,1)S(1)}, f32[128]{0:T(128)S(1)}, f32[128,512]{1,0:T(8,128)}) fusion(f32[128,512]{1,0:T(8,128)S(1)} %get-tuple-element.63, f32[128]{0:T(128)S(1)} %add_rsqrt_fusion, f32[512]{0:T(512)S(1)} %copy-done.22, bf16[512,2048]{1,0:T(8,128)(2,1)S(1)} %copy-done, bf16[128,1024]{1,0:T(8,128)(2,1)S(1)} %get-tuple-element.52, ...), kind=kOutput, calls=%fused_computation.64 | convolution fusion | flops 269876608 | bytes 3149824 | tf_op jit(solution)/shard_map/rf,df->rd/dot_general | solution.py:526
  47.8 0.4 convolution_convert_fusion.3
  48.3 1.1 fusion.53
  49.5 1.1 convolution_convert_fusion.4
  50.6 1.5 pad_maximum_fusion
  52.1 1.0 constant_dynamic-slice_fusion.1
  53.1 1.0 copy.98
  54.1 0.5 collective-permute-start.1
  54.6 0.8 convolution_convert_fusion
  55.4 1.2 constant_dynamic-slice_fusion.3
  56.6 1.0 copy.97
  57.8 0.3 fusion.6
  58.1 0.8 copy.69
  58.9 5.5 %all-to-all-start = ((bf16[16,32,128]{2,1,0:T(8,128)(2,1)}), bf16[16,32,128]{2,1,0:T(8,128)(2,1)S(1)}, u32[]{:S(2)}, u32[]{:S(2)}) async-start(bf16[16,32,128]{2,1,0:T(8,128)(2,1)} %bitcast.15), calls=%async_computation | async-start | bytes 262144 | tf_op jit(solution)/shard_map/all_to_all | solution.py:227
  64.5 2.6 %fusion.2 = bf16[2,2,2,32,1536]{4,3,2,0,1:T(8,128)(2,1)} fusion(bf16[2,2,2,32,1536]{4,3,2,0,1:T(8,128)(2,1)} %collective-permute-done.1, bf16[2,2,2,1,32,1536]{5,4,3,2,1,0:T(8,128)(2,1)} %get-tuple-element.49), kind=kLoop, calls=%fused_computation.9 | loop fusion | flops 1572864 | bytes 2359296 | tf_op jit(solution)/shard_map/convert_element_type | solution.py:246
  67.0 2.6 %fusion = bf16[2,2,2,32,2048]{4,3,0,1,2:T(8,128)(2,1)} fusion(bf16[2,2,2,32,2048]{4,3,0,1,2:T(8,128)(2,1)} %collective-permute-done, bf16[2,2,2,1,32,2048]{5,4,3,2,1,0:T(8,128)(2,1)S(1)} %copy-done.2), kind=kLoop, calls=%fused_computation.4 | loop fusion | flops 2097152 | bytes 3145728 | tf_op jit(solution)/shard_map/convert_element_type | solution.py:246
  69.6 2.7 %all-to-all-done.grad_ref = bf16[16,32,128]{2,1,0:T(8,128)(2,1)S(1)} async-done(((bf16[16,32,128]{2,1,0:T(8,128)(2,1)}), bf16[16,32,128]{2,1,0:T(8,128)(2,1)S(1)}, u32[]{:S(2)}, u32[]{:S(2)}) %all-to-all-start) | async-done | bytes 131104 | tf_op jit(solution)/shard_map/all_to_all | solution.py:227
  72.3 1.8 %dynamic-slice_bitcast_fusion.1 = bf16[2,2,32,1536]{3,2,1,0:T(8,128)(2,1)} fusion(bf16[2,2,2,32,1536]{4,3,2,0,1:T(8,128)(2,1)} %fusion.2, s32[]{:T(128)S(6)} %select_n.96), kind=kLoop, calls=%fused_computation.47 | loop fusion | bytes 786436 | tf_op jit(solution)/shard_map/jit(dynamic_index_in_dim)/squeeze | solution.py:240
  74.1 1.9 %dynamic-slice_bitcast_fusion = bf16[2,2,32,2048]{3,2,0,1:T(8,128)(2,1)} fusion(bf16[2,2,2,32,2048]{4,3,0,1,2:T(8,128)(2,1)} %fusion, s32[]{:T(128)S(6)} %select_n.92), kind=kLoop, calls=%fused_computation.37 | loop fusion | bytes 1048580 | tf_op jit(solution)/shard_map/jit(dynamic_index_in_dim)/squeeze | solution.py:240
  76.1 0.6 collective-permute-start.2
  76.7 10.3 %shard_map.164 = (bf16[16,32,128]{2,1,0:T(8,128)(2,1)S(1)}, bf16[16,64,128]{2,1,0:T(8,128)(2,1)S(1)}, f32[64,32]{1,0:T(8,128)S(1)}) custom-call(s32[16,5]{1,0:T(8,128)S(1)} %bitcast.107, bf16[16,96,128]{2,1,0:T(8,128)(2,1)S(1)} %get-tuple-element.25.qkv_ref, bf16[2,32,32]{2,1,0:T(8,128)(2,1)S(1)} %convolution_convert_fusion.7.virt_ref, ...), custom_call_target="tpu_custom_call" | custom-call | flops 356515840 | bytes 1179648 | tf_op jit(solution)/shard_map/pallas_call | solution.py:209
  87.1 1.2 fusion.11
  88.3 1.6 %collective-permute-done.2 = bf16[2,2,32,2048]{3,2,0,1:T(8,128)(2,1)} collective-permute-done((bf16[2,2,32,2048]{3,2,0,1:T(8,128)(2,1)}, bf16[2,2,32,2048]{3,2,0,1:T(8,128)(2,1)}, u32[]{:S(2)}, u32[]{:S(2)}) %collective-permute-start.2) | collective-permute-done | bytes 524320 | tf_op jit(solution)/shard_map/ppermute | solution.py:241
  89.9 2.2 %fusion.7 = bf16[2,2,32,2048]{3,2,0,1:T(8,128)(2,1)} fusion(bf16[2,2,32,2048]{3,2,0,1:T(8,128)(2,1)} %collective-permute-done.2, bf16[2,2,2,32,2048]{4,3,0,1,2:T(8,128)(2,1)} %fusion, s32[]{:T(128)S(6)} %select_n.91), kind=kLoop, calls=%fused_computation.25 | loop fusion | flops 1048576 | bytes 1572868 | tf_op jit(solution)/shard_map/convert_element_type | solution.py:246
  92.1 0.8 pad_maximum_fusion.2
  92.9 3.9 %all-to-all-start.1 = ((bf16[16,112,128]{2,1,0:T(8,128)(2,1)}), bf16[16,112,128]{2,1,0:T(8,128)(2,1)S(1)}, u32[]{:S(2)}, u32[]{:S(2)}) async-start(bf16[16,112,128]{2,1,0:T(8,128)(2,1)} %pad_maximum_fusion.2), calls=%async_computation.1 | async-start | bytes 917504 | tf_op jit(solution)/shard_map/all_to_all | solution.py:227
  97.0 2.3 %fusion.5 = bf16[128,512]{1,0:T(8,128)(2,1)} fusion(f32[128,512]{1,0:T(8,128)S(1)} %get-tuple-element.63, bf16[128,1024]{1,0:T(8,128)(2,1)} %copy-done.12, bf16[1024,512]{1,0:T(8,128)(2,1)} %param.17), kind=kOutput, calls=%fused_computation.18 | convolution fusion | flops 134348800 | bytes 1703936 | tf_op jit(solution)/shard_map/dot_general | solution.py:519
  99.3 1.7 %dynamic-slice_bitcast_fusion.2 = bf16[2,32,2048]{2,1,0:T(8,128)(2,1)} fusion(bf16[2,2,32,2048]{3,2,0,1:T(8,128)(2,1)} %fusion.7, s32[]{:T(128)S(6)} %select_n.96), kind=kLoop, calls=%fused_computation.63 | loop fusion | bytes 524292 | tf_op jit(solution)/shard_map/jit(dynamic_index_in_dim)/squeeze | solution.py:240
  101.0 1.9 %collective-permute-start.4 = (bf16[2,32,2048]{2,1,0:T(8,128)(2,1)}, bf16[2,32,2048]{2,1,0:T(8,128)(2,1)}, u32[]{:S(2)}, u32[]{:S(2)}) collective-permute-start(bf16[2,32,2048]{2,1,0:T(8,128)(2,1)} %dynamic-slice_bitcast_fusion.2), channel_id=1, source_target_pairs={{0,4},{1,5},{2,6},{3,7},{4,0},{5,1},{6,2},{7,3},{8,12},{9,13},{10,... | collective-permute-start | bytes 786440 | tf_op jit(solution)/shard_map/ppermute | solution.py:241
  102.8 0.7 dynamic-slice_bitcast_fusion.3
  103.5 2.4 %collective-permute-start.5 = (bf16[2,32,1536]{2,1,0:T(8,128)(2,1)}, bf16[2,32,1536]{2,1,0:T(8,128)(2,1)}, u32[]{:S(2)}, u32[]{:S(2)}) collective-permute-start(bf16[2,32,1536]{2,1,0:T(8,128)(2,1)} %dynamic-slice_bitcast_fusion.3), channel_id=1, source_target_pairs={{0,8},{1,9},{2,10},{3,11},{4,12},{5,13},{6,14},{7,15},{8,0},{9,1},... | collective-permute-start | bytes 589832 | tf_op jit(solution)/shard_map/ppermute | solution.py:241
  105.9 4.7 %all-to-all-done.1 = bf16[16,112,128]{2,1,0:T(8,128)(2,1)S(1)} async-done(((bf16[16,112,128]{2,1,0:T(8,128)(2,1)}), bf16[16,112,128]{2,1,0:T(8,128)(2,1)S(1)}, u32[]{:S(2)}, u32[]{:S(2)}) %all-to-all-start.1) | async-done | bytes 458784 | tf_op jit(solution)/shard_map/all_to_all | solution.py:227
  110.7 1.3 copy-done.1
  112.0 1.4 fusion.56
  113.4 1.8 %convolution_convert_fusion.1 = bf16[512,1536]{1,0:T(8,128)(2,1)} fusion(bf16[1536,128]{1,0:T(8,128)(2,1)S(1)} %bitcast.112, bf16[128,512]{1,0:T(8,128)(2,1)S(1)} %copy-done.3, f32[512]{0:T(512)S(1)} %copy-done.23, f32[128]{0:T(128)S(1)} %add_rsqrt_fusion.2), kind=kOutput, calls=%fused_computation.1 | convolution fusion | flops 202375168 | bytes 2099712 | tf_op jit(solution)/shard_map/rd,cr->dc/dot_general | solution.py:598
  115.4 0.4 copy.78
  115.8 0.3 reshape.197
  116.1 1.8 %multiply_reduce_fusion.3 = (f32[32]{0:T(128)S(1)}, f32[32,512]{1,0:T(8,128)S(1)}) fusion(f32[32]{0:T(128)S(1)} %copy-done.25, f32[32,512]{1,0:T(8,128)S(1)} %reshape.191, f32[32]{0:T(128)S(1)} %div.76, bf16[1024,32]{0,1:T(8,128)(2,1)S(1)} %reshape.197, bf16[512,1536]{1,0:T(8,128)(2,1)} %param.14), kind=kOutput, calls=%fused_computation.80 | convolution fusion | flops 33619936 | bytes 1245568 | tf_op jit(solution)/shard_map/sp,ds->pd/dot_general | solution.py:593
  117.9 1.1 fusion.26
  119.1 1.5 %fusion.52 = (bf16[16,32,768]{2,1,0:T(8,128)(2,1)S(1)}, bf16[16,32,768]{2,1,0:T(8,128)(2,1)S(1)}) fusion(bf16[16,32,1536]{2,1,0:T(8,128)(2,1)} %bitcast.109), kind=kLoop, calls=%fused_computation.114 | loop fusion | bytes 3145728 | tf_op jit(solution)/shard_map/slice | solution.py:624
  120.6 1.1 fusion.12.refs_2_
  121.8 1.0 fusion.14.refs_3_
  122.9 22.9 %shard_map.165 = (f32[32,768]{1,0:T(8,128)S(1)}, f32[32,896]{1,0:T(8,128)S(1)}, f32[32,2048]{1,0:T(8,128)S(1)}, f32[32,1536]{1,0:T(8,128)S(1)}) custom-call(bf16[2,2,2,2,32,768]{5,4,3,2,1,0:T(8,128)(2,1)S(1)} %bitcast.102, bf16[2,2,2,2,32,896]{5,4,3,2,1,0:T(8,128)(2,1)S(1)} %bitcast.101, bf16[2,32,2048]{2,1,0:T(8,128)(2,1)S(1)} %fusion.12.refs_2_, ...), custom_call_target="tpu_custom_call" | custom-call | flops 393216 | bytes 8650752 | tf_op jit(solution)/shard_map/pallas_call | solution.py:405
  145.8 0.5 slice_bitcast_fusion
  146.4 1.0 convolution_add_fusion.3
  147.3 0.6 fusion.55
  148.0 0.8 fusion.25
  148.8 0.7 pad_maximum_fusion.6
  149.5 0.7 pad_maximum_fusion.8
  150.1 0.7 copy.101
  (103 shorter events, 2.4 us)
Async XLA Ops:
  0.6 43.2 %copy-start = (bf16[512,2048]{1,0:T(8,128)(2,1)S(1)}, bf16[512,2048]{1,0:T(8,128)(2,1)}, u32[]{:S(2)}) copy-start(bf16[512,2048]{1,0:T(8,128)(2,1)} %param.16) | copy-start | bytes 6291460
  5.7 3.8 %copy-start.26 = (s32[1,4]{1,0:T(1,128)S(1)}, s32[1,4]{1,0:T(1,128)}, u32[]{:S(2)}) copy-start(s32[1,4]{1,0:T(1,128)} %param.18) | copy-start | bytes 52
  30.2 13.2 %copy-start.24 = (f32[32]{0:T(128)}, f32[32]{0:T(128)S(1)}, u32[]{:S(2)}) copy-start(f32[32]{0:T(128)S(1)} %add_rsqrt_fusion.1) | copy-start | bytes 388
  30.5 1.0 copy-start.21
  31.5 11.9 %copy-start.3 = (bf16[128,512]{1,0:T(8,128)(2,1)S(1)}, bf16[128,512]{1,0:T(8,128)(2,1)}, u32[]{:S(2)}) copy-start(bf16[128,512]{1,0:T(8,128)(2,1)} %param.11) | copy-start | bytes 393220
  31.5 11.9 %copy-start.4 = (bf16[512,512]{1,0:T(8,128)(2,1)S(1)}, bf16[512,512]{1,0:T(8,128)(2,1)}, u32[]{:S(2)}) copy-start(bf16[512,512]{1,0:T(8,128)(2,1)} %param.15) | copy-start | bytes 1572868
  31.5 12.3 %copy-start.22 = (f32[512]{0:T(512)S(1)}, f32[512]{0:T(512)}, u32[]{:S(2)}) copy-start(f32[512]{0:T(512)} %param.13) | copy-start | bytes 6148
  43.8 1.2 copy-start.11
  43.8 1.2 copy-start.13
  45.6 0.7 copy-start.17
  45.6 2.3 %copy-start.19 = (bf16[128,1024]{1,0:T(8,128)(2,1)}, bf16[128,1024]{1,0:T(8,128)(2,1)S(1)}, u32[]{:S(2)}) copy-start(bf16[128,1024]{1,0:T(8,128)(2,1)S(1)} %get-tuple-element.52) | copy-start | bytes 786436
  45.6 2.7 %copy-start.12 = (bf16[128,1024]{1,0:T(8,128)(2,1)}, bf16[128,1024]{1,0:T(8,128)(2,1)S(1)}, u32[]{:S(2)}) copy-start(bf16[128,1024]{1,0:T(8,128)(2,1)S(1)} %get-tuple-element.55) | copy-start | bytes 786436
  47.8 1.5 %copy-start.16 = (f32[128,512]{1,0:T(8,128)S(1)}, f32[128,512]{1,0:T(8,128)}, u32[]{:S(2)}) copy-start(f32[128,512]{1,0:T(8,128)} %get-tuple-element.64) | copy-start | bytes 786436
  49.5 8.2 %copy-start.7 = (bf16[128,512]{1,0:T(8,128)(2,1)}, bf16[128,512]{1,0:T(8,128)(2,1)S(1)}, u32[]{:S(2)}) copy-start(bf16[128,512]{1,0:T(8,128)(2,1)S(1)} %add_convert_fusion) | copy-start | bytes 393220
  52.1 2.5 %copy-start.18 = (bf16[128,1024]{1,0:T(8,128)(2,1)S(1)}, bf16[128,1024]{1,0:T(8,128)(2,1)}, u32[]{:S(2)}) copy-start(bf16[128,1024]{1,0:T(8,128)(2,1)} %copy-done.17) | copy-start | bytes 786436
  52.1 2.5 %copy-start.20 = (bf16[128,1024]{1,0:T(8,128)(2,1)S(1)}, bf16[128,1024]{1,0:T(8,128)(2,1)}, u32[]{:S(2)}) copy-start(bf16[128,1024]{1,0:T(8,128)(2,1)} %copy-done.19) | copy-start | bytes 786436
  54.1 10.4 %collective-permute-start.1 = (bf16[2,2,2,32,1536]{4,3,2,0,1:T(8,128)(2,1)}, bf16[2,2,2,32,1536]{4,3,2,0,1:T(8,128)(2,1)}, u32[]{:S(2)}, u32[]{:S(2)}) collective-permute-start(bf16[2,2,2,32,1536]{4,3,2,0,1:T(8,128)(2,1)} %bitcast.99), channel_id=1, source_target_pairs={{0,1},{1,0},{2,3},{3,2},{4,5},{5,4},{6,7},{7,6},{8,9},{9,8},{10,11... | collective-permute-start | bytes 2359304 | tf_op jit(solution)/shard_map/ppermute | solution.py:241
  56.6 1.2 copy-start.5
  57.7 9.4 %collective-permute-start = (bf16[2,2,2,32,2048]{4,3,0,1,2:T(8,128)(2,1)}, bf16[2,2,2,32,2048]{4,3,0,1,2:T(8,128)(2,1)}, u32[]{:S(2)}, u32[]{:S(2)}) collective-permute-start(bf16[2,2,2,32,2048]{4,3,0,1,2:T(8,128)(2,1)} %bitcast.98), channel_id=1, source_target_pairs={{0,1},{1,0},{2,3},{3,2},{4,5},{5,4},{6,7},{7,6},{8,9},{9,8},{10,11... | collective-permute-start | bytes 3145736 | tf_op jit(solution)/shard_map/ppermute | solution.py:241
  58.9 13.4 %all-to-all-start = ((bf16[16,32,128]{2,1,0:T(8,128)(2,1)}), bf16[16,32,128]{2,1,0:T(8,128)(2,1)S(1)}, u32[]{:S(2)}, u32[]{:S(2)}) async-start(bf16[16,32,128]{2,1,0:T(8,128)(2,1)} %bitcast.15), calls=%async_computation | async-start | bytes 262144 | tf_op jit(solution)/shard_map/all_to_all | solution.py:227
  64.4 2.6 %copy-start.2 = (bf16[2,2,2,1,32,2048]{5,4,3,2,1,0:T(8,128)(2,1)S(1)}, bf16[2,2,2,1,32,2048]{5,4,3,2,1,0:T(8,128)(2,1)}, u32[]{:S(2)}) copy-start(bf16[2,2,2,1,32,2048]{5,4,3,2,1,0:T(8,128)(2,1)} %get-tuple-element.45) | copy-start | bytes 3145732
  74.1 12.9 %collective-permute-start.3 = (bf16[2,2,32,1536]{3,2,1,0:T(8,128)(2,1)}, bf16[2,2,32,1536]{3,2,1,0:T(8,128)(2,1)}, u32[]{:S(2)}, u32[]{:S(2)}) collective-permute-start(bf16[2,2,32,1536]{3,2,1,0:T(8,128)(2,1)} %dynamic-slice_bitcast_fusion.1), channel_id=1, source_target_pairs={{0,4},{1,5},{2,6},{3,7},{4,0},{5,1},{6,2},{7,3},{8,12},{9,13},{10,... | collective-permute-start | bytes 1179656 | tf_op jit(solution)/shard_map/ppermute | solution.py:241
  76.1 13.9 %collective-permute-start.2 = (bf16[2,2,32,2048]{3,2,0,1:T(8,128)(2,1)}, bf16[2,2,32,2048]{3,2,0,1:T(8,128)(2,1)}, u32[]{:S(2)}, u32[]{:S(2)}) collective-permute-start(bf16[2,2,32,2048]{3,2,0,1:T(8,128)(2,1)} %dynamic-slice_bitcast_fusion), channel_id=1, source_target_pairs={{0,2},{1,3},{2,0},{3,1},{4,6},{5,7},{6,4},{7,5},{8,10},{9,11},{10,... | collective-permute-start | bytes 1572872 | tf_op jit(solution)/shard_map/ppermute | solution.py:241
  88.3 14.6 %copy-start.9 = (bf16[2,2,32,1536]{3,2,1,0:T(8,128)(2,1)}, bf16[2,2,32,1536]{3,2,1,0:T(8,128)(2,1)S(1)}, u32[]{:S(2)}) copy-start(bf16[2,2,32,1536]{3,2,1,0:T(8,128)(2,1)S(1)} %fusion.11) | copy-start | bytes 1179652
  92.9 17.7 %all-to-all-start.1 = ((bf16[16,112,128]{2,1,0:T(8,128)(2,1)}), bf16[16,112,128]{2,1,0:T(8,128)(2,1)S(1)}, u32[]{:S(2)}, u32[]{:S(2)}) async-start(bf16[16,112,128]{2,1,0:T(8,128)(2,1)} %pad_maximum_fusion.2), calls=%async_computation.1 | async-start | bytes 917504 | tf_op jit(solution)/shard_map/all_to_all | solution.py:227
  101.0 19.7 %collective-permute-start.4 = (bf16[2,32,2048]{2,1,0:T(8,128)(2,1)}, bf16[2,32,2048]{2,1,0:T(8,128)(2,1)}, u32[]{:S(2)}, u32[]{:S(2)}) collective-permute-start(bf16[2,32,2048]{2,1,0:T(8,128)(2,1)} %dynamic-slice_bitcast_fusion.2), channel_id=1, source_target_pairs={{0,4},{1,5},{2,6},{3,7},{4,0},{5,1},{6,2},{7,3},{8,12},{9,13},{10,... | collective-permute-start | bytes 786440 | tf_op jit(solution)/shard_map/ppermute | solution.py:241
  103.5 9.8 %copy-start.23 = (f32[512]{0:T(512)S(1)}, f32[512]{0:T(512)}, u32[]{:S(2)}) copy-start(f32[512]{0:T(512)} %param.12) | copy-start | bytes 6148
  103.5 18.2 %collective-permute-start.5 = (bf16[2,32,1536]{2,1,0:T(8,128)(2,1)}, bf16[2,32,1536]{2,1,0:T(8,128)(2,1)}, u32[]{:S(2)}, u32[]{:S(2)}) collective-permute-start(bf16[2,32,1536]{2,1,0:T(8,128)(2,1)} %dynamic-slice_bitcast_fusion.3), channel_id=1, source_target_pairs={{0,8},{1,9},{2,10},{3,11},{4,12},{5,13},{6,14},{7,15},{8,0},{9,1},... | collective-permute-start | bytes 589832 | tf_op jit(solution)/shard_map/ppermute | solution.py:241
  110.6 1.4 copy-start.1
  113.3 2.8 %copy-start.25 = (f32[32]{0:T(128)S(1)}, f32[32]{0:T(128)}, u32[]{:S(2)}) copy-start(f32[32]{0:T(128)} %copy-done.24) | copy-start | bytes 388
  115.2 2.7 %copy-start.27 = (s32[128]{0:T(128)S(1)}, s32[128]{0:T(128)}, u32[]{:S(2)}) copy-start(s32[128]{0:T(128)} %param.20) | copy-start | bytes 1540
  115.2 2.7 %copy-start.15 = (f32[128,512]{1,0:T(8,128)S(1)}, f32[128,512]{1,0:T(8,128)}, u32[]{:S(2)}) copy-start(f32[128,512]{1,0:T(8,128)} %fusion.56) | copy-start | bytes 786436
  119.0 1.7 %copy-start.6 = (bf16[2,2,32,2048]{3,2,0,1:T(8,128)(2,1)S(1)}, bf16[2,2,32,2048]{3,2,0,1:T(8,128)(2,1)}, u32[]{:S(2)}) copy-start(bf16[2,2,32,2048]{3,2,0,1:T(8,128)(2,1)} %fusion.7) | copy-start | bytes 1572868
  120.6 1.2 copy-start.10
  121.8 26.1 %copy-start.8 = (bf16[128,512]{1,0:T(8,128)(2,1)S(1)}, bf16[128,512]{1,0:T(8,128)(2,1)}, u32[]{:S(2)}) copy-start(bf16[128,512]{1,0:T(8,128)(2,1)} %copy-done.7) | copy-start | bytes 393220
  121.8 26.1 %copy-start.14 = (f32[128,512]{1,0:T(8,128)S(1)}, f32[128,512]{1,0:T(8,128)}, u32[]{:S(2)}) copy-start(f32[128,512]{1,0:T(8,128)} %get-tuple-element.67) | copy-start | bytes 786436
